TPU v7x, 32 devices: a whole 2x2x4 slice. The times are simulated.
32 devices in a mesh: dp: 4 (over y, x), tensor: 8 (over z, core).
Axes of the slice: x: 2, y: 2, z: 4, core: 2. Of those that a mesh axis runs over, the one named last changes fastest.
Arguments:
- tokens: bfloat16 [8192, 2048], P(('dp', 'tensor')), may hold values from -6 to 6
- lengths: int32 [4, 2], replicated, may hold values from 1 to 1365, as said below
- attention_gain: float32 [2048], replicated, may hold values from 0.25 to 1.75
- attention_shift: float32 [2048], replicated, may hold values from -4 to 4
- query_key_value: bfloat16 [2048, 3, 2048], P(None, None, 'tensor'), may hold values from -0.125 to 0.125
- query_value_bias: float32 [2, 2048], P(None, 'tensor'), may hold values from -4 to 4
- output_weight: bfloat16 [2048, 2048], P('tensor'), may hold values from -0.5 to 0.5
- output_bias: float32 [2048], replicated, may hold values from -4 to 4
- feedforward_gain: float32 [2048], replicated, may hold values from 0.25 to 1.75
- feedforward_shift: float32 [2048], replicated, may hold values from -4 to 4
- expand_weight: bfloat16 [2048, 8192], P(None, 'tensor'), may hold values from -0.125 to 0.125
- expand_bias: float32 [8192], P('tensor'), may hold values from -6 to 6
- contract_weight: bfloat16 [8192, 2048], P('tensor'), may hold values from -0.0625 to 0.0625
- contract_bias: float32 [2048], replicated, may hold values from -4 to 4
- cotangent: bfloat16 [8192, 2048], P(('dp', 'tensor')), may hold values from -6 to 6
Outputs:
- layer_output: bfloat16 [8192, 2048], P(('dp', 'tensor'))
- input_gradient: bfloat16 [8192, 2048], P(('dp', 'tensor'))
- attention_gain_gradient: float32 [2048], P('tensor')
- attention_shift_gradient: float32 [2048], P('tensor')
- projection_gradient: float32 [2048, 3, 2048], P(None, None, 'tensor')
- query_value_gradient: float32 [2, 2048], P(None, 'tensor')
- output_gradient: float32 [2048, 2048], P('tensor')
- output_bias_gradient: float32 [2048], P('tensor')
- feedforward_gain_gradient: float32 [2048], P('tensor')
- feedforward_shift_gradient: float32 [2048], P('tensor')
- expand_gradient: float32 [2048, 8192], P(None, 'tensor')
- expand_bias_gradient: float32 [8192], P('tensor')
- contract_gradient: float32 [8192, 2048], P('tensor')
- contract_bias_gradient: float32 [2048], P('tensor')
Inputs may be any that keep to these rules, and one draw needn't show every extreme that they name: Each group's 2 lengths are in order long then short and sum to at most 2048; in exactly one group they sum to 2048, and there the first is 1365.
All inputs are finite; a program needn't handle non-finite values.
Results may differ from a plain program's by a relative error of at most 0.015.
Values may be sent and summed in bfloat16 or wider, within the bound.
No kernel may reach another device: no remote copies, remote signals or barrier semaphores. Data moves between devices by JAX's collectives and lax.ppermute only.
A program may use at most 256 MiB of HBM per device.

v0:
```python
import jax
import jax.numpy as jnp
from jax import lax
from jax.sharding import PartitionSpec as P

HEAD_DIM = 128
BLOCK = 512


EPSILON = 1e-05


def layer_norm(values, gain_row, shift_row):
    center = values - jnp.mean(values, axis=-1, keepdims=True)
    spread = jnp.mean(center * center, axis=-1, keepdims=True)
    return center * lax.rsqrt(spread + EPSILON) * gain_row + shift_row


def gelu_tanh(values):
    return jax.nn.gelu(values, approximate=True)


def shards(
    tokens,
    lengths,
    attention_gain,
    attention_shift,
    query_key_value,
    query_value_bias,
    output_weight,
    output_bias,
    feedforward_gain,
    feedforward_shift,
    expand_weight,
    expand_bias,
    contract_weight,
    contract_bias,
    cotangent,
):
    shard_rows = tokens.shape[0]
    tensor_size = lax.axis_size("tensor")
    group_rows = shard_rows * tensor_size
    local_width = query_key_value.shape[2]
    local_heads = local_width // HEAD_DIM
    block_count = group_rows // BLOCK
    score_scale = HEAD_DIM ** (-0.5)
    bounds = jnp.cumsum(lengths, axis=1)
    own_bounds = lax.dynamic_index_in_dim(bounds, lax.axis_index("dp"), 0, keepdims=False)
    own_count = own_bounds[-1]
    group_share = own_count.astype(jnp.float32) / jnp.sum(bounds[:, -1]).astype(jnp.float32)
    row_index = jnp.arange(group_rows, dtype=jnp.int32)
    segment = jnp.sum((row_index[:, None] >= own_bounds[None, :]).astype(jnp.int32), axis=1)
    live_rows = row_index < own_count
    first_row = lax.axis_index("tensor") * shard_rows
    local_live = lax.dynamic_slice_in_dim(live_rows, first_row, shard_rows).astype(jnp.float32)[
        :, None
    ]
    input_rows = tokens.astype(jnp.float32)
    all_tokens = lax.all_gather(tokens, "tensor", axis=0, tiled=True)
    normed = layer_norm(all_tokens.astype(jnp.float32), attention_gain, attention_shift).astype(
        jnp.bfloat16
    )
    full_bias = jnp.stack(
        [query_value_bias[0], jnp.zeros_like(query_value_bias[0]), query_value_bias[1]]
    )
    projected = (
        jnp.einsum("td,dcj->tcj", normed, query_key_value, preferred_element_type=jnp.float32)
        + full_bias
    ).astype(jnp.bfloat16)
    query_heads = projected[:, 0].reshape(group_rows, local_heads, HEAD_DIM)
    key_heads = projected[:, 1].reshape(group_rows, local_heads, HEAD_DIM)
    value_heads = projected[:, 2].reshape(group_rows, local_heads, HEAD_DIM)

    def block_scores(offset):
        query_block = lax.dynamic_slice_in_dim(query_heads, offset, BLOCK)
        raw_scores = (
            jnp.einsum("qhe,khe->hqk", query_block, key_heads, preferred_element_type=jnp.float32)
            * score_scale
        )
        query_rows = offset + jnp.arange(BLOCK, dtype=jnp.int32)
        query_segment = lax.dynamic_slice_in_dim(segment, offset, BLOCK)
        allowed = (query_segment[:, None] == segment[None, :]) & (
            row_index[None, :] <= query_rows[:, None]
        )
        return (jnp.where(allowed[None], raw_scores, -1000000000.0), query_block)

    def attend(block_index):
        scores, _ = block_scores(block_index * BLOCK)
        highest = jnp.max(scores, axis=-1, keepdims=True)
        exponent = jnp.exp(scores - highest)
        row_sum = jnp.sum(exponent, axis=-1, keepdims=True)
        weights_low = (exponent / row_sum).astype(jnp.bfloat16)
        context_block = jnp.einsum(
            "hqk,khe->qhe", weights_low, value_heads, preferred_element_type=jnp.float32
        ).astype(jnp.bfloat16)
        return (context_block, (highest + jnp.log(row_sum))[..., 0])

    block_numbers = jnp.arange(block_count, dtype=jnp.int32)
    context_blocks, log_totals = lax.map(attend, block_numbers)
    context = context_blocks.reshape(group_rows, local_width)
    partial_sum = jnp.dot(context, output_weight, preferred_element_type=jnp.float32)
    hidden_all = all_tokens.astype(jnp.float32) + lax.psum(partial_sum, "tensor") + output_bias
    hidden = lax.dynamic_slice_in_dim(hidden_all, first_row, shard_rows)
    mixed = layer_norm(hidden_all, feedforward_gain, feedforward_shift).astype(jnp.bfloat16)
    pre_act = jnp.dot(mixed, expand_weight, preferred_element_type=jnp.float32) + expand_bias
    activated = gelu_tanh(pre_act).astype(jnp.bfloat16)
    branch = lax.psum_scatter(
        jnp.dot(activated, contract_weight, preferred_element_type=jnp.float32).astype(
            jnp.bfloat16
        ),
        "tensor",
        scatter_dimension=0,
        tiled=True,
    ).astype(jnp.float32)
    layer_output = (local_live * (hidden + branch + contract_bias)).astype(jnp.bfloat16)
    grad_local = local_live * cotangent.astype(jnp.float32)
    cotangent_all = lax.all_gather(cotangent, "tensor", axis=0, tiled=True)
    grad_out_all = jnp.where(live_rows[:, None], cotangent_all, jnp.zeros_like(cotangent_all))
    contract_gradient = jnp.einsum(
        "tf,td->fd", activated, grad_out_all, preferred_element_type=jnp.float32
    )
    grad_activated = jnp.einsum(
        "td,fd->tf", grad_out_all, contract_weight, preferred_element_type=jnp.float32
    )
    _, gelu_pull = jax.vjp(gelu_tanh, pre_act)
    grad_pre = gelu_pull(grad_activated)[0].astype(jnp.bfloat16)
    expand_gradient = jnp.einsum("td,tf->df", mixed, grad_pre, preferred_element_type=jnp.float32)
    expand_bias_gradient = jnp.sum(grad_pre.astype(jnp.float32), axis=0)
    grad_mixed = lax.psum_scatter(
        jnp.einsum("tf,df->td", grad_pre, expand_weight, preferred_element_type=jnp.float32),
        "tensor",
        scatter_dimension=0,
        tiled=True,
    )
    _, second_pull = jax.vjp(layer_norm, hidden, feedforward_gain, feedforward_shift)
    hidden_part, second_gain, second_shift = second_pull(grad_mixed)
    grad_hidden = grad_local + hidden_part
    grad_hidden_all = lax.all_gather(grad_hidden.astype(jnp.bfloat16), "tensor", axis=0, tiled=True)
    output_gradient = jnp.einsum(
        "tj,td->jd", context, grad_hidden_all, preferred_element_type=jnp.float32
    )
    grad_context = jnp.einsum(
        "td,jd->tj", grad_hidden_all, output_weight, preferred_element_type=jnp.float32
    ).astype(jnp.bfloat16)
    grad_context = grad_context.reshape(group_rows, local_heads, HEAD_DIM)

    def back_step(running, inputs):
        block_index, log_total = inputs
        offset = block_index * BLOCK
        scores, query_block = block_scores(offset)
        attention = jnp.exp(scores - log_total[..., None])
        grad_block = lax.dynamic_slice_in_dim(grad_context, offset, BLOCK)
        grad_attention = jnp.einsum(
            "qhe,khe->hqk", grad_block, value_heads, preferred_element_type=jnp.float32
        )
        inner_sum = jnp.sum(attention * grad_attention, axis=-1, keepdims=True)
        score_grad = (attention * (grad_attention - inner_sum)).astype(jnp.bfloat16)
        query_grad = (
            jnp.einsum("hqk,khe->qhe", score_grad, key_heads, preferred_element_type=jnp.float32)
            * score_scale
        )
        key_part = (
            jnp.einsum("hqk,qhe->khe", score_grad, query_block, preferred_element_type=jnp.float32)
            * score_scale
        )
        value_part = jnp.einsum(
            "hqk,qhe->khe",
            attention.astype(jnp.bfloat16),
            grad_block,
            preferred_element_type=jnp.float32,
        )
        return ((running[0] + key_part, running[1] + value_part), query_grad)

    empty_heads = jnp.zeros((group_rows, local_heads, HEAD_DIM), jnp.float32)
    (key_grad, value_grad), query_grads = lax.scan(
        back_step, (empty_heads, empty_heads), (block_numbers, log_totals)
    )
    projected_grad = jnp.stack(
        [
            query_grads.reshape(group_rows, local_width),
            key_grad.reshape(group_rows, local_width),
            value_grad.reshape(group_rows, local_width),
        ],
        axis=1,
    ).astype(jnp.bfloat16)
    projection_gradient = jnp.einsum(
        "td,tcj->dcj", normed, projected_grad, preferred_element_type=jnp.float32
    )
    column_sums = jnp.sum(projected_grad.astype(jnp.float32), axis=0)
    query_value_gradient = jnp.stack([column_sums[0], column_sums[2]])
    grad_normed = lax.psum_scatter(
        jnp.einsum(
            "tcj,dcj->td", projected_grad, query_key_value, preferred_element_type=jnp.float32
        ),
        "tensor",
        scatter_dimension=0,
        tiled=True,
    )
    _, first_pull = jax.vjp(layer_norm, input_rows, attention_gain, attention_shift)
    input_part, first_gain, first_shift = first_pull(grad_normed)
    input_gradient = (grad_hidden + input_part).astype(jnp.bfloat16)
    norm_gain_one, norm_shift_one, bias_hidden, norm_gain_two, norm_shift_two, bias_out = (
        lax.psum_scatter(first_gain, "tensor", scatter_dimension=0, tiled=True),
        lax.psum_scatter(first_shift, "tensor", scatter_dimension=0, tiled=True),
        lax.psum_scatter(jnp.sum(grad_hidden, axis=0), "tensor", scatter_dimension=0, tiled=True),
        lax.psum_scatter(second_gain, "tensor", scatter_dimension=0, tiled=True),
        lax.psum_scatter(second_shift, "tensor", scatter_dimension=0, tiled=True),
        lax.psum_scatter(jnp.sum(grad_local, axis=0), "tensor", scatter_dimension=0, tiled=True),
    )
    (
        projection_gradient,
        query_value_gradient,
        output_gradient,
        norm_gain_one,
        norm_shift_one,
        bias_hidden,
        norm_gain_two,
        norm_shift_two,
        bias_out,
        contract_gradient,
        expand_gradient,
        expand_bias_gradient,
    ) = (
        lax.psum((group_share * projection_gradient).astype(jnp.bfloat16), "dp").astype(
            jnp.float32
        ),
        lax.psum((group_share * query_value_gradient).astype(jnp.bfloat16), "dp").astype(
            jnp.float32
        ),
        lax.psum((group_share * output_gradient).astype(jnp.bfloat16), "dp").astype(jnp.float32),
        lax.psum((group_share * norm_gain_one).astype(jnp.bfloat16), "dp").astype(jnp.float32),
        lax.psum((group_share * norm_shift_one).astype(jnp.bfloat16), "dp").astype(jnp.float32),
        lax.psum((group_share * bias_hidden).astype(jnp.bfloat16), "dp").astype(jnp.float32),
        lax.psum((group_share * norm_gain_two).astype(jnp.bfloat16), "dp").astype(jnp.float32),
        lax.psum((group_share * norm_shift_two).astype(jnp.bfloat16), "dp").astype(jnp.float32),
        lax.psum((group_share * bias_out).astype(jnp.bfloat16), "dp").astype(jnp.float32),
        lax.psum((group_share * contract_gradient).astype(jnp.bfloat16), "dp").astype(jnp.float32),
        lax.psum((group_share * expand_gradient).astype(jnp.bfloat16), "dp").astype(jnp.float32),
        lax.psum((group_share * expand_bias_gradient).astype(jnp.bfloat16), "dp").astype(
            jnp.float32
        ),
    )
    return (
        layer_output,
        input_gradient,
        norm_gain_one,
        norm_shift_one,
        projection_gradient,
        query_value_gradient,
        output_gradient,
        bias_hidden,
        norm_gain_two,
        norm_shift_two,
        expand_gradient,
        expand_bias_gradient,
        contract_gradient,
        bias_out,
    )


def solution(mesh):
    placed = (
        P(("dp", "tensor"), None),
        P(),
        P(),
        P(),
        P(None, None, "tensor"),
        P(None, "tensor"),
        P("tensor", None),
        P(),
        P(),
        P(),
        P(None, "tensor"),
        P("tensor"),
        P("tensor", None),
        P(),
        P(("dp", "tensor"), None),
    )
    return jax.shard_map(
        shards,
        mesh=mesh,
        in_specs=placed,
        out_specs=(
            P(("dp", "tensor"), None),
            P(("dp", "tensor"), None),
            P("tensor"),
            P("tensor"),
            P(None, None, "tensor"),
            P(None, "tensor"),
            P("tensor", None),
            P("tensor"),
            P("tensor"),
            P("tensor"),
            P(None, "tensor"),
            P("tensor"),
            P("tensor", None),
            P("tensor"),
        ),
        check_vma=False,
    )
```

profile of v0, /device:TPU:0, one launch (start us, length us, event | category | flops | bytes accessed | tf_op | source)
XLA Modules:
  0.0 1579.6 jit_solution(6465452662989562798)
XLA Ops:
  10.3 84.1 %all-gather.4.cloned.1.call-done = bf16[2048,2048]{1,0:T(8,128)(2,1)} async-done(((bf16[256,2048]{1,0:T(8,128)(2,1)}), bf16[2048,2048]{1,0:T(8,128)(2,1)}) %all-gather.4.cloned.1.call-update) | async-done | bytes 8388624 | tf_op jit(solution)/shard_map/all_gather | solution.py:59
  94.4 4.7 convert_reduce_fusion
  102.6 8.6 add_convert_fusion.1
  119.7 51.7 %while.28 = (s32[]{:T(128)}, bf16[4,512,2,128]{3,2,1,0:T(2,128)(2,1)}, f32[4,2,512]{2,1,0:T(2,128)}, s32[4]{0:T(128)S(1)}, s32[2048]{0:T(1024)S(1)}, /*index=5*/...) while((s32[]{:T(128)}, ...), condition=%wide.region_7.8_spmd.clone, body=%wide.region_4.7_spmd.clone.sunk | while | flops 1102183936 | bytes 36751592 | solution.py:99
  135.2 3.4 fusion.144
  160.9 3.4 fusion.144
  171.4 9.6 fusion.71
  183.0 329.6 %all-reduce.12.cloned.1.call-done = f32[2048,2048]{1,0:T(8,128)} async-done(((f32[2048,2048]{1,0:T(8,128)}), f32[2048,2048]{1,0:T(8,128)}) %all-reduce.12.cloned.1.call-update) | async-done | bytes 16777232 | tf_op jit(solution)/shard_map/psum | solution.py:102
  512.6 15.9 %fusion.92 = (f32[2048]{0:T(1024)S(1)}, f32[2048,2048]{1,0:T(8,128)}) fusion(f32[2048]{0:T(1024)S(1)} %copy-done.29, f32[2048,2048]{1,0:T(8,128)} %all-reduce.12.cloned.1.call-done, bf16[2048,2048]{1,0:T(8,128)(2,1)} %all-gather.4.cloned.1.call-done), kind=kLoop, calls=%fused_computation.157 | loop fusion | flops 16775168 | bytes 41959424 | tf_op jit(solution)/shard_map/reduce_sum | solution.py:14
  528.5 7.7 multiply_reduce_fusion.1
  536.2 7.9 add_convert_fusion
  547.3 11.0 fusion.98
  558.3 38.1 %all-gather.6.cloned.1.call-done = bf16[2048,2048]{1,0:T(8,128)(2,1)} async-done(((bf16[256,2048]{1,0:T(8,128)(2,1)}), bf16[2048,2048]{1,0:T(8,128)(2,1)}) %all-gather.6.cloned.1.call-update) | async-done | bytes 8388624 | tf_op jit(solution)/shard_map/all_gather | solution.py:117
  596.4 20.9 %convert_reduce_fusion.1 = (f32[1024]{0:T(1024)}, bf16[2048,1024]{1,0:T(8,128)(2,1)S(1)}) fusion(f32[2048,1024]{1,0:T(8,128)} %fusion.98, f32[1024]{0:T(1024)S(1)} %copy-done.41, bf16[1024,2048]{1,0:T(8,128)(2,1)} %param.31, bf16[2048,2048]{1,0:T(8,128)(2,1)} %all-gather.6.cloned.1.call-done, pred[2048]{0:T(1024)(128)(4,1)S(1)} %iota_compare_fusion.2), kind=kOutput, calls=%fused_computation.74 | convolution fusion | flops 8642362368 | bytes 25176064 | tf_op jit(solution)/shard_map/td,fd->tf/dot_general | solution.py:122
  619.3 11.7 fusion.99
  631.1 15.4 convolution_convert_fusion
  650.9 147.1 %reduce-scatter.6.cloned.1.call-done = f32[256,2048]{1,0:T(8,128)} async-done(((f32[2048,2048]{1,0:T(8,128)}), f32[256,2048]{1,0:T(8,128)}) %reduce-scatter.6.cloned.1.call-update) | async-done | bytes 2097168 | tf_op jit(solution)/shard_map/reduce_scatter | solution.py:129
  798.0 3.5 multiply_reduce_fusion.2
  801.5 87.2 %reduce-scatter.4.cloned.1.call-done = bf16[256,2048]{1,0:T(8,128)(2,1)} async-done(((bf16[2048,2048]{1,0:T(8,128)(2,1)}), bf16[256,2048]{1,0:T(8,128)(2,1)}) %reduce-scatter.4.cloned.1.call-update) | async-done | bytes 1048592 | tf_op jit(solution)/shard_map/reduce_scatter | solution.py:107
  888.7 4.5 fusion.91
  898.0 14.2 multiply_convert_fusion.2
  912.2 17.2 %multiply_convert_fusion.1 = bf16[1024,2048]{1,0:T(8,128)(2,1)} fusion(f32[]{:T(128)S(6)} %div.73, bf16[2048,2048]{1,0:T(8,128)(2,1)} %all-gather.6.cloned.1.call-done, pred[2048]{0:T(1024)(128)(4,1)S(1)} %iota_compare_fusion.2, f32[2048,1024]{1,0:T(8,128)} %fusion.98, f32[1024]{0:T(1024)S(1)} %copy-done.41), kind=kOutput, calls=%fused_computation.73 | convolution fusion | flops 8619294720 | bytes 20977668 | tf_op jit(solution)/shard_map/tf,td->fd/dot_general | solution.py:119
  929.4 47.1 %all-gather.8.cloned.1.call-done = bf16[2048,2048]{1,0:T(8,128)(2,1)} async-done(((bf16[256,2048]{1,0:T(8,128)(2,1)}), bf16[2048,2048]{1,0:T(8,128)(2,1)}) %all-gather.8.cloned.1.call-update) | async-done | bytes 8388624 | tf_op jit(solution)/shard_map/all_gather | solution.py:138
  976.5 6.9 convolution_convert_fusion.1
  983.5 90.0 %while.29 = (s32[]{:T(128)}, f32[2048,2,128]{0,2,1:T(8,128)}, f32[2048,2,128]{0,2,1:T(8,128)}, bf16[4,512,2,128]{3,1,2,0:T(8,128)(2,1)}, s32[4]{0:T(128)S(1)}, /...) while((s32[]{:T(128)}, f32[2048,2,128]{0,2,1:T(8,128)}, ...), condition=%wide.region_19.20_spmd.clone, body=%wide.region_17.19_spmd.clone.sunk | while | flops 2721709568 | bytes 101235080 | solution.py:175
  989.5 3.7 fusion.159
  993.3 3.8 multiply_reduce_fusion.6
  1001.1 3.4 fusion.158
  1010.4 5.0 fusion.159
  1015.4 3.9 multiply_reduce_fusion.6
  1023.2 4.3 fusion.158
  1033.4 5.0 fusion.159
  1038.4 3.8 multiply_reduce_fusion.6
  1046.2 4.3 fusion.158
  1056.4 5.0 fusion.159
  1061.4 3.9 multiply_reduce_fusion.6
  1069.2 4.3 fusion.158
  1089.6 7.2 fusion.62
  1096.8 13.1 multiply_convert_fusion.4
  1109.9 12.3 convolution_bitcast_fusion
  1128.3 221.9 %all-reduce.14.cloned.1.call-done = (bf16[2048,3,256]{2,0,1:T(8,128)(2,1)}, bf16[256,2048]{1,0:T(8,128)(2,1)}, bf16[2048,1024]{1,0:T(8,128)(2,1)}, bf16[1024,2048]{1,0:T(8,128)(2,1)}) async-done(((bf16[2048,3,256]{2,0,1:T(8,128)(2,1)}, bf16[256,2048]{1,0:T(8,128)(2,1)}, bf16[2048,1024]{1,0:T(8,128)(2,1)}, bf16[1024,2048]{1,0:T(8,128)(2,1)}), (bf16[2048,3,256]{2,0,1:T(8,128)(2,1)}, ...) | async-done | bytes 12582928 | tf_op jit(solution)/shard_map/psum | solution.py:224
  1353.1 5.1 convert_element_type.172
  1358.3 4.4 convert_element_type.185
  1362.7 4.4 convert_element_type.190
  1367.2 153.7 %reduce-scatter.8.cloned.1.call-done = f32[256,2048]{1,0:T(8,128)} async-done(((f32[2048,2048]{1,0:T(8,128)}), f32[256,2048]{1,0:T(8,128)}) %reduce-scatter.8.cloned.1.call-update) | async-done | bytes 2097168 | tf_op jit(solution)/shard_map/reduce_scatter | solution.py:191
  1526.2 5.1 fusion.69
  1531.3 26.4 %all-reduce.6 = (f32[2048]{0:T(1024)S(1)}, f32[2048]{0:T(1024)S(1)}, f32[2048]{0:T(1024)S(1)}, f32[2048]{0:T(1024)S(1)}, f32[2048]{0:T(1024)S(1)}, /*index=5*/f32[2048]{0:T(1024)S(1)}) all-reduce(f32[2048]{0:T(1024)S(1)} %get-tuple-element.265, ...), channel_id=5, replica_groups=mesh['dp'=4,'tensor'=8] {'tensor'}, use_global_device_ids=true, to_apply=%region_27.28.clone | all-reduce | flops 12288 | bytes 98304
  1558.0 10.0 all-reduce.7
  (268 shorter events, 142.9 us)
Async XLA Ops:
  7.2 95.3 %copy-start = (bf16[2048,3,256]{2,0,1:T(8,128)(2,1)S(1)}, bf16[2048,3,256]{2,0,1:T(8,128)(2,1)}, u32[]{:S(2)}) copy-start(bf16[2048,3,256]{2,0,1:T(8,128)(2,1)} %param.23) | copy-start | bytes 9437188
  7.2 87.2 %all-gather.4.cloned.1.call-start = ((), (), s32[]{:S(2)}) async-start(), calls=%async_computation.3 | async-start | bytes 9437184 | tf_op jit(solution)/shard_map/all_gather | solution.py:59
  7.9 504.7 %all-reduce.12.cloned.1.call-start = ((), (), s32[]{:S(2)}) async-start(), calls=%async_computation.4 | async-start | bytes 33554432 | tf_op jit(solution)/shard_map/psum | solution.py:102
  10.3 92.2 %copy-start.18 = (f32[2048]{0:T(1024)S(1)}, f32[2048]{0:T(1024)}, u32[]{:S(2)}) copy-start(f32[2048]{0:T(1024)} %param.21) | copy-start | bytes 24580
  10.3 92.2 %copy-start.39 = (f32[2048]{0:T(1024)S(1)}, f32[2048]{0:T(1024)}, u32[]{:S(2)}) copy-start(f32[2048]{0:T(1024)} %param.22) | copy-start | bytes 24580
  94.4 5.8 copy-start.2
  100.2 11.0 copy-start.23
  102.5 8.7 copy-start.31
  122.3 5.9 copy-start.3
  135.1 5.9 copy-start.3
  148.0 5.9 copy-start.3
  160.9 5.9 copy-start.3
  171.4 9.6 copy-start.14
  181.0 331.5 %copy-start.29 = (f32[2048]{0:T(1024)S(1)}, f32[2048]{0:T(1024)}, u32[]{:S(2)}) copy-start(f32[2048]{0:T(1024)} %param.26) | copy-start | bytes 24580
  181.1 415.3 %all-gather.6.cloned.1.call-start = ((), (), s32[]{:S(2)}) async-start(), calls=%async_computation.6 | async-start | bytes 9437184 | tf_op jit(solution)/shard_map/all_gather | solution.py:117
  181.8 616.2 %reduce-scatter.6.cloned.1.call-start = ((), (), s32[]{:S(2)}) async-start(), calls=%async_computation.7 | async-start | bytes 18874368 | tf_op jit(solution)/shard_map/reduce_scatter | solution.py:129
  528.5 7.7 copy-start.20
  528.5 7.7 copy-start.30
  536.2 11.1 copy-start.37
  547.3 49.1 %copy-start.41 = (f32[1024]{0:T(1024)S(1)}, f32[1024]{0:T(1024)}, u32[]{:S(2)}) copy-start(f32[1024]{0:T(1024)} %param.30) | copy-start | bytes 12292
  596.4 22.9 %copy-start.38 = (bf16[2048,1024]{1,0:T(8,128)(2,1)S(1)}, bf16[2048,1024]{1,0:T(8,128)(2,1)}, u32[]{:S(2)}) copy-start(bf16[2048,1024]{1,0:T(8,128)(2,1)} %param.29) | copy-start | bytes 12582916
  631.0 257.6 %reduce-scatter.4.cloned.1.call-start = ((), (), s32[]{:S(2)}) async-start(), calls=%async_computation.5 | async-start | bytes 9437184 | tf_op jit(solution)/shard_map/reduce_scatter | solution.py:107
  646.5 242.2 %copy-start.33 = (f32[2048]{0:T(1024)S(1)}, f32[2048]{0:T(1024)}, u32[]{:S(2)}) copy-start(f32[2048]{0:T(1024)} %param.32) | copy-start | bytes 24580
  646.6 330.0 %all-gather.8.cloned.1.call-start = ((), (), s32[]{:S(2)}) async-start(), calls=%async_computation.8 | async-start | bytes 9437184 | tf_op jit(solution)/shard_map/all_gather | solution.py:138
  647.1 246.1 %copy-start.25 = (f32[256]{0:T(256)}, f32[256]{0:T(256)S(1)}, u32[]{:S(2)}) copy-start(f32[256]{0:T(256)S(1)} %dynamic-slice_convert_fusion) | copy-start | bytes 3076
  650.9 245.8 %copy-start.35 = (s32[4,2]{0,1:T(2,128)S(1)}, s32[4,2]{0,1:T(2,128)}, u32[]{:S(2)}) copy-start(s32[4,2]{0,1:T(2,128)} %copy-done.34) | copy-start | bytes 100
  888.7 5.9 copy-start.6
  896.0 454.2 %all-reduce.14.cloned.1.call-start = ((), (), s32[]{:S(2)}) async-start(), calls=%async_computation.10 | async-start | bytes 25165824 | tf_op jit(solution)/shard_map/psum | solution.py:224
  929.4 54.0 %copy-start.15 = (s32[2048]{0:T(1024)S(1)}, s32[2048]{0:T(1024)}, u32[]{:S(2)}) copy-start(s32[2048]{0:T(1024)} %copy-done.14) | copy-start | bytes 24580
  1005.7 4.6 copy-start.13
  1010.4 5.0 copy-start.4
  1028.7 4.6 copy-start.13
  1033.4 5.0 copy-start.4
  1051.7 4.6 copy-start.13
  1056.4 5.0 copy-start.4
  1089.5 7.2 copy-start.10
  1089.5 7.2 copy-start.11
  1089.5 7.2 copy-start.12
  1089.5 7.2 copy-start.19
  1089.5 7.2 copy-start.24
  1089.5 7.2 copy-start.32
  1089.5 7.2 copy-start.40
  1109.9 411.0 %reduce-scatter.8.cloned.1.call-start = ((), (), s32[]{:S(2)}) async-start(), calls=%async_computation.9 | async-start | bytes 18874368 | tf_op jit(solution)/shard_map/reduce_scatter | solution.py:191
  1350.2 8.1 copy-start.9
  1362.7 163.5 %copy-start.26 = (f32[256]{0:T(256)S(1)}, f32[256]{0:T(256)}, u32[]{:S(2)}) copy-start(f32[256]{0:T(256)} %copy-done.25) | copy-start | bytes 3076
  1362.7 163.5 %copy-start.28 = (f32[256]{0:T(256)S(1)}, f32[256]{0:T(256)}, u32[]{:S(2)}) copy-start(f32[256]{0:T(256)} %copy-done.27) | copy-start | bytes 3076
  1367.2 164.2 %copy-start.21 = (f32[2048]{0:T(1024)S(1)}, f32[2048]{0:T(1024)}, u32[]{:S(2)}) copy-start(f32[2048]{0:T(1024)} %get-tuple-element.263) | copy-start | bytes 24580
  1367.2 164.2 %copy-start.22 = (f32[2048]{0:T(1024)S(1)}, f32[2048]{0:T(1024)}, u32[]{:S(2)}) copy-start(f32[2048]{0:T(1024)} %get-tuple-element.267) | copy-start | bytes 24580
  (22 other events, 62.7 us)
Sparse Core Ops, SparseCore 0:
  9.6 84.7 all-gather.3
  181.2 331.3 all-reduce.11
  514.2 82.1 all-gather.5
  631.2 166.7 reduce-scatter.5
  800.7 87.9 reduce-scatter.3
  896.1 80.3 all-gather.7
  1110.0 240.1 all-reduce.13
  1352.6 168.2 reduce-scatter.7
where the time goes:
time: 1580 us
  waiting for transfers between devices  1110 us (70%)
  matrix products  239 us (15%)
  other arithmetic  128 us (8%)
  local copies, waits for them, and re-layouts  42.2 us (3%)
  blocking collectives  36.4 us (2%)
  between operations  16.9 us (1%)
    psum x1, waiting for transfers between devices, shards(): lax.psum(partial_sum, 'tensor')  330 us
    psum x1, waiting for transfers between devices, shards(): lax.psum((group_share * projection_gradient).astype(jnp.bfloat16), 'dp')  222 us
    reduce_scatter x1, waiting for transfers between devices, shards(): lax.psum_scatter(jnp.einsum('tcj,dcj->td', projected_grad, query_key_valu...  154 us
    reduce_scatter x1, waiting for transfers between devices, shards(): lax.psum_scatter(jnp.einsum('tf,df->td', grad_pre, expand_weight, preferr...  147 us
    reduce_scatter x1, waiting for transfers between devices, shards(): lax.psum_scatter(jnp.dot(activated, contract_weight, preferred_element_ty...  87.2 us
    all_gather x1, waiting for transfers between devices, shards(): all_tokens = lax.all_gather(tokens, 'tensor', axis=0, tiled=True)  84.1 us
    all_gather x1, waiting for transfers between devices, shards(): lax.all_gather(grad_hidden.astype(jnp.bfloat16), 'tensor', axis=0, tiled=...  47.1 us
    all_gather x1, waiting for transfers between devices, shards(): cotangent_all = lax.all_gather(cotangent, 'tensor', axis=0, tiled=True)  38.1 us
  transfers between devices with their start and end apart: 8, of which 8 were waited for; matrix products, arithmetic and copies ran while one was open for 9% of the time, Pallas kernels for 0%

commit v1 on v0

v1 whole, which is shorter than its diff:
```python
import functools
import math

import jax
import jax.numpy as jnp
from jax import lax
from jax.experimental import pallas as pl
from jax.experimental.pallas import tpu as pltpu
from jax.sharding import PartitionSpec as P

HEAD_DIM = 128
BLOCK = 512
EPSILON = 1e-05
SCALE = HEAD_DIM ** (-0.5)
SCALE_LOG2 = SCALE * math.log2(math.e)
MASKED = -1e30
VMEM_LIMIT = 48 * 1024 * 1024


def dot(a, b, contract):
    return lax.dot_general(a, b, (contract, ((), ())), preferred_element_type=jnp.float32)


def segment_start(position, first, second):
    return jnp.where(position >= second, second, jnp.where(position >= first, first, 0))


def segment_end(position, first, second, rows):
    return jnp.where(position >= second, rows, jnp.where(position >= first, second, first))


def attend_kernel(block, bounds_ref, q_ref, k_ref, v_ref, out_ref, total_ref):
    query_block = pl.program_id(1)
    first, second = bounds_ref[0], bounds_ref[1]
    offset = query_block * block
    q = q_ref[...]
    q_pos = offset + lax.broadcasted_iota(jnp.int32, (1, block), 1)
    start = segment_start(q_pos, first, second)
    k_row = lax.broadcasted_iota(jnp.int32, (block, block), 0)

    def step(key_block, carry):
        highest, row_sum, acc = carry
        rows = pl.ds(pl.multiple_of(key_block * block, block), block)
        scores = dot(k_ref[rows, :], q, ((1,), (1,)))
        base = key_block * block
        allowed = (k_row <= q_pos - base) & (k_row >= start - base)
        scores = jnp.where(allowed, scores * SCALE_LOG2, MASKED)
        new_highest = jnp.maximum(highest, jnp.max(scores, axis=0, keepdims=True))
        weights = jnp.exp2(scores - new_highest)
        decay = jnp.exp2(highest - new_highest)
        row_sum = row_sum * decay + jnp.sum(weights, axis=0, keepdims=True)
        acc = acc * decay + dot(v_ref[rows, :], weights.astype(jnp.bfloat16), ((0,), (0,)))
        return new_highest, row_sum, acc

    low = segment_start(offset, first, second) // block
    highest, row_sum, acc = lax.fori_loop(
        low,
        query_block + 1,
        step,
        (
            jnp.full((1, block), MASKED, jnp.float32),
            jnp.zeros((1, block), jnp.float32),
            jnp.zeros((HEAD_DIM, block), jnp.float32),
        ),
    )
    out_ref[...] = jnp.transpose(acc / row_sum).astype(jnp.bfloat16)
    total_ref[0] = highest + jnp.log2(row_sum)


def attend(bounds, projected, local_heads):
    rows = projected.shape[0]
    block = min(BLOCK, rows)
    return pl.pallas_call(
        functools.partial(attend_kernel, block),
        grid_spec=pltpu.PrefetchScalarGridSpec(
            num_scalar_prefetch=1,
            grid=(local_heads, rows // block),
            in_specs=[
                pl.BlockSpec((block, HEAD_DIM), lambda h, i, _: (i, h)),
                pl.BlockSpec((rows, HEAD_DIM), lambda h, i, _: (0, local_heads + h)),
                pl.BlockSpec((rows, HEAD_DIM), lambda h, i, _: (0, 2 * local_heads + h)),
            ],
            out_specs=[
                pl.BlockSpec((block, HEAD_DIM), lambda h, i, _: (i, h)),
                pl.BlockSpec((1, 1, block), lambda h, i, _: (h, 0, i)),
            ],
        ),
        out_shape=[
            jax.ShapeDtypeStruct((rows, local_heads * HEAD_DIM), jnp.bfloat16),
            jax.ShapeDtypeStruct((local_heads, 1, rows), jnp.float32),
        ],
        compiler_params=pltpu.CompilerParams(vmem_limit_bytes=VMEM_LIMIT),
        cost_estimate=pl.CostEstimate(
            flops=4 * local_heads * rows * rows * HEAD_DIM,
            bytes_accessed=8 * rows * local_heads * HEAD_DIM,
            transcendentals=local_heads * rows * rows,
        ),
    )(bounds, projected, projected, projected)


def attend_back_kernel(
    block,
    local_heads,
    bounds_ref,
    q_ref,
    k_ref,
    v_ref,
    grad_ref,
    context_ref,
    total_ref,
    out_ref,
    query_acc,
    key_acc,
    value_acc,
    inner_ref,
):
    head = pl.program_id(0)
    first, second = bounds_ref[0], bounds_ref[1]
    rows = q_ref.shape[0]
    width = local_heads * HEAD_DIM
    k_row = lax.broadcasted_iota(jnp.int32, (block, block), 0)
    q_col = lax.broadcasted_iota(jnp.int32, (1, block), 1)
    for i in range(rows // block):
        part = pl.ds(i * block, block)
        product = grad_ref[part, :].astype(jnp.float32) * context_ref[part, :].astype(jnp.float32)
        inner_ref[:, part] = jnp.sum(jnp.transpose(product), axis=0, keepdims=True)
    query_acc[...] = jnp.zeros_like(query_acc)

    def key_step(key_block, _):
        base = pl.multiple_of(key_block * block, block)
        key_rows = pl.ds(base, block)
        key_acc[...] = jnp.zeros_like(key_acc)
        value_acc[...] = jnp.zeros_like(value_acc)

        def query_step(query_block, _):
            offset = pl.multiple_of(query_block * block, block)
            query_rows = pl.ds(offset, block)
            k = k_ref[key_rows, :]
            q = q_ref[query_rows, :]
            grad = grad_ref[query_rows, :]
            q_pos = offset + q_col
            start = segment_start(q_pos, first, second)
            scores = dot(k, q, ((1,), (1,)))
            allowed = (k_row <= q_pos - base) & (k_row >= start - base)
            exponent = jnp.where(
                allowed, scores * SCALE_LOG2 - total_ref[0, :, query_rows], MASKED
            )
            weights = jnp.exp2(exponent)
            grad_weights = dot(v_ref[key_rows, :], grad, ((1,), (1,)))
            score_grad = (weights * (grad_weights - inner_ref[:, query_rows])).astype(jnp.bfloat16)
            value_acc[...] += dot(weights.astype(jnp.bfloat16), grad, ((1,), (0,)))
            key_acc[...] += dot(score_grad, q, ((1,), (0,)))
            query_acc[query_rows, :] += dot(score_grad, k, ((0,), (0,)))
            return 0

        last = segment_end(base + block - 1, first, second, rows) - 1
        lax.fori_loop(key_block, last // block + 1, query_step, 0)
        key_columns = pl.ds(pl.multiple_of(width + head * HEAD_DIM, HEAD_DIM), HEAD_DIM)
        value_columns = pl.ds(pl.multiple_of(2 * width + head * HEAD_DIM, HEAD_DIM), HEAD_DIM)
        out_ref[key_rows, key_columns] = (key_acc[...] * SCALE).astype(jnp.bfloat16)
        out_ref[key_rows, value_columns] = value_acc[...].astype(jnp.bfloat16)
        return 0

    lax.fori_loop(0, rows // block, key_step, 0)
    query_columns = pl.ds(pl.multiple_of(head * HEAD_DIM, HEAD_DIM), HEAD_DIM)
    out_ref[:, query_columns] = (query_acc[...] * SCALE).astype(jnp.bfloat16)


def attend_back(bounds, projected, grad_context, context, totals, local_heads):
    rows = projected.shape[0]
    block = min(BLOCK, rows)
    width = local_heads * HEAD_DIM
    column = pl.BlockSpec((rows, HEAD_DIM), lambda h, _: (0, h))
    return pl.pallas_call(
        functools.partial(attend_back_kernel, block, local_heads),
        grid_spec=pltpu.PrefetchScalarGridSpec(
            num_scalar_prefetch=1,
            grid=(local_heads,),
            in_specs=[
                column,
                pl.BlockSpec((rows, HEAD_DIM), lambda h, _: (0, local_heads + h)),
                pl.BlockSpec((rows, HEAD_DIM), lambda h, _: (0, 2 * local_heads + h)),
                column,
                column,
                pl.BlockSpec((1, 1, rows), lambda h, _: (h, 0, 0)),
            ],
            out_specs=pl.BlockSpec((rows, 3 * width), lambda h, _: (0, 0)),
            scratch_shapes=[
                pltpu.VMEM((rows, HEAD_DIM), jnp.float32),
                pltpu.VMEM((block, HEAD_DIM), jnp.float32),
                pltpu.VMEM((block, HEAD_DIM), jnp.float32),
                pltpu.VMEM((1, rows), jnp.float32),
            ],
        ),
        out_shape=jax.ShapeDtypeStruct((rows, 3 * width), jnp.bfloat16),
        compiler_params=pltpu.CompilerParams(vmem_limit_bytes=VMEM_LIMIT),
        cost_estimate=pl.CostEstimate(
            flops=10 * local_heads * rows * rows * HEAD_DIM,
            bytes_accessed=16 * rows * width,
            transcendentals=local_heads * rows * rows,
        ),
    )(bounds, projected, projected, projected, grad_context, context, totals)


def normalize(values):
    center = values - jnp.mean(values, axis=-1, keepdims=True)
    inverse = lax.rsqrt(jnp.mean(center * center, axis=-1, keepdims=True) + EPSILON)
    return center * inverse, inverse


def normalize_back(grad, gain, unit, inverse):
    scaled = grad * gain
    return inverse * (
        scaled
        - jnp.mean(scaled, axis=-1, keepdims=True)
        - unit * jnp.mean(scaled * unit, axis=-1, keepdims=True)
    )


def gelu_tanh(values):
    return jax.nn.gelu(values, approximate=True)


def after(value, *earlier):
    return lax.optimization_barrier((value,) + earlier)[0]


def ring_order(chips):
    return [c for c in range(chips) if c == 0 or c % 2] + [
        c for c in reversed(range(2, chips)) if c % 2 == 0
    ]


def ring_step(value):
    size = lax.axis_size("tensor")
    order = ring_order(size // 2)
    pairs = []
    for place, chip in enumerate(order):
        following = order[(place + 1) % len(order)]
        pairs += [(2 * chip, 2 * following), (2 * chip + 1, 2 * following + 1)]
    return lax.ppermute(value, "tensor", pairs)


def swap_cores(value):
    return lax.ppermute(value, "tensor", [(i, i ^ 1) for i in range(lax.axis_size("tensor"))])


def ring_chip(step):
    chips = lax.axis_size("tensor") // 2
    order = ring_order(chips)
    places = jnp.array([order.index(c) for c in range(chips)], jnp.int32)
    place = places[lax.axis_index("tensor") // 2]
    return jnp.array(order, jnp.int32)[(place + chips - step) % chips]


def ring_gather(block):
    moving = block
    pairs = []
    for step in range(lax.axis_size("tensor") // 2):
        if step:
            moving = ring_step(moving)
        pairs.append((moving, swap_cores(moving)))
    return pairs


def ring_scatter(part):
    arrived = None
    chips = lax.axis_size("tensor") // 2
    for step in list(range(1, chips)) + [0]:
        mine, other = part(step)
        total = mine.astype(jnp.float32) + swap_cores(other).astype(jnp.float32)
        if arrived is not None:
            total = total + arrived.astype(jnp.float32)
        if step:
            arrived = ring_step(total.astype(jnp.bfloat16))
    return total


def in_order(pairs):
    size = lax.axis_size("tensor")
    core = lax.axis_index("tensor") % 2
    block = pairs[0][0]
    full = jnp.zeros((size,) + block.shape, block.dtype)
    for step, (mine, other) in enumerate(pairs):
        chip = ring_chip(step)
        full = lax.dynamic_update_index_in_dim(full, mine, 2 * chip + core, 0)
        full = lax.dynamic_update_index_in_dim(full, other, 2 * chip + 1 - core, 0)
    return full


def dp_sum(value):
    size = lax.axis_size("dp")
    me = lax.axis_index("dp")
    bits = [1 << i for i in range((size - 1).bit_length())]

    def flip(x, bit):
        return lax.ppermute(x, "dp", [(i, i ^ bit) for i in range(size)])

    def one(x, bits):
        for bit in bits:
            half = x.shape[0] // 2
            up = (me & bit) != 0
            keep = lax.dynamic_slice_in_dim(x, jnp.where(up, half, 0), half)
            give = lax.dynamic_slice_in_dim(x, jnp.where(up, 0, half), half)
            got = flip(give, bit)
            x = (keep.astype(jnp.float32) + got.astype(jnp.float32)).astype(x.dtype)
        for bit in reversed(bits):
            up = (me & bit) != 0
            got = flip(x, bit)
            x = jnp.concatenate([jnp.where(up, got, x), jnp.where(up, x, got)], axis=0)
        return x

    half = value.shape[0] // 2
    return jnp.concatenate([one(value[:half], bits), one(value[half:], bits[::-1])], axis=0)


def small_sum(value, axes):
    for axis in axes:
        size = lax.axis_size(axis)
        bit = 1
        while bit < size:
            value = value + lax.ppermute(value, axis, [(i, i ^ bit) for i in range(size)])
            bit *= 2
    return value


def shards(
    tokens,
    lengths,
    attention_gain,
    attention_shift,
    query_key_value,
    query_value_bias,
    output_weight,
    output_bias,
    feedforward_gain,
    feedforward_shift,
    expand_weight,
    expand_bias,
    contract_weight,
    contract_bias,
    cotangent,
):
    bf16, f32 = jnp.bfloat16, jnp.float32
    shard_rows, features = tokens.shape
    tensor_size = lax.axis_size("tensor")
    group_count = lax.axis_size("dp")
    group = lax.axis_index("dp")
    rank = lax.axis_index("tensor")
    core = rank % 2
    chips = tensor_size // 2
    group_rows = shard_rows * tensor_size
    local_width = query_key_value.shape[2]
    local_heads = local_width // HEAD_DIM
    bounds = jnp.cumsum(lengths, axis=1)
    own_bounds = lax.dynamic_index_in_dim(bounds, group, 0, keepdims=False)
    own_count = own_bounds[-1]
    share = own_count.astype(f32) / jnp.sum(bounds[:, -1]).astype(f32)
    local_rows = rank * shard_rows + jnp.arange(shard_rows, dtype=jnp.int32)
    local_live = (local_rows < own_count).astype(f32)[:, None]

    input_rows = tokens.astype(f32)
    unit_one, inverse_one = normalize(input_rows)
    normed_rows = (unit_one * attention_gain + attention_shift).astype(bf16)
    normed = lax.all_gather(normed_rows, "tensor", axis=0, tiled=True)

    piece = output_weight.shape[0] // group_count
    own_piece = lax.dynamic_slice_in_dim(output_weight, group * piece, piece)
    pieces = in_order(ring_gather(own_piece))
    output_full = lax.all_gather(pieces, "dp", axis=1, tiled=False).reshape(features, features)

    weight_flat = query_key_value.reshape(features, 3 * local_width)
    bias_flat = jnp.concatenate(
        [query_value_bias[0], jnp.zeros_like(query_value_bias[0]), query_value_bias[1]]
    )
    projected = (jnp.dot(normed, weight_flat, preferred_element_type=f32) + bias_flat).astype(bf16)

    grad_rows_low = jnp.where(local_live > 0, cotangent, jnp.zeros_like(cotangent))
    grad_out = [
        jnp.concatenate(pair, axis=0) for pair in ring_gather(after(grad_rows_low, normed))
    ]
    grad_activated = [
        jnp.einsum("td,fd->tf", block, contract_weight, preferred_element_type=f32)
        for block in grad_out
    ]

    context, totals = attend(own_bounds, projected, local_heads)
    context_rows = lax.all_to_all(context, "tensor", split_axis=0, concat_axis=1, tiled=True)
    hidden = (
        input_rows + jnp.dot(context_rows, output_full, preferred_element_type=f32) + output_bias
    )
    unit_two, inverse_two = normalize(hidden)
    mixed_rows = (unit_two * feedforward_gain + feedforward_shift).astype(bf16)

    mixed = [jnp.concatenate(pair, axis=0) for pair in ring_gather(mixed_rows)]
    activated, grad_pre = [None] * chips, [None] * chips
    for step in range(chips):
        pre_act = jnp.dot(mixed[step], expand_weight, preferred_element_type=f32) + expand_bias
        value, gelu_pull = jax.vjp(gelu_tanh, pre_act)
        activated[step] = value.astype(bf16)
        grad_pre[step] = gelu_pull(grad_activated[step])[0].astype(bf16)

    def mixed_part(step):
        part = jnp.einsum(
            "tf,df->td", grad_pre[step], expand_weight, preferred_element_type=f32
        ).astype(bf16)
        return part[:shard_rows], part[shard_rows:]

    grad_mixed = ring_scatter(mixed_part)

    grad_local = grad_rows_low.astype(f32)
    grad_hidden = grad_local + normalize_back(grad_mixed, feedforward_gain, unit_two, inverse_two)
    grad_hidden_low = grad_hidden.astype(bf16)
    grad_context_rows = jnp.einsum(
        "td,jd->tj", grad_hidden_low, output_full, preferred_element_type=f32
    ).astype(bf16)
    grad_context = lax.all_to_all(
        grad_context_rows, "tensor", split_axis=1, concat_axis=0, tiled=True
    )
    projected_grad = attend_back(own_bounds, projected, grad_context, context, totals, local_heads)

    def normed_part(step):
        rows = lax.dynamic_slice_in_dim(
            projected_grad, ring_chip(step) * 2 * shard_rows, 2 * shard_rows
        )
        part = jnp.einsum("tj,dj->td", rows, weight_flat, preferred_element_type=f32).astype(bf16)
        return (
            lax.dynamic_slice_in_dim(part, core * shard_rows, shard_rows),
            lax.dynamic_slice_in_dim(part, (1 - core) * shard_rows, shard_rows),
        )

    grad_normed = ring_scatter(normed_part)
    input_gradient = (
        grad_hidden + normalize_back(grad_normed, attention_gain, unit_one, inverse_one)
    ).astype(bf16)

    def branch_part(step):
        part = jnp.dot(
            after(activated[step], grad_mixed), contract_weight, preferred_element_type=f32
        ).astype(bf16)
        return part[:shard_rows], part[shard_rows:]

    branch = ring_scatter(branch_part)
    layer_output = (local_live * (hidden + branch + contract_bias)).astype(bf16)

    activated_all = jnp.concatenate(activated, axis=0)
    grad_out_all = jnp.concatenate(grad_out, axis=0)
    contract_gradient = dp_sum(
        (
            share
            * jnp.einsum("tf,td->fd", activated_all, grad_out_all, preferred_element_type=f32)
        ).astype(bf16)
    )
    mixed_all = jnp.concatenate(mixed, axis=0)
    grad_pre_all = jnp.concatenate(grad_pre, axis=0)
    expand_gradient = dp_sum(
        (
            share * jnp.einsum("td,tf->df", mixed_all, grad_pre_all, preferred_element_type=f32)
        ).astype(bf16)
    )
    grad_hidden_all = lax.all_gather(
        after(grad_hidden_low, grad_context), "tensor", axis=0, tiled=True
    )
    output_gradient = dp_sum(
        (
            share * jnp.einsum("tj,td->jd", context, grad_hidden_all, preferred_element_type=f32)
        ).astype(bf16)
    )
    projection_gradient = dp_sum(
        (
            share * jnp.einsum("td,tj->dj", normed, projected_grad, preferred_element_type=f32)
        ).astype(bf16)
    ).reshape(features, 3, local_width)

    column_sums = jnp.sum(projected_grad.astype(f32), axis=0)
    sums_by_width = share * jnp.concatenate(
        [
            column_sums[:local_width],
            column_sums[2 * local_width :],
            jnp.sum(grad_pre_all.astype(f32), axis=0),
        ]
    )
    sums_by_width = small_sum(sums_by_width, ("dp",))
    query_value_gradient = sums_by_width[: 2 * local_width].reshape(2, local_width)
    expand_bias_gradient = sums_by_width[2 * local_width :]

    early_sums = share * jnp.stack(
        [
            jnp.sum(grad_hidden, axis=0),
            jnp.sum(grad_mixed * unit_two, axis=0),
            jnp.sum(grad_mixed, axis=0),
            jnp.sum(grad_local, axis=0),
        ]
    )
    late_sums = share * jnp.stack(
        [jnp.sum(grad_normed * unit_one, axis=0), jnp.sum(grad_normed, axis=0)]
    )
    columns = features // tensor_size
    early_sums = lax.dynamic_slice_in_dim(
        small_sum(early_sums, ("tensor", "dp")), rank * columns, columns, 1
    )
    late_sums = lax.dynamic_slice_in_dim(
        small_sum(late_sums, ("tensor", "dp")), rank * columns, columns, 1
    )
    return (
        layer_output,
        input_gradient,
        late_sums[0],
        late_sums[1],
        projection_gradient.astype(f32),
        query_value_gradient,
        output_gradient.astype(f32),
        early_sums[0],
        early_sums[1],
        early_sums[2],
        expand_gradient.astype(f32),
        expand_bias_gradient,
        contract_gradient.astype(f32),
        early_sums[3],
    )


def solution(mesh):
    placed = (
        P(("dp", "tensor"), None),
        P(),
        P(),
        P(),
        P(None, None, "tensor"),
        P(None, "tensor"),
        P("tensor", None),
        P(),
        P(),
        P(),
        P(None, "tensor"),
        P("tensor"),
        P("tensor", None),
        P(),
        P(("dp", "tensor"), None),
    )
    return jax.shard_map(
        shards,
        mesh=mesh,
        in_specs=placed,
        out_specs=(
            P(("dp", "tensor"), None),
            P(("dp", "tensor"), None),
            P("tensor"),
            P("tensor"),
            P(None, None, "tensor"),
            P(None, "tensor"),
            P("tensor", None),
            P("tensor"),
            P("tensor"),
            P("tensor"),
            P(None, "tensor"),
            P("tensor"),
            P("tensor", None),
            P("tensor"),
        ),
        check_vma=False,
    )
```

time: 1580 us -> 848 us (0.54)
  waiting for transfers between devices: 1110 us -> 427 us
  matrix products: 239 us -> 136 us
  starting transfers between devices: 0.73 us -> 97.6 us
  other arithmetic: 128 us -> 65 us
  Pallas kernels: 0 us -> 37.5 us
  blocking collectives: 36.4 us -> 0 us
    psum x2 -> x0, waiting for transfers between devices: 551 us -> none  [the longest x1 330 us: shards(): lax.psum(partial_sum, 'tensor')]
    ppermute x0 -> x86, waiting for transfers between devices: none -> 392 us  [the longest x18 295 us: ring_step(): return lax.ppermute(value, 'tensor', pairs)]
    reduce_scatter x3 -> x0, waiting for transfers between devices: 388 us -> none  [the longest x1 154 us: shards(): lax.psum_scatter(jnp.einsum('tcj,dcj->td', projected_grad, query_key_valu...]
    all_gather x3, waiting for transfers between devices: 169 us -> 34.1 us  [the longest x1 24.1 us: shards(): normed = lax.all_gather(normed_rows, 'tensor', axis=0, tiled=True)]
    dot_general x39 -> x26, matrix products: 232 us -> 131 us  [the longest x4 32.1 us: shards(): jnp.einsum('td,fd->tf', block, contract_weight, preferred_element_type=f32)]
    ppermute x0 -> x86, starting transfers between devices: none -> 88.7 us  [the longest x32 40 us: flip(): return lax.ppermute(x, 'dp', [(i, i ^ bit) for i in range(size)])]
    reduce_sum x18 -> x9, other arithmetic: 62.5 us -> 13.5 us  [the longest x1 4.16 us: shards(): jnp.sum(grad_normed * unit_one, axis=0)]
    pallas_call x0 -> x2, Pallas kernels: none -> 37.5 us  [the longest x1 21.6 us: attend_back(): pl.pallas_call(functools.partial(attend_back_kernel, block, local_heads),...]
  transfers between devices with their start and end apart: 8 -> 91, of which waited for: 8 -> 43; matrix products, arithmetic and copies ran while one was open for 9% -> 28% of each run, Pallas kernels for 0% -> 4%
where the time goes in v1:
time: 848 us; the launch traced here: 843 us
  waiting for transfers between devices  427 us (50%)
  matrix products  136 us (16%)
  starting transfers between devices  97.6 us (12%)
  other arithmetic  65 us (8%)
  local copies, waits for them, and re-layouts  55.4 us (7%)
  Pallas kernels  37.5 us (4%)
  between operations  24.9 us (3%)
    ppermute x18, waiting for transfers between devices, ring_step(): return lax.ppermute(value, 'tensor', pairs)  295 us
    ppermute x32, waiting for transfers between devices, flip(): return lax.ppermute(x, 'dp', [(i, i ^ bit) for i in range(size)])  67.7 us
    ppermute x32, starting transfers between devices, flip(): return lax.ppermute(x, 'dp', [(i, i ^ bit) for i in range(size)])  40 us
    dot_general x4, matrix products, shards(): jnp.einsum('td,fd->tf', block, contract_weight, preferred_element_type=f32)  32.1 us
    ppermute x18, starting transfers between devices, ring_step(): return lax.ppermute(value, 'tensor', pairs)  30.3 us
    ppermute x12, waiting for transfers between devices, small_sum(): lax.ppermute(value, axis, [(i, i ^ bit) for i in range(size)])  29.5 us
    unnamed x111, local copies, waits for them, and re-layouts  26.8 us
    all_gather x1, waiting for transfers between devices, shards(): normed = lax.all_gather(normed_rows, 'tensor', axis=0, tiled=True)  24.1 us
  transfers between devices with their start and end apart: 91, of which 43 were waited for; matrix products, arithmetic and copies ran while one was open for 28% of the time, Pallas kernels for 4%

profile of v1, /device:TPU:0, one launch (start us, length us, event | category | flops | bytes accessed | tf_op | source)
XLA Modules:
  0.0 843.3 jit_solution(8713718514374306004)
XLA Ops:
  24.9 11.8 %collective-permute-done.1 = bf16[64,2048]{1,0:T(8,128)(2,1)S(1)} collective-permute-done((bf16[64,2048]{1,0:T(8,128)(2,1)S(1)}, bf16[64,2048]{1,0:T(8,128)(2,1)S(1)}, u32[]{:S(2)}, u32[]{:S(2)}) %collective-permute-start.1) | collective-permute-done | bytes 262176 | tf_op jit(solution)/shard_map/ppermute | solution.py:241
  36.7 8.3 collective-permute-start.3
  46.4 11.3 %collective-permute-done.3 = bf16[64,2048]{1,0:T(8,128)(2,1)S(1)} collective-permute-done((bf16[64,2048]{1,0:T(8,128)(2,1)S(1)}, bf16[64,2048]{1,0:T(8,128)(2,1)S(1)}, u32[]{:S(2)}, u32[]{:S(2)}) %collective-permute-start.3) | collective-permute-done | bytes 262176 | tf_op jit(solution)/shard_map/ppermute | solution.py:241
  57.7 8.2 collective-permute-start.5
  67.3 12.3 %collective-permute-done.5 = bf16[64,2048]{1,0:T(8,128)(2,1)S(1)} collective-permute-done((bf16[64,2048]{1,0:T(8,128)(2,1)S(1)}, bf16[64,2048]{1,0:T(8,128)(2,1)S(1)}, u32[]{:S(2)}, u32[]{:S(2)}) %collective-permute-start.5) | collective-permute-done | bytes 262176 | tf_op jit(solution)/shard_map/ppermute | solution.py:241
  81.9 4.7 copy.47
  86.8 24.1 %all-gather.4.cloned.1.call-done = bf16[2048,2048]{1,0:T(8,128)(2,1)} async-done(((bf16[256,2048]{1,0:T(8,128)(2,1)}), bf16[2048,2048]{1,0:T(8,128)(2,1)}) %all-gather.4.cloned.1.call-update) | async-done | bytes 8388624 | tf_op jit(solution)/shard_map/all_gather | solution.py:365
  110.9 10.1 %add_convert_fusion.q_ref.k_ref.v_ref = bf16[2048,768]{1,0:T(8,128)(2,1)S(1)} fusion(f32[768]{0:T(1024)S(1)} %pad_maximum_fusion.10, bf16[2048,2048]{1,0:T(8,128)(2,1)} %all-gather.4.cloned.1.call-done, bf16[2048,768]{0,1:T(8,128)(2,1)} %bitcast.103), kind=kOutput, calls=%fused_computation.5 | convolution fusion | flops 6445596672 | bytes 14683136 | tf_op jit(solution)/shard_map/dot_general | solution.py:376
  121.0 15.9 %shard_map.398 = (bf16[2048,256]{1,0:T(8,128)(2,1)S(1)}, f32[2,1,2048]{2,1,0:T(1,128)S(1)}) custom-call(s32[2]{0:T(128)S(1)} %get-tuple-element.76.bounds_ref, bf16[2048,768]{1,0:T(8,128)(2,1)S(1)} %add_convert_fusion.q_ref.k_ref.v_ref, bf16[2048,768]{1,0:T(8,128)(2,1)S(1)} %add_convert_fusion.q_ref.k_ref.v_ref, ...), custom_call_target="tpu_custom_call" | custom-call | flops 4294967296 | bytes 4194304 | tf_op jit(solution)/shard_map/pallas_call | solution.py:73
  138.2 4.8 all-to-all-start
  149.0 43.2 %collective-permute-done.10 = bf16[256,2048]{1,0:T(8,128)(2,1)} collective-permute-done((bf16[256,2048]{1,0:T(8,128)(2,1)S(1)}, bf16[256,2048]{1,0:T(8,128)(2,1)}, u32[]{:S(2)}, u32[]{:S(2)}) %collective-permute-start.10) | collective-permute-done | bytes 1048608 | tf_op jit(solution)/shard_map/ppermute | solution.py:241
  192.2 9.9 %all-gather.6.cloned.1.call-done = bf16[8,4,64,2048]{3,2,1,0:T(8,128)(2,1)} async-done(((bf16[8,1,64,2048]{3,2,1,0:T(8,128)(2,1)}), bf16[8,4,64,2048]{3,2,1,0:T(8,128)(2,1)}) %all-gather.6.cloned.1.call-update) | async-done | bytes 8388624 | tf_op jit(solution)/shard_map/all_gather | solution.py:370
  202.2 6.2 fusion.124
  224.6 17.2 %collective-permute-done.14 = bf16[256,2048]{1,0:T(8,128)(2,1)S(1)} collective-permute-done((bf16[256,2048]{1,0:T(8,128)(2,1)}, bf16[256,2048]{1,0:T(8,128)(2,1)S(1)}, u32[]{:S(2)}, u32[]{:S(2)}) %collective-permute-start.14) | collective-permute-done | bytes 1048608 | tf_op jit(solution)/shard_map/ppermute | solution.py:241
  245.2 19.0 %collective-permute-done.12 = bf16[256,2048]{1,0:T(8,128)(2,1)S(1)} collective-permute-done((bf16[256,2048]{1,0:T(8,128)(2,1)}, bf16[256,2048]{1,0:T(8,128)(2,1)S(1)}, u32[]{:S(2)}, u32[]{:S(2)}) %collective-permute-start.12) | collective-permute-done | bytes 1048608 | tf_op jit(solution)/shard_map/ppermute | solution.py:241
  264.4 21.9 %collective-permute-done.15 = bf16[256,2048]{1,0:T(8,128)(2,1)S(1)} collective-permute-done((bf16[256,2048]{1,0:T(8,128)(2,1)S(1)}, bf16[256,2048]{1,0:T(8,128)(2,1)S(1)}, u32[]{:S(2)}, u32[]{:S(2)}) %collective-permute-start.15) | collective-permute-done | bytes 1048608 | tf_op jit(solution)/shard_map/ppermute | solution.py:241
  289.0 6.3 fusion.51
  300.5 12.5 %collective-permute-done.16 = bf16[256,2048]{1,0:T(8,128)(2,1)S(1)} collective-permute-done((bf16[256,2048]{1,0:T(8,128)(2,1)S(1)}, bf16[256,2048]{1,0:T(8,128)(2,1)S(1)}, u32[]{:S(2)}, u32[]{:S(2)}) %collective-permute-start.16) | collective-permute-done | bytes 1048608 | tf_op jit(solution)/shard_map/ppermute | solution.py:241
  316.8 17.1 %fusion.44 = bf16[512,1024]{1,0:T(8,128)(2,1)S(1)} fusion(f32[512,1024]{1,0:T(8,128)} %fusion.72, bf16[1024,2048]{1,0:T(8,128)(2,1)} %param.43, bf16[256,2048]{1,0:T(8,128)(2,1)S(1)} %collective-permute-done.19, bf16[256,2048]{1,0:T(8,128)(2,1)} %collective-permute-done.11, f32[1024]{0:T(1024)S(1)} %copy-done.42), kind=kOutput, calls=%fused_computation.81 | convolution fusion | flops 2162688000 | bytes 9441280 | tf_op jit(solution)/shard_map/td,fd->tf/dot_general | solution.py:383
  342.8 7.3 multiply_convert_fusion.7
  350.2 4.7 fusion.30
  364.6 11.4 %multiply_convert_fusion.1 = bf16[2048,1024]{1,0:T(8,128)(2,1)S(1)} fusion(bf16[2048,2048]{1,0:T(8,128)(2,1)} %constant_dynamic-update-slice_fusion, f32[]{:T(128)S(6)} %div.53, bf16[512,1024]{1,0:T(8,128)(2,1)S(1)} %fusion.37, bf16[512,1024]{1,0:T(8,128)(2,1)S(1)} %fusion.44, bf16[512,1024]{1,0:T(8,128)(2,1)S(1)} %fusion.51, bf16[512,1024]{1,0:T(8,128)(2,1)S(1)} %fusion.30), kind=kOutput, calls=%fused_computation.1 | convolution fusion | flops 8610906112 | bytes 16777220 | tf_op jit(solution)/shard_map/td,tf->df/dot_general | solution.py:458
  381.0 13.2 %multiply_convert_fusion = bf16[1024,2048]{1,0:T(8,128)(2,1)S(1)} fusion(bf16[2048,2048]{1,0:T(8,128)(2,1)} %copy-done.23, bf16[512,1024]{1,0:T(8,128)(2,1)} %get-tuple-element.25, bf16[512,1024]{1,0:T(8,128)(2,1)} %get-tuple-element.26, bf16[512,1024]{1,0:T(8,128)(2,1)} %get-tuple-element.27, bf16[512,1024]{1,0:T(8,128)(2,1)} %get-tuple-element.24, f32[]{:T(128)S(6)} %div.53), kind=kOutput, calls=%fused_computation | convolution fusion | flops 8610906112 | bytes 16777220 | tf_op jit(solution)/shard_map/tf,td->fd/dot_general | solution.py:451
  398.6 5.3 collective-permute-done.74
  408.9 16.4 %collective-permute-done.82 = bf16[256,2048]{1,0:T(8,128)(2,1)S(1)} collective-permute-done((bf16[256,2048]{1,0:T(8,128)(2,1)S(1)}, bf16[256,2048]{1,0:T(8,128)(2,1)S(1)}, u32[]{:S(2)}, u32[]{:S(2)}) %collective-permute-start.82) | collective-permute-done | bytes 1048608 | tf_op jit(solution)/shard_map/ppermute | solution.py:297
  432.5 7.7 collective-permute-done.75
  444.1 7.4 collective-permute-done.83
  455.5 7.8 collective-permute-done.27
  484.3 23.0 %collective-permute-done.32 = bf16[256,2048]{1,0:T(8,128)(2,1)S(1)} collective-permute-done((bf16[256,2048]{1,0:T(8,128)(2,1)S(1)}, bf16[256,2048]{1,0:T(8,128)(2,1)S(1)}, u32[]{:S(2)}, u32[]{:S(2)}) %collective-permute-start.32) | collective-permute-done | bytes 1048608 | tf_op jit(solution)/shard_map/ppermute | solution.py:241
  510.3 23.3 %collective-permute-done.33 = bf16[256,2048]{1,0:T(8,128)(2,1)S(1)} collective-permute-done((bf16[256,2048]{1,0:T(8,128)(2,1)S(1)}, bf16[256,2048]{1,0:T(8,128)(2,1)S(1)}, u32[]{:S(2)}, u32[]{:S(2)}) %collective-permute-start.33) | collective-permute-done | bytes 1048608 | tf_op jit(solution)/shard_map/ppermute | solution.py:241
  538.1 22.6 %collective-permute-done.34 = bf16[256,2048]{1,0:T(8,128)(2,1)S(1)} collective-permute-done((bf16[256,2048]{1,0:T(8,128)(2,1)S(1)}, bf16[256,2048]{1,0:T(8,128)(2,1)S(1)}, u32[]{:S(2)}, u32[]{:S(2)}) %collective-permute-start.34) | collective-permute-done | bytes 1048608 | tf_op jit(solution)/shard_map/ppermute | solution.py:241
  564.9 6.1 convolution_convert_fusion.12
  578.1 5.3 maximum_convert_fusion.1
  583.4 10.8 %collective-permute-done.66 = f32[4,2048]{1,0:T(4,128)S(1)} collective-permute-done((f32[4,2048]{1,0:T(4,128)S(1)}, f32[4,2048]{1,0:T(4,128)S(1)}, u32[]{:S(2)}, u32[]{:S(2)}) %collective-permute-start.66) | collective-permute-done | bytes 32800 | tf_op jit(solution)/shard_map/ppermute | solution.py:322
  594.3 4.6 collective-permute-start.67
  612.3 21.6 %shard_map.399 = bf16[2048,768]{1,0:T(8,128)(2,1)S(1)} custom-call(s32[2]{0:T(128)S(1)} %copy-done.1, bf16[2048,768]{1,0:T(8,128)(2,1)} %copy-done.2, bf16[2048,768]{1,0:T(8,128)(2,1)} %copy-done.2, bf16[2048,768]{1,0:T(8,128)(2,1)} %copy-done.2, bf16[2048,256]{1,0:T(8,128)(2,1)S(1)} %bitcast.98, bf16[2048,256]{1,0:T(8,128)(2,1)S(1)} %get-tuple-element.22.context_ref, ...), custom_call_target="tpu_custom_call" | custom-call | flops 10737418240 | bytes 8388608 | tf_op jit(solution)/shard_map/pallas_call | solution.py:174
  635.4 9.5 %multiply_convert_fusion.2 = bf16[2048,768]{1,0:T(8,128)(2,1)S(1)} fusion(bf16[2048,2048]{1,0:T(8,128)(2,1)} %all-gather.4.cloned.1.call-done, bf16[2048,768]{1,0:T(8,128)(2,1)S(1)} %shard_map.399, f32[]{:T(128)S(6)} %div.53), kind=kOutput, calls=%fused_computation.4 | convolution fusion | flops 6445596672 | bytes 14680068 | tf_op jit(solution)/shard_map/td,tj->dj/dot_general | solution.py:471
  656.6 6.0 collective-permute-done.51
  665.9 47.0 %collective-permute-done.39 = bf16[256,2048]{1,0:T(8,128)(2,1)S(1)} collective-permute-done((bf16[256,2048]{1,0:T(8,128)(2,1)S(1)}, bf16[256,2048]{1,0:T(8,128)(2,1)S(1)}, u32[]{:S(2)}, u32[]{:S(2)}) %collective-permute-start.39) | collective-permute-done | bytes 1048608 | tf_op jit(solution)/shard_map/ppermute | solution.py:241
  716.4 8.3 collective-permute-done.53
  727.7 11.7 %collective-permute-done.40 = bf16[256,2048]{1,0:T(8,128)(2,1)S(1)} collective-permute-done((bf16[256,2048]{1,0:T(8,128)(2,1)S(1)}, bf16[256,2048]{1,0:T(8,128)(2,1)S(1)}, u32[]{:S(2)}, u32[]{:S(2)}) %collective-permute-start.40) | collective-permute-done | bytes 1048608 | tf_op jit(solution)/shard_map/ppermute | solution.py:241
  743.0 8.8 %collective-permute-done.56 = f32[1536]{0:T(1024)S(1)} collective-permute-done((f32[1536]{0:T(1024)S(1)}, f32[1536]{0:T(1024)S(1)}, u32[]{:S(2)}, u32[]{:S(2)}) %collective-permute-start.56) | collective-permute-done | bytes 6176 | tf_op jit(solution)/shard_map/ppermute | solution.py:322
  756.0 10.3 %collective-permute-done.41 = bf16[256,2048]{1,0:T(8,128)(2,1)} collective-permute-done((bf16[256,2048]{1,0:T(8,128)(2,1)}, bf16[256,2048]{1,0:T(8,128)(2,1)}, u32[]{:S(2)}, u32[]{:S(2)}) %collective-permute-start.41) | collective-permute-done | bytes 1048608 | tf_op jit(solution)/shard_map/ppermute | solution.py:241
  766.3 4.2 fusion.22
  775.0 6.7 copy.50
  781.7 6.6 copy.51
  798.5 4.0 fusion.21
  802.5 5.7 fusion.8
  (428 shorter events, 226.4 us)
Async XLA Ops:
  7.2 103.7 %all-gather.4.cloned.1.call-start = ((), (), s32[]{:S(2)}) async-start(), calls=%async_computation.2 | async-start | bytes 9437184 | tf_op jit(solution)/shard_map/all_gather | solution.py:365
  12.0 190.2 %all-gather.6.cloned.1.call-start = ((), (), s32[]{:S(2)}) async-start(), calls=%async_computation.3 | async-start | bytes 10485760 | tf_op jit(solution)/shard_map/all_gather | solution.py:370
  138.2 63.9 %all-to-all-start = ((bf16[8,256,256]{1,2,0:T(8,128)(2,1)}), bf16[8,256,256]{1,2,0:T(8,128)(2,1)}, u32[]{:S(2)}, u32[]{:S(2)}) async-start(bf16[8,256,256]{1,2,0:T(8,128)(2,1)} %copy.48), calls=%async_computation | async-start | bytes 2097152 | tf_op jit(solution)/shard_map/all_to_all | solution.py:388
  146.4 45.9 %collective-permute-start.10 = (bf16[256,2048]{1,0:T(8,128)(2,1)S(1)}, bf16[256,2048]{1,0:T(8,128)(2,1)}, u32[]{:S(2)}, u32[]{:S(2)}) collective-permute-start(bf16[256,2048]{1,0:T(8,128)(2,1)S(1)} %get-tuple-element.23), channel_id=1, source_target_pairs={{0,2},{1,3},{2,6},{3,7},{6,4},{7,5},{4,0},{5,1},{8,10},{9,11},{10,... | collective-permute-start | bytes 3145736 | tf_op jit(solution)/shard_map/ppermute | solution.py:241
  149.0 68.7 %collective-permute-start.8 = (bf16[256,2048]{1,0:T(8,128)(2,1)S(1)}, bf16[256,2048]{1,0:T(8,128)(2,1)}, u32[]{:S(2)}, u32[]{:S(2)}) collective-permute-start(bf16[256,2048]{1,0:T(8,128)(2,1)S(1)} %get-tuple-element.23), channel_id=1, source_target_pairs={{0,1},{1,0},{2,3},{3,2},{4,5},{5,4},{6,7},{7,6},{8,9},{9,8},{10,11... | collective-permute-start | bytes 3145736 | tf_op jit(solution)/shard_map/ppermute | solution.py:245
  192.2 31.1 %collective-permute-start.22 = (bf16[256,2048]{1,0:T(8,128)(2,1)}, bf16[256,2048]{1,0:T(8,128)(2,1)}, u32[]{:S(2)}, u32[]{:S(2)}) collective-permute-start(bf16[256,2048]{1,0:T(8,128)(2,1)} %collective-permute-done.10), channel_id=1, source_target_pairs={{0,1},{1,0},{2,3},{3,2},{4,5},{5,4},{6,7},{7,6},{8,9},{9,8},{10,11... | collective-permute-start | bytes 3145736 | tf_op jit(solution)/shard_map/ppermute | solution.py:245
  192.2 27.2 %collective-permute-start.11 = (bf16[256,2048]{1,0:T(8,128)(2,1)}, bf16[256,2048]{1,0:T(8,128)(2,1)}, u32[]{:S(2)}, u32[]{:S(2)}) collective-permute-start(bf16[256,2048]{1,0:T(8,128)(2,1)} %collective-permute-done.10), channel_id=1, source_target_pairs={{0,2},{1,3},{2,6},{3,7},{6,4},{7,5},{4,0},{5,1},{8,10},{9,11},{10,... | collective-permute-start | bytes 3145736 | tf_op jit(solution)/shard_map/ppermute | solution.py:241
  210.9 30.9 %collective-permute-start.14 = (bf16[256,2048]{1,0:T(8,128)(2,1)}, bf16[256,2048]{1,0:T(8,128)(2,1)S(1)}, u32[]{:S(2)}, u32[]{:S(2)}) collective-permute-start(bf16[256,2048]{1,0:T(8,128)(2,1)} %get-tuple-element.67), channel_id=1, source_target_pairs={{0,2},{1,3},{2,6},{3,7},{6,4},{7,5},{4,0},{5,1},{8,10},{9,11},{10,... | collective-permute-start | bytes 3145736 | tf_op jit(solution)/shard_map/ppermute | solution.py:241
  217.6 25.5 %collective-permute-start.7 = (bf16[256,2048]{1,0:T(8,128)(2,1)}, bf16[256,2048]{1,0:T(8,128)(2,1)S(1)}, u32[]{:S(2)}, u32[]{:S(2)}) collective-permute-start(bf16[256,2048]{1,0:T(8,128)(2,1)} %get-tuple-element.67), channel_id=1, source_target_pairs={{0,1},{1,0},{2,3},{3,2},{4,5},{5,4},{6,7},{7,6},{8,9},{9,8},{10,11... | collective-permute-start | bytes 3145736 | tf_op jit(solution)/shard_map/ppermute | solution.py:245
  219.4 44.8 %collective-permute-start.19 = (bf16[256,2048]{1,0:T(8,128)(2,1)}, bf16[256,2048]{1,0:T(8,128)(2,1)S(1)}, u32[]{:S(2)}, u32[]{:S(2)}) collective-permute-start(bf16[256,2048]{1,0:T(8,128)(2,1)} %collective-permute-done.11), channel_id=1, source_target_pairs={{0,1},{1,0},{2,3},{3,2},{4,5},{5,4},{6,7},{7,6},{8,9},{9,8},{10,11... | collective-permute-start | bytes 3145736 | tf_op jit(solution)/shard_map/ppermute | solution.py:245
  219.6 44.6 %collective-permute-start.12 = (bf16[256,2048]{1,0:T(8,128)(2,1)}, bf16[256,2048]{1,0:T(8,128)(2,1)S(1)}, u32[]{:S(2)}, u32[]{:S(2)}) collective-permute-start(bf16[256,2048]{1,0:T(8,128)(2,1)} %collective-permute-done.11), channel_id=1, source_target_pairs={{0,2},{1,3},{2,6},{3,7},{6,4},{7,5},{4,0},{5,1},{8,10},{9,11},{10,... | collective-permute-start | bytes 3145736 | tf_op jit(solution)/shard_map/ppermute | solution.py:241
  241.8 44.8 %collective-permute-start.23 = (bf16[256,2048]{1,0:T(8,128)(2,1)S(1)}, bf16[256,2048]{1,0:T(8,128)(2,1)S(1)}, u32[]{:S(2)}, u32[]{:S(2)}) collective-permute-start(bf16[256,2048]{1,0:T(8,128)(2,1)S(1)} %collective-permute-done.14), channel_id=1, source_target_pairs={{0,1},{1,0},{2,3},{3,2},{4,5},{5,4},{6,7},{7,6},{8,9},{9,8},{10,11... | collective-permute-start | bytes 3145736 | tf_op jit(solution)/shard_map/ppermute | solution.py:245
  241.8 44.6 %collective-permute-start.15 = (bf16[256,2048]{1,0:T(8,128)(2,1)S(1)}, bf16[256,2048]{1,0:T(8,128)(2,1)S(1)}, u32[]{:S(2)}, u32[]{:S(2)}) collective-permute-start(bf16[256,2048]{1,0:T(8,128)(2,1)S(1)} %collective-permute-done.14), channel_id=1, source_target_pairs={{0,2},{1,3},{2,6},{3,7},{6,4},{7,5},{4,0},{5,1},{8,10},{9,11},{10,... | collective-permute-start | bytes 3145736 | tf_op jit(solution)/shard_map/ppermute | solution.py:241
  264.2 36.2 %collective-permute-start.13 = (bf16[256,2048]{1,0:T(8,128)(2,1)S(1)}, bf16[256,2048]{1,0:T(8,128)(2,1)S(1)}, u32[]{:S(2)}, u32[]{:S(2)}) collective-permute-start(bf16[256,2048]{1,0:T(8,128)(2,1)S(1)} %collective-permute-done.12), channel_id=1, source_target_pairs={{0,1},{1,0},{2,3},{3,2},{4,5},{5,4},{6,7},{7,6},{8,9},{9,8},{10,11... | collective-permute-start | bytes 3145736 | tf_op jit(solution)/shard_map/ppermute | solution.py:245
  286.3 26.7 %collective-permute-start.20 = (bf16[256,2048]{1,0:T(8,128)(2,1)S(1)}, bf16[256,2048]{1,0:T(8,128)(2,1)S(1)}, u32[]{:S(2)}, u32[]{:S(2)}) collective-permute-start(bf16[256,2048]{1,0:T(8,128)(2,1)S(1)} %collective-permute-done.15), channel_id=1, source_target_pairs={{0,1},{1,0},{2,3},{3,2},{4,5},{5,4},{6,7},{7,6},{8,9},{9,8},{10,11... | collective-permute-start | bytes 3145736 | tf_op jit(solution)/shard_map/ppermute | solution.py:245
  286.3 26.7 %collective-permute-start.16 = (bf16[256,2048]{1,0:T(8,128)(2,1)S(1)}, bf16[256,2048]{1,0:T(8,128)(2,1)S(1)}, u32[]{:S(2)}, u32[]{:S(2)}) collective-permute-start(bf16[256,2048]{1,0:T(8,128)(2,1)S(1)} %collective-permute-done.15), channel_id=1, source_target_pairs={{0,2},{1,3},{2,6},{3,7},{6,4},{7,5},{4,0},{5,1},{8,10},{9,11},{10,... | collective-permute-start | bytes 3145736 | tf_op jit(solution)/shard_map/ppermute | solution.py:241
  297.8 39.6 %collective-permute-start.24 = (bf16[256,2048]{1,0:T(8,128)(2,1)S(1)}, bf16[256,2048]{1,0:T(8,128)(2,1)S(1)}, u32[]{:S(2)}, u32[]{:S(2)}) collective-permute-start(bf16[256,2048]{1,0:T(8,128)(2,1)S(1)} %slice.171), channel_id=1, source_target_pairs={{0,1},{1,0},{2,3},{3,2},{4,5},{5,4},{6,7},{7,6},{8,9},{9,8},{10,11... | collective-permute-start | bytes 3145736 | tf_op jit(solution)/shard_map/ppermute | solution.py:245
  313.0 27.4 %collective-permute-start.17 = (bf16[256,2048]{1,0:T(8,128)(2,1)S(1)}, bf16[256,2048]{1,0:T(8,128)(2,1)S(1)}, u32[]{:S(2)}, u32[]{:S(2)}) collective-permute-start(bf16[256,2048]{1,0:T(8,128)(2,1)S(1)} %collective-permute-done.16), channel_id=1, source_target_pairs={{0,1},{1,0},{2,3},{3,2},{4,5},{5,4},{6,7},{7,6},{8,9},{9,8},{10,11... | collective-permute-start | bytes 3145736 | tf_op jit(solution)/shard_map/ppermute | solution.py:245
  337.7 57.6 %collective-permute-start.25 = (bf16[256,2048]{1,0:T(8,128)(2,1)S(1)}, bf16[256,2048]{1,0:T(8,128)(2,1)}, u32[]{:S(2)}, u32[]{:S(2)}) collective-permute-start(bf16[256,2048]{1,0:T(8,128)(2,1)S(1)} %add_convert_fusion.13), channel_id=1, source_target_pairs={{0,2},{1,3},{2,6},{3,7},{6,4},{7,5},{4,0},{5,1},{8,10},{9,11},{10,... | collective-permute-start | bytes 3145736 | tf_op jit(solution)/shard_map/ppermute | solution.py:241
  337.8 58.0 %collective-permute-start.21 = (bf16[256,2048]{1,0:T(8,128)(2,1)}, bf16[256,2048]{1,0:T(8,128)(2,1)}, u32[]{:S(2)}, u32[]{:S(2)}) collective-permute-start(bf16[256,2048]{1,0:T(8,128)(2,1)} %slice.169), channel_id=1, source_target_pairs={{0,1},{1,0},{2,3},{3,2},{4,5},{5,4},{6,7},{7,6},{8,9},{9,8},{10,11... | collective-permute-start | bytes 3145736 | tf_op jit(solution)/shard_map/ppermute | solution.py:245
  377.7 26.2 %collective-permute-start.74 = (bf16[512,1024]{1,0:T(8,128)(2,1)S(1)}, bf16[512,1024]{1,0:T(8,128)(2,1)}, u32[]{:S(2)}, u32[]{:S(2)}) collective-permute-start(bf16[512,1024]{1,0:T(8,128)(2,1)S(1)} %constant_dynamic-slice_fusion.15), channel_id=1, source_target_pairs={{0,16},{8,24},{16,0},{24,8},{1,17},{9,25},{17,1},{25,9},{2,18},{10... | collective-permute-start | bytes 3145736 | tf_op jit(solution)/shard_map/ppermute | solution.py:297
  379.5 27.6 %collective-permute-start.70 = (bf16[512,1024]{1,0:T(8,128)(2,1)S(1)}, bf16[512,1024]{1,0:T(8,128)(2,1)}, u32[]{:S(2)}, u32[]{:S(2)}) collective-permute-start(bf16[512,1024]{1,0:T(8,128)(2,1)S(1)} %constant_dynamic-slice_fusion.3), channel_id=1, source_target_pairs={{0,8},{8,0},{16,24},{24,16},{1,9},{9,1},{17,25},{25,17},{2,10},{10... | collective-permute-start | bytes 3145736 | tf_op jit(solution)/shard_map/ppermute | solution.py:297
  394.7 30.6 %collective-permute-start.82 = (bf16[256,2048]{1,0:T(8,128)(2,1)S(1)}, bf16[256,2048]{1,0:T(8,128)(2,1)S(1)}, u32[]{:S(2)}, u32[]{:S(2)}) collective-permute-start(bf16[256,2048]{1,0:T(8,128)(2,1)S(1)} %constant_dynamic-slice_fusion.21), channel_id=1, source_target_pairs={{0,16},{8,24},{16,0},{24,8},{1,17},{9,25},{17,1},{25,9},{2,18},{10... | collective-permute-start | bytes 3145736 | tf_op jit(solution)/shard_map/ppermute | solution.py:297
  395.3 32.1 %collective-permute-start.78 = (bf16[256,2048]{1,0:T(8,128)(2,1)S(1)}, bf16[256,2048]{1,0:T(8,128)(2,1)S(1)}, u32[]{:S(2)}, u32[]{:S(2)}) collective-permute-start(bf16[256,2048]{1,0:T(8,128)(2,1)S(1)} %constant_dynamic-slice_fusion.18), channel_id=1, source_target_pairs={{0,8},{8,0},{16,24},{24,16},{1,9},{9,1},{17,25},{25,17},{2,10},{10... | collective-permute-start | bytes 3145736 | tf_op jit(solution)/shard_map/ppermute | solution.py:297
  395.8 59.1 %collective-permute-start.9 = (bf16[256,2048]{1,0:T(8,128)(2,1)S(1)}, bf16[256,2048]{1,0:T(8,128)(2,1)S(1)}, u32[]{:S(2)}, u32[]{:S(2)}) collective-permute-start(bf16[256,2048]{1,0:T(8,128)(2,1)S(1)} %slice.165), channel_id=1, source_target_pairs={{0,1},{1,0},{2,3},{3,2},{4,5},{5,4},{6,7},{7,6},{8,9},{9,8},{10,11... | collective-permute-start | bytes 3145736 | tf_op jit(solution)/shard_map/ppermute | solution.py:245
  403.9 25.6 %collective-permute-start.26 = (bf16[256,2048]{1,0:T(8,128)(2,1)S(1)}, bf16[256,2048]{1,0:T(8,128)(2,1)S(1)}, u32[]{:S(2)}, u32[]{:S(2)}) collective-permute-start(bf16[256,2048]{1,0:T(8,128)(2,1)S(1)} %add_convert_fusion.12), channel_id=1, source_target_pairs={{0,2},{1,3},{2,6},{3,7},{6,4},{7,5},{4,0},{5,1},{8,10},{9,11},{10,... | collective-permute-start | bytes 3145736 | tf_op jit(solution)/shard_map/ppermute | solution.py:241
  453.2 27.3 %collective-permute-start.84 = (bf16[128,2048]{1,0:T(8,128)(2,1)S(1)}, bf16[128,2048]{1,0:T(8,128)(2,1)S(1)}, u32[]{:S(2)}, u32[]{:S(2)}) collective-permute-start(bf16[128,2048]{1,0:T(8,128)(2,1)S(1)} %add_convert_fusion.17), channel_id=1, source_target_pairs={{0,8},{8,0},{16,24},{24,16},{1,9},{9,1},{17,25},{25,17},{2,10},{10... | collective-permute-start | bytes 1572872 | tf_op jit(solution)/shard_map/ppermute | solution.py:297
  454.9 53.1 %collective-permute-start.80 = (bf16[128,2048]{1,0:T(8,128)(2,1)S(1)}, bf16[128,2048]{1,0:T(8,128)(2,1)S(1)}, u32[]{:S(2)}, u32[]{:S(2)}) collective-permute-start(bf16[128,2048]{1,0:T(8,128)(2,1)S(1)} %add_convert_fusion.18), channel_id=1, source_target_pairs={{0,16},{8,24},{16,0},{24,8},{1,17},{9,25},{17,1},{25,9},{2,18},{10... | collective-permute-start | bytes 1572872 | tf_op jit(solution)/shard_map/ppermute | solution.py:297
  465.8 133.0 %collective-permute-start.77 = (bf16[512,1024]{1,0:T(8,128)(2,1)}, bf16[512,1024]{1,0:T(8,128)(2,1)}, u32[]{:S(2)}, u32[]{:S(2)}) collective-permute-start(bf16[512,1024]{1,0:T(8,128)(2,1)} %pad_maximum_fusion.2), channel_id=1, source_target_pairs={{0,16},{8,24},{16,0},{24,8},{1,17},{9,25},{17,1},{25,9},{2,18},{10... | collective-permute-start | bytes 3145736 | tf_op jit(solution)/shard_map/ppermute | solution.py:297
  468.9 135.3 %collective-permute-start.73 = (bf16[512,1024]{1,0:T(8,128)(2,1)}, bf16[512,1024]{1,0:T(8,128)(2,1)}, u32[]{:S(2)}, u32[]{:S(2)}) collective-permute-start(bf16[512,1024]{1,0:T(8,128)(2,1)} %pad_maximum_fusion.1), channel_id=1, source_target_pairs={{0,8},{8,0},{16,24},{24,16},{1,9},{9,1},{17,25},{25,17},{2,10},{10... | collective-permute-start | bytes 3145736 | tf_op jit(solution)/shard_map/ppermute | solution.py:297
  480.6 26.7 %collective-permute-start.32 = (bf16[256,2048]{1,0:T(8,128)(2,1)S(1)}, bf16[256,2048]{1,0:T(8,128)(2,1)S(1)}, u32[]{:S(2)}, u32[]{:S(2)}) collective-permute-start(bf16[256,2048]{1,0:T(8,128)(2,1)S(1)} %add_convert_fusion.10), channel_id=1, source_target_pairs={{0,2},{1,3},{2,6},{3,7},{6,4},{7,5},{4,0},{5,1},{8,10},{9,11},{10,... | collective-permute-start | bytes 3145736 | tf_op jit(solution)/shard_map/ppermute | solution.py:241
  484.0 25.7 %collective-permute-start.29 = (bf16[256,2048]{1,0:T(8,128)(2,1)S(1)}, bf16[256,2048]{1,0:T(8,128)(2,1)S(1)}, u32[]{:S(2)}, u32[]{:S(2)}) collective-permute-start(bf16[256,2048]{1,0:T(8,128)(2,1)S(1)} %slice.175), channel_id=1, source_target_pairs={{0,1},{1,0},{2,3},{3,2},{4,5},{5,4},{6,7},{7,6},{8,9},{9,8},{10,11... | collective-permute-start | bytes 3145736 | tf_op jit(solution)/shard_map/ppermute | solution.py:245
  507.9 25.7 %collective-permute-start.33 = (bf16[256,2048]{1,0:T(8,128)(2,1)S(1)}, bf16[256,2048]{1,0:T(8,128)(2,1)S(1)}, u32[]{:S(2)}, u32[]{:S(2)}) collective-permute-start(bf16[256,2048]{1,0:T(8,128)(2,1)S(1)} %add_convert_fusion.9), channel_id=1, source_target_pairs={{0,2},{1,3},{2,6},{3,7},{6,4},{7,5},{4,0},{5,1},{8,10},{9,11},{10,... | collective-permute-start | bytes 3145736 | tf_op jit(solution)/shard_map/ppermute | solution.py:241
  508.0 26.1 %collective-permute-start.85 = (bf16[256,2048]{1,0:T(8,128)(2,1)S(1)}, bf16[256,2048]{1,0:T(8,128)(2,1)S(1)}, u32[]{:S(2)}, u32[]{:S(2)}) collective-permute-start(bf16[256,2048]{1,0:T(8,128)(2,1)S(1)} %pad_maximum_fusion.4), channel_id=1, source_target_pairs={{0,16},{8,24},{16,0},{24,8},{1,17},{9,25},{17,1},{25,9},{2,18},{10... | collective-permute-start | bytes 3145736 | tf_op jit(solution)/shard_map/ppermute | solution.py:297
  509.7 26.6 %collective-permute-start.81 = (bf16[256,2048]{1,0:T(8,128)(2,1)S(1)}, bf16[256,2048]{1,0:T(8,128)(2,1)S(1)}, u32[]{:S(2)}, u32[]{:S(2)}) collective-permute-start(bf16[256,2048]{1,0:T(8,128)(2,1)S(1)} %pad_maximum_fusion.3), channel_id=1, source_target_pairs={{0,8},{8,0},{16,24},{24,16},{1,9},{9,1},{17,25},{25,17},{2,10},{10... | collective-permute-start | bytes 3145736 | tf_op jit(solution)/shard_map/ppermute | solution.py:297
  534.2 26.5 %collective-permute-start.34 = (bf16[256,2048]{1,0:T(8,128)(2,1)S(1)}, bf16[256,2048]{1,0:T(8,128)(2,1)S(1)}, u32[]{:S(2)}, u32[]{:S(2)}) collective-permute-start(bf16[256,2048]{1,0:T(8,128)(2,1)S(1)} %add_convert_fusion.8), channel_id=1, source_target_pairs={{0,2},{1,3},{2,6},{3,7},{6,4},{7,5},{4,0},{5,1},{8,10},{9,11},{10,... | collective-permute-start | bytes 3145736 | tf_op jit(solution)/shard_map/ppermute | solution.py:241
  572.0 40.2 %all-to-all-start.1 = ((bf16[256,8,256]{2,0,1:T(8,128)(2,1)}), bf16[256,8,256]{2,0,1:T(8,128)(2,1)S(1)}, u32[]{:S(2)}, u32[]{:S(2)}) async-start(bf16[256,8,256]{2,0,1:T(8,128)(2,1)} %bitcast.102), calls=%async_computation.1 | async-start | bytes 2097152 | tf_op jit(solution)/shard_map/all_to_all | solution.py:417
  575.6 226.9 %all-gather.8.cloned.1.call-start = ((), (), s32[]{:S(2)}) async-start(), calls=%async_computation.4 | async-start | bytes 9437184 | tf_op jit(solution)/shard_map/all_gather | solution.py:461
  634.4 106.5 %collective-permute-start.55 = (f32[1536]{0:T(1024)S(1)}, f32[1536]{0:T(1024)S(1)}, u32[]{:S(2)}, u32[]{:S(2)}) collective-permute-start(f32[1536]{0:T(1024)S(1)} %maximum_multiply_fusion.2), channel_id=1, source_target_pairs={{0,8},{8,0},{16,24},{24,16},{1,9},{9,1},{17,25},{25,17},{2,10},{10... | collective-permute-start | bytes 18440 | tf_op jit(solution)/shard_map/ppermute | solution.py:322
  654.6 58.3 %collective-permute-start.39 = (bf16[256,2048]{1,0:T(8,128)(2,1)S(1)}, bf16[256,2048]{1,0:T(8,128)(2,1)S(1)}, u32[]{:S(2)}, u32[]{:S(2)}) collective-permute-start(bf16[256,2048]{1,0:T(8,128)(2,1)S(1)} %add_convert_fusion.7), channel_id=1, source_target_pairs={{0,2},{1,3},{2,6},{3,7},{6,4},{7,5},{4,0},{5,1},{8,10},{9,11},{10,... | collective-permute-start | bytes 3145736 | tf_op jit(solution)/shard_map/ppermute | solution.py:241
  662.6 64.5 %collective-permute-start.36 = (bf16[256,2048]{1,0:T(8,128)(2,1)S(1)}, bf16[256,2048]{1,0:T(8,128)(2,1)S(1)}, u32[]{:S(2)}, u32[]{:S(2)}) collective-permute-start(bf16[256,2048]{1,0:T(8,128)(2,1)S(1)} %constant_dynamic-slice_fusion.19), channel_id=1, source_target_pairs={{0,1},{1,0},{2,3},{3,2},{4,5},{5,4},{6,7},{7,6},{8,9},{9,8},{10,11... | collective-permute-start | bytes 3145736 | tf_op jit(solution)/shard_map/ppermute | solution.py:245
  663.6 49.9 %collective-permute-start.52 = (bf16[256,768]{1,0:T(8,128)(2,1)S(1)}, bf16[256,768]{1,0:T(8,128)(2,1)S(1)}, u32[]{:S(2)}, u32[]{:S(2)}) collective-permute-start(bf16[256,768]{1,0:T(8,128)(2,1)S(1)} %constant_dynamic-slice_fusion.9), channel_id=1, source_target_pairs={{0,8},{8,0},{16,24},{24,16},{1,9},{9,1},{17,25},{25,17},{2,10},{10... | collective-permute-start | bytes 1179656 | tf_op jit(solution)/shard_map/ppermute | solution.py:297
  665.1 51.2 %collective-permute-start.48 = (bf16[256,768]{1,0:T(8,128)(2,1)S(1)}, bf16[256,768]{1,0:T(8,128)(2,1)S(1)}, u32[]{:S(2)}, u32[]{:S(2)}) collective-permute-start(bf16[256,768]{1,0:T(8,128)(2,1)S(1)} %constant_dynamic-slice_fusion.11), channel_id=1, source_target_pairs={{0,16},{8,24},{16,0},{24,8},{1,17},{9,25},{17,1},{25,9},{2,18},{10... | collective-permute-start | bytes 1179656 | tf_op jit(solution)/shard_map/ppermute | solution.py:297
  713.4 26.0 %collective-permute-start.40 = (bf16[256,2048]{1,0:T(8,128)(2,1)S(1)}, bf16[256,2048]{1,0:T(8,128)(2,1)S(1)}, u32[]{:S(2)}, u32[]{:S(2)}) collective-permute-start(bf16[256,2048]{1,0:T(8,128)(2,1)S(1)} %add_convert_fusion.6), channel_id=1, source_target_pairs={{0,2},{1,3},{2,6},{3,7},{6,4},{7,5},{4,0},{5,1},{8,10},{9,11},{10,... | collective-permute-start | bytes 3145736 | tf_op jit(solution)/shard_map/ppermute | solution.py:241
  716.2 39.8 %collective-permute-start.35 = (bf16[256,2048]{1,0:T(8,128)(2,1)}, bf16[256,2048]{1,0:T(8,128)(2,1)}, u32[]{:S(2)}, u32[]{:S(2)}) collective-permute-start(bf16[256,2048]{1,0:T(8,128)(2,1)} %constant_dynamic-slice_fusion.22), channel_id=1, source_target_pairs={{0,1},{1,0},{2,3},{3,2},{4,5},{5,4},{6,7},{7,6},{8,9},{9,8},{10,11... | collective-permute-start | bytes 3145736 | tf_op jit(solution)/shard_map/ppermute | solution.py:245
  724.7 28.4 %collective-permute-start.49 = (bf16[256,768]{1,0:T(8,128)(2,1)S(1)}, bf16[256,768]{1,0:T(8,128)(2,1)S(1)}, u32[]{:S(2)}, u32[]{:S(2)}) collective-permute-start(bf16[256,768]{1,0:T(8,128)(2,1)S(1)} %add_convert_fusion.22), channel_id=1, source_target_pairs={{0,16},{8,24},{16,0},{24,8},{1,17},{9,25},{17,1},{25,9},{2,18},{10... | collective-permute-start | bytes 1179656 | tf_op jit(solution)/shard_map/ppermute | solution.py:297
  727.1 27.5 %collective-permute-start.54 = (bf16[512,768]{1,0:T(8,128)(2,1)}, bf16[512,768]{1,0:T(8,128)(2,1)}, u32[]{:S(2)}, u32[]{:S(2)}) collective-permute-start(bf16[512,768]{1,0:T(8,128)(2,1)} %pad_maximum_fusion.6), channel_id=1, source_target_pairs={{0,16},{8,24},{16,0},{24,8},{1,17},{9,25},{17,1},{25,9},{2,18},{10... | collective-permute-start | bytes 2359304 | tf_op jit(solution)/shard_map/ppermute | solution.py:297
  740.9 25.4 %collective-permute-start.41 = (bf16[256,2048]{1,0:T(8,128)(2,1)}, bf16[256,2048]{1,0:T(8,128)(2,1)}, u32[]{:S(2)}, u32[]{:S(2)}) collective-permute-start(bf16[256,2048]{1,0:T(8,128)(2,1)} %add_convert_fusion.5), channel_id=1, source_target_pairs={{0,2},{1,3},{2,6},{3,7},{6,4},{7,5},{4,0},{5,1},{8,10},{9,11},{10,... | collective-permute-start | bytes 3145736 | tf_op jit(solution)/shard_map/ppermute | solution.py:241
  (91 other events, 1088.8 us)
Sparse Core Ops, SparseCore 0:
  12.1 98.7 all-gather.3
  113.3 88.7 all-gather.5
  612.4 97.9 all-gather.7

commit v2 on v1

--- a/solution.py
+++ b/solution.py
@@ -263,17 +263,20 @@
     return pairs
 
 
-def ring_scatter(part):
-    arrived = None
+def ring_scatter(part, ties=()):
+    arrivals = []
     chips = lax.axis_size("tensor") // 2
     for step in list(range(1, chips)) + [0]:
         mine, other = part(step)
         total = mine.astype(jnp.float32) + swap_cores(other).astype(jnp.float32)
-        if arrived is not None:
-            total = total + arrived.astype(jnp.float32)
+        if arrivals:
+            total = total + arrivals[-1].astype(jnp.float32)
         if step:
             arrived = ring_step(total.astype(jnp.bfloat16))
-    return total
+            if len(arrivals) < len(ties):
+                arrived = after(arrived, *ties[len(arrivals)])
+            arrivals.append(arrived)
+    return total, arrivals
 
 
 def in_order(pairs):
@@ -288,30 +291,64 @@
     return full
 
 
-def dp_sum(value):
+def flip_dp(value, bit):
     size = lax.axis_size("dp")
+    return lax.ppermute(value, "dp", [(i, i ^ bit) for i in range(size)])
+
+
+def dp_bits():
+    return [1 << i for i in range((lax.axis_size("dp") - 1).bit_length())]
+
+
+def tied(ties):
+    left = list(ties)
+
+    def tie(value):
+        return after(value, *left.pop(0)) if left else value
+
+    return tie
+
+
+def dp_halves(value, bits, axis, ties):
+    tie = tied(ties)
     me = lax.axis_index("dp")
-    bits = [1 << i for i in range((size - 1).bit_length())]
-
-    def flip(x, bit):
-        return lax.ppermute(x, "dp", [(i, i ^ bit) for i in range(size)])
-
-    def one(x, bits):
-        for bit in bits:
-            half = x.shape[0] // 2
-            up = (me & bit) != 0
-            keep = lax.dynamic_slice_in_dim(x, jnp.where(up, half, 0), half)
-            give = lax.dynamic_slice_in_dim(x, jnp.where(up, 0, half), half)
-            got = flip(give, bit)
-            x = (keep.astype(jnp.float32) + got.astype(jnp.float32)).astype(x.dtype)
-        for bit in reversed(bits):
-            up = (me & bit) != 0
-            got = flip(x, bit)
-            x = jnp.concatenate([jnp.where(up, got, x), jnp.where(up, x, got)], axis=0)
-        return x
-
-    half = value.shape[0] // 2
-    return jnp.concatenate([one(value[:half], bits), one(value[half:], bits[::-1])], axis=0)
+    stages = [value]
+    for bit in bits:
+        half = value.shape[axis] // 2
+        up = (me & bit) != 0
+        keep = lax.dynamic_slice_in_dim(value, jnp.where(up, half, 0), half, axis)
+        give = lax.dynamic_slice_in_dim(value, jnp.where(up, 0, half), half, axis)
+        got = tie(flip_dp(give, bit))
+        value = (keep.astype(jnp.float32) + got.astype(jnp.float32)).astype(value.dtype)
+        stages.append(value)
+    return stages
+
+
+def dp_blocks(value, bits, ties):
+    tie = tied(ties)
+    blocks = [(0, value)]
+    first = None
+    for bit in bits:
+        got = tie(flip_dp(jnp.concatenate([block for _, block in blocks], axis=0), bit))
+        first = got if first is None else first
+        blocks += [
+            (mask ^ bit, piece) for (mask, _), piece in zip(blocks, jnp.split(got, len(blocks)))
+        ]
+    return blocks, first
+
+
+def cut_place(mask, bits, size):
+    device = lax.axis_index("dp") ^ mask
+    place = 0
+    for bit in bits:
+        size //= 2
+        place = place + jnp.where((device & bit) != 0, size, 0)
+    return place
+
+
+def put(full, block, rows, column=0):
+    block = block.astype(full.dtype).reshape(block.shape[:1] + full.shape[1:2] + (-1,)) if full.ndim == 3 else block.astype(full.dtype)
+    return lax.dynamic_update_slice(full, block, (rows, column) + (0,) * (full.ndim - 2))
 
 
 def small_sum(value, axes):
@@ -359,119 +396,241 @@
     local_rows = rank * shard_rows + jnp.arange(shard_rows, dtype=jnp.int32)
     local_live = (local_rows < own_count).astype(f32)[:, None]
 
+    def dot(a, b, a_axis, b_axis):
+        return lax.dot_general(
+            a, b, (((a_axis,), (b_axis,)), ((), ())), preferred_element_type=jnp.float32
+        )
+
+    def chip_rows(rows, step):
+        first = ring_chip(step) * 2 * shard_rows
+        return jnp.concatenate(
+            [
+                lax.dynamic_slice_in_dim(rows, first + core * shard_rows, shard_rows),
+                lax.dynamic_slice_in_dim(rows, first + (1 - core) * shard_rows, shard_rows),
+            ],
+            axis=0,
+        )
+
+    def ordered(blocks):
+        return in_order([(b[:shard_rows], b[shard_rows:]) for b in blocks]).reshape(
+            group_rows, blocks[0].shape[1]
+        )
+
     input_rows = tokens.astype(f32)
     unit_one, inverse_one = normalize(input_rows)
     normed_rows = (unit_one * attention_gain + attention_shift).astype(bf16)
     normed = lax.all_gather(normed_rows, "tensor", axis=0, tiled=True)
 
-    piece = output_weight.shape[0] // group_count
-    own_piece = lax.dynamic_slice_in_dim(output_weight, group * piece, piece)
-    pieces = in_order(ring_gather(own_piece))
-    output_full = lax.all_gather(pieces, "dp", axis=1, tiled=False).reshape(features, features)
+    columns = features // group_count
+    moving = lax.dynamic_slice_in_dim(output_weight, group * columns, columns, 1)
+    pieces = [moving]
+    for _ in range(1, chips):
+        with jax.named_scope("weight_ring"):
+            moving = ring_step(moving)
+        pieces.append(moving)
+    bits = dp_bits()
+    pieces = jnp.concatenate(pieces, axis=0)
+    half = pieces.shape[0] // 2
+
+    weight_own = jnp.zeros((2 * half, features), bf16)
+    with jax.named_scope("weight_dp"):
+        for start, order in ((0, bits), (half, bits[::-1])):
+            for mask, block in dp_blocks(pieces[start : start + half], order, [])[0]:
+                weight_own = put(weight_own, block, start, (group ^ mask) * columns)
+    weight_other = swap_cores(weight_own)
 
     weight_flat = query_key_value.reshape(features, 3 * local_width)
     bias_flat = jnp.concatenate(
         [query_value_bias[0], jnp.zeros_like(query_value_bias[0]), query_value_bias[1]]
     )
-    projected = (jnp.dot(normed, weight_flat, preferred_element_type=f32) + bias_flat).astype(bf16)
-
+    normed, weight_own, weight_other, weight_flat = lax.optimization_barrier(
+        (normed, weight_own, weight_other, weight_flat)
+    )
     grad_rows_low = jnp.where(local_live > 0, cotangent, jnp.zeros_like(cotangent))
-    grad_out = [
-        jnp.concatenate(pair, axis=0) for pair in ring_gather(after(grad_rows_low, normed))
-    ]
-    grad_activated = [
-        jnp.einsum("td,fd->tf", block, contract_weight, preferred_element_type=f32)
-        for block in grad_out
-    ]
-
+    grad_out = lax.all_gather(after(grad_rows_low, normed), "tensor", axis=0, tiled=True)
+
+    projected = (dot(normed, weight_flat, 1, 0) + bias_flat).astype(bf16)
     context, totals = attend(own_bounds, projected, local_heads)
-    context_rows = lax.all_to_all(context, "tensor", split_axis=0, concat_axis=1, tiled=True)
+
+    arrived = lax.all_to_all(
+        context.reshape(tensor_size, shard_rows, local_width), "tensor", 0, 0, tiled=True
+    )
+
+    def heads_of(parity):
+        return jnp.concatenate(
+            [
+                lax.dynamic_index_in_dim(arrived, 2 * ring_chip(step) + parity, 0, False)
+                for step in range(chips)
+            ],
+            axis=1,
+        )
+
+    context_own, context_other = heads_of(core), heads_of(1 - core)
     hidden = (
-        input_rows + jnp.dot(context_rows, output_full, preferred_element_type=f32) + output_bias
+        input_rows
+        + dot(context_own, weight_own, 1, 0)
+        + dot(context_other, weight_other, 1, 0)
+        + output_bias
     )
     unit_two, inverse_two = normalize(hidden)
     mixed_rows = (unit_two * feedforward_gain + feedforward_shift).astype(bf16)
 
-    mixed = [jnp.concatenate(pair, axis=0) for pair in ring_gather(mixed_rows)]
-    activated, grad_pre = [None] * chips, [None] * chips
+    mixed, activated, grad_pre, mixed_terms, mixed_arrivals = [], [], [], [], []
+    moving = after(mixed_rows, grad_out)
+
+    def mixed_step(step):
+        mixed.append(jnp.concatenate([moving, swap_cores(moving)], axis=0))
+        rows = mixed[step]
+        if step > 2:
+            rows = after(rows, mixed_arrivals[step - 3])
+        grad_activated = dot(chip_rows(grad_out, step), contract_weight, 1, 1)
+        pre_act = dot(rows, expand_weight, 1, 0) + expand_bias
+        value, gelu_pull = jax.vjp(gelu_tanh, pre_act)
+        activated.append(value.astype(bf16))
+        grad_pre.append(gelu_pull(grad_activated)[0].astype(bf16))
+        mixed_terms.append(dot(grad_pre[step], expand_weight, 1, 1).astype(bf16))
+
+    def chip_total(terms, arrivals):
+        total = terms[:shard_rows].astype(f32) + swap_cores(terms[shard_rows:]).astype(f32)
+        return total + arrivals[-1].astype(f32) if arrivals else total
+
     for step in range(chips):
-        pre_act = jnp.dot(mixed[step], expand_weight, preferred_element_type=f32) + expand_bias
-        value, gelu_pull = jax.vjp(gelu_tanh, pre_act)
-        activated[step] = value.astype(bf16)
-        grad_pre[step] = gelu_pull(grad_activated[step])[0].astype(bf16)
-
-    def mixed_part(step):
-        part = jnp.einsum(
-            "tf,df->td", grad_pre[step], expand_weight, preferred_element_type=f32
-        ).astype(bf16)
-        return part[:shard_rows], part[shard_rows:]
-
-    grad_mixed = ring_scatter(mixed_part)
+        with jax.named_scope(f"mixed_ring{step}"):
+            if step:
+                moving = ring_step(moving if step < 3 else after(moving, mixed_terms[step - 2]))
+            mixed_step(step)
+        if step:
+            with jax.named_scope(f"grad_mixed_ring{step}"):
+                total = chip_total(mixed_terms[step], mixed_arrivals)
+                mixed_arrivals.append(ring_step(total.astype(bf16)))
+    second = mixed_arrivals[-2]
+    activated_all = after(ordered(activated), second)
+    grad_pre_all = after(ordered(grad_pre), second)
+    mixed_all = ordered(mixed)
+    with jax.named_scope("contract_gradient"):
+        contract_local = (share * dot(activated_all, grad_out, 0, 0)).astype(bf16)
+    with jax.named_scope("expand_gradient"):
+        expand_local = (share * dot(mixed_all, grad_pre_all, 0, 0)).astype(bf16)
+    mixed_arrivals[-1] = after(mixed_arrivals[-1], contract_local, expand_local)
+    with jax.named_scope("grad_mixed_own"):
+        grad_mixed = chip_total(mixed_terms[0], mixed_arrivals)
 
     grad_local = grad_rows_low.astype(f32)
     grad_hidden = grad_local + normalize_back(grad_mixed, feedforward_gain, unit_two, inverse_two)
     grad_hidden_low = grad_hidden.astype(bf16)
-    grad_context_rows = jnp.einsum(
-        "td,jd->tj", grad_hidden_low, output_full, preferred_element_type=f32
-    ).astype(bf16)
-    grad_context = lax.all_to_all(
-        grad_context_rows, "tensor", split_axis=1, concat_axis=0, tiled=True
-    )
+    with jax.named_scope("grad_hidden_gather"):
+        grad_hidden_all = lax.all_gather(grad_hidden_low, "tensor", axis=0, tiled=True)
+
+    with jax.named_scope("contract_dp"):
+        contract_half = dp_halves(contract_local, bits[:1], 0, [(grad_hidden_low,)])[-1]
+        contract_cut = dp_halves(contract_half, bits[1:], 0, [(grad_hidden_all,)])[-1]
+    with jax.named_scope("expand_dp"):
+        expand_half = dp_halves(expand_local, bits[::-1][:1], 0, [(grad_hidden_low,)])[-1]
+        expand_cut = dp_halves(expand_half, bits[::-1][1:], 0, [(grad_hidden_all,)])[-1]
+    grad_hidden_all = after(grad_hidden_all, contract_cut, expand_cut)
+    with jax.named_scope("grad_context"):
+        grad_context = dot(grad_hidden_all, output_weight, 1, 1).astype(bf16)
+
+    branch_terms = [
+        dot(after(block, grad_hidden_low), contract_weight, 1, 0).astype(bf16) for block in activated
+    ]
+
+    def branch_part(step):
+        block = after(branch_terms[step], grad_hidden_all)
+        return block[:shard_rows], block[shard_rows:]
+
+    def branch_total(step):
+        mine, other = branch_part(step)
+        return mine.astype(f32) + swap_cores(other).astype(f32)
+
+    with jax.named_scope("branch_ring1"):
+        branch_arrived = ring_step(branch_total(1).astype(bf16))
+
+    with jax.named_scope("output_gradient"):
+        output_local = (share * dot(context, grad_hidden_all, 0, 0)).astype(bf16)
+    with jax.named_scope("output_dp"):
+        output_gradient = lax.psum(output_local, "dp")
     projected_grad = attend_back(own_bounds, projected, grad_context, context, totals, local_heads)
-
-    def normed_part(step):
-        rows = lax.dynamic_slice_in_dim(
-            projected_grad, ring_chip(step) * 2 * shard_rows, 2 * shard_rows
-        )
-        part = jnp.einsum("tj,dj->td", rows, weight_flat, preferred_element_type=f32).astype(bf16)
-        return (
-            lax.dynamic_slice_in_dim(part, core * shard_rows, shard_rows),
-            lax.dynamic_slice_in_dim(part, (1 - core) * shard_rows, shard_rows),
-        )
-
-    grad_normed = ring_scatter(normed_part)
+    projected_grad, branch_arrived = lax.optimization_barrier((projected_grad, branch_arrived))
+
+    normed_terms = []
+    with jax.named_scope("normed_terms"):
+        for step in range(chips):
+            rows = lax.dynamic_slice_in_dim(
+                projected_grad, ring_chip(step) * 2 * shard_rows, 2 * shard_rows
+            )
+            normed_terms.append(dot(rows, weight_flat, 1, 1).astype(bf16))
+    projected_late = after(projected_grad, *normed_terms)
+    with jax.named_scope("projection_gradient"):
+        projection_local = (share * dot(normed, projected_late, 0, 0)).astype(bf16)
+
+    def normed_total(step):
+        mine = lax.dynamic_slice_in_dim(normed_terms[step], core * shard_rows, shard_rows)
+        other = lax.dynamic_slice_in_dim(normed_terms[step], (1 - core) * shard_rows, shard_rows)
+        return mine.astype(f32) + swap_cores(other).astype(f32)
+
+
+    normed_arrivals = []
+
+    def normed_step(step, *meanwhile):
+        total = normed_total(step)
+        if normed_arrivals:
+            total = total + after(normed_arrivals[-1], *meanwhile).astype(f32)
+        with jax.named_scope(f"grad_normed_ring{step}"):
+            normed_arrivals.append(ring_step(total.astype(bf16)))
+
+    with jax.named_scope("contract_dp"):
+        contract_blocks, contract_first = dp_blocks(
+            contract_cut, bits[::-1], [(projected_late,), (projected_late,)]
+        )
+    with jax.named_scope("expand_dp"):
+        expand_blocks, expand_first = dp_blocks(
+            expand_cut, bits, [(projected_late,), (projected_late,)]
+        )
+    for step in range(1, chips):
+        normed_step(step, *((contract_first, expand_first) if step == 2 else ()))
+    last = normed_arrivals[-1]
+    with jax.named_scope("projection_dp"):
+        projection_gradient = lax.psum(
+            after(projection_local, normed_arrivals[0], output_gradient), "dp"
+        )
+    projection_gradient = projection_gradient.reshape(features, 3, local_width).astype(f32)
+    output_gradient = output_gradient.astype(f32)
+    with jax.named_scope("grad_normed_own"):
+        grad_normed = normed_total(0) + last.astype(f32)
+
+    branch_arrived = after(branch_arrived, last)
+    for step in range(2, chips):
+        with jax.named_scope(f"branch_ring{step}"):
+            total = branch_total(step) + branch_arrived.astype(f32)
+            branch_arrived = ring_step(total.astype(bf16))
+    with jax.named_scope("branch_own"):
+        branch = branch_total(0) + branch_arrived.astype(f32)
+    layer_output = (local_live * (hidden + branch + contract_bias)).astype(bf16)
     input_gradient = (
         grad_hidden + normalize_back(grad_normed, attention_gain, unit_one, inverse_one)
     ).astype(bf16)
 
-    def branch_part(step):
-        part = jnp.dot(
-            after(activated[step], grad_mixed), contract_weight, preferred_element_type=f32
-        ).astype(bf16)
-        return part[:shard_rows], part[shard_rows:]
-
-    branch = ring_scatter(branch_part)
-    layer_output = (local_live * (hidden + branch + contract_bias)).astype(bf16)
-
-    activated_all = jnp.concatenate(activated, axis=0)
-    grad_out_all = jnp.concatenate(grad_out, axis=0)
-    contract_gradient = dp_sum(
-        (
-            share
-            * jnp.einsum("tf,td->fd", activated_all, grad_out_all, preferred_element_type=f32)
-        ).astype(bf16)
-    )
-    mixed_all = jnp.concatenate(mixed, axis=0)
-    grad_pre_all = jnp.concatenate(grad_pre, axis=0)
-    expand_gradient = dp_sum(
-        (
-            share * jnp.einsum("td,tf->df", mixed_all, grad_pre_all, preferred_element_type=f32)
-        ).astype(bf16)
-    )
-    grad_hidden_all = lax.all_gather(
-        after(grad_hidden_low, grad_context), "tensor", axis=0, tiled=True
-    )
-    output_gradient = dp_sum(
-        (
-            share * jnp.einsum("tj,td->jd", context, grad_hidden_all, preferred_element_type=f32)
-        ).astype(bf16)
-    )
-    projection_gradient = dp_sum(
-        (
-            share * jnp.einsum("td,tj->dj", normed, projected_grad, preferred_element_type=f32)
-        ).astype(bf16)
-    ).reshape(features, 3, local_width)
-
+    contract_gradient = jnp.zeros(contract_local.shape, f32)
+    for mask, block in contract_blocks:
+        contract_gradient = put(
+            contract_gradient, after(block, last), cut_place(mask, bits, contract_local.shape[0])
+        )
+    expand_gradient = jnp.zeros(expand_local.shape, f32)
+    for mask, block in expand_blocks:
+        expand_gradient = put(
+            expand_gradient, after(block, last), cut_place(mask, bits[::-1], expand_local.shape[0])
+        )
+    sums_by_row = share * jnp.stack(
+        [
+            jnp.sum(grad_normed * unit_one, axis=0),
+            jnp.sum(grad_normed, axis=0),
+            jnp.sum(grad_hidden, axis=0),
+            jnp.sum(grad_mixed * unit_two, axis=0),
+            jnp.sum(grad_mixed, axis=0),
+            jnp.sum(grad_local, axis=0),
+        ]
+    )
     column_sums = jnp.sum(projected_grad.astype(f32), axis=0)
     sums_by_width = share * jnp.concatenate(
         [
@@ -480,43 +639,30 @@
             jnp.sum(grad_pre_all.astype(f32), axis=0),
         ]
     )
-    sums_by_width = small_sum(sums_by_width, ("dp",))
+    own_columns = features // tensor_size
+    with jax.named_scope("small_sums"):
+        sums_by_row = small_sum(sums_by_row, ("tensor",))
+        sums_by_row = lax.dynamic_slice_in_dim(sums_by_row, rank * own_columns, own_columns, 1)
+        sums = small_sum(jnp.concatenate([sums_by_row.reshape(-1), sums_by_width]), ("dp",))
+    sums_by_row = sums[: 6 * own_columns].reshape(6, own_columns)
+    sums_by_width = sums[6 * own_columns :]
     query_value_gradient = sums_by_width[: 2 * local_width].reshape(2, local_width)
     expand_bias_gradient = sums_by_width[2 * local_width :]
-
-    early_sums = share * jnp.stack(
-        [
-            jnp.sum(grad_hidden, axis=0),
-            jnp.sum(grad_mixed * unit_two, axis=0),
-            jnp.sum(grad_mixed, axis=0),
-            jnp.sum(grad_local, axis=0),
-        ]
-    )
-    late_sums = share * jnp.stack(
-        [jnp.sum(grad_normed * unit_one, axis=0), jnp.sum(grad_normed, axis=0)]
-    )
-    columns = features // tensor_size
-    early_sums = lax.dynamic_slice_in_dim(
-        small_sum(early_sums, ("tensor", "dp")), rank * columns, columns, 1
-    )
-    late_sums = lax.dynamic_slice_in_dim(
-        small_sum(late_sums, ("tensor", "dp")), rank * columns, columns, 1
-    )
     return (
         layer_output,
         input_gradient,
-        late_sums[0],
-        late_sums[1],
-        projection_gradient.astype(f32),
+        sums_by_row[0],
+        sums_by_row[1],
+        projection_gradient,
         query_value_gradient,
-        output_gradient.astype(f32),
-        early_sums[0],
-        early_sums[1],
-        early_sums[2],
-        expand_gradient.astype(f32),
+        output_gradient,
+        sums_by_row[2],
+        sums_by_row[3],
+        sums_by_row[4],
+        expand_gradient,
         expand_bias_gradient,
-        contract_gradient.astype(f32),
-        early_sums[3],
+        contract_gradient,
+        sums_by_row[5],
     )
 
 

time: 848 us -> 732 us (0.86)
  waiting for transfers between devices: 427 us -> 316 us
  starting transfers between devices: 97.6 us -> 51 us
  local copies, waits for them, and re-layouts: 55.4 us -> 73.9 us
  other arithmetic: 65 us -> 75.9 us
    ppermute x18 -> x15, waiting for transfers between devices: 295 us -> 127 us  [ring_step(): return lax.ppermute(value, 'tensor', pairs)]
    all_to_all x2 -> x1, waiting for transfers between devices: 0.01 us -> 45.1 us  [shards(): lax.all_to_all(context.reshape(tensor_size, shard_rows, local_width), 'te...]
    psum x0 -> x2, waiting for transfers between devices: none -> 32.4 us  [the longest x1 16.7 us: shards(): output_gradient = lax.psum(output_local, 'dp')]
    all_gather x1, waiting for transfers between devices: 24.1 us -> 0.01 us  [shards(): normed = lax.all_gather(normed_rows, 'tensor', axis=0, tiled=True)]
    ppermute x32 -> x12, waiting for transfers between devices: 67.7 us -> 91.1 us  [flip_dp(): return lax.ppermute(value, 'dp', [(i, i ^ bit) for i in range(size)])]
    ppermute x12 -> x5, waiting for transfers between devices: 29.5 us -> 6.68 us  [small_sum(): lax.ppermute(value, axis, [(i, i ^ bit) for i in range(size)])]
    ppermute x32 -> x12, starting transfers between devices: 40 us -> 17.3 us  [flip_dp(): return lax.ppermute(value, 'dp', [(i, i ^ bit) for i in range(size)])]
    ppermute x18 -> x15, starting transfers between devices: 30.3 us -> 11.7 us  [ring_step(): return lax.ppermute(value, 'tensor', pairs)]
  transfers between devices with their start and end apart: 91 -> 55, of which waited for: 43 -> 25; matrix products, arithmetic and copies ran while one was open for 28% -> 37% of each run, Pallas kernels for 4% -> 5%
where the time goes in v2:
time: 732 us; the launch traced here: 723 us
  waiting for transfers between devices  316 us (43%)
  matrix products  142 us (19%)
  other arithmetic  75.9 us (10%)
  local copies, waits for them, and re-layouts  73.9 us (10%)
  starting transfers between devices  51 us (7%)
  Pallas kernels  38.1 us (5%)
  between operations  25.2 us (3%)
    dot_general x28, matrix products, dot(): lax.dot_general(a, b, (((a_axis,), (b_axis,)), ((), ())), preferred_eleme...  142 us
    ppermute x15, waiting for transfers between devices, ring_step(): return lax.ppermute(value, 'tensor', pairs)  127 us
    ppermute x12, waiting for transfers between devices, flip_dp(): return lax.ppermute(value, 'dp', [(i, i ^ bit) for i in range(size)])  91.1 us
    all_to_all x1, waiting for transfers between devices, shards(): lax.all_to_all(context.reshape(tensor_size, shard_rows, local_width), 'te...  45.1 us
    pallas_call x1, Pallas kernels, attend_back(): pl.pallas_call(functools.partial(attend_back_kernel, block, local_heads),...  21.6 us
    unnamed x149, local copies, waits for them, and re-layouts  18 us
    ppermute x12, starting transfers between devices, flip_dp(): return lax.ppermute(value, 'dp', [(i, i ^ bit) for i in range(size)])  17.3 us
    psum x1, waiting for transfers between devices, shards(): output_gradient = lax.psum(output_local, 'dp')  16.7 us
  transfers between devices with their start and end apart: 55, of which 25 were waited for; matrix products, arithmetic and copies ran while one was open for 37% of the time, Pallas kernels for 5%

profile of v2, /device:TPU:0, one launch (start us, length us, event | category | flops | bytes accessed | tf_op | source)
XLA Modules:
  0.0 722.7 jit_solution(16499340155165654787)
XLA Ops:
  15.2 7.3 %collective-permute-done = bf16[256,512]{1,0:T(8,128)(2,1)S(1)} collective-permute-done((bf16[256,512]{1,0:T(8,128)(2,1)S(1)}, bf16[256,512]{1,0:T(8,128)(2,1)S(1)}, u32[]{:S(2)}, u32[]{:S(2)}) %collective-permute-start) | collective-permute-done | bytes 262176 | tf_op jit(solution)/shard_map/weight_ring/ppermute | solution.py:241
  25.6 18.9 %collective-permute-done.3 = bf16[256,512]{1,0:T(8,128)(2,1)S(1)} collective-permute-done((bf16[256,512]{1,0:T(8,128)(2,1)S(1)}, bf16[256,512]{1,0:T(8,128)(2,1)S(1)}, u32[]{:S(2)}, u32[]{:S(2)}) %collective-permute-start.3) | collective-permute-done | bytes 262176 | tf_op jit(solution)/shard_map/weight_ring/ppermute | solution.py:241
  48.8 16.5 %collective-permute-done.4 = bf16[256,512]{1,0:T(8,128)(2,1)S(1)} collective-permute-done((bf16[256,512]{1,0:T(8,128)(2,1)S(1)}, bf16[256,512]{1,0:T(8,128)(2,1)S(1)}, u32[]{:S(2)}, u32[]{:S(2)}) %collective-permute-start.4) | collective-permute-done | bytes 262176 | tf_op jit(solution)/shard_map/weight_ring/ppermute | solution.py:241
  66.9 13.3 %collective-permute-done.5 = bf16[512,512]{1,0:T(8,128)(2,1)S(1)} collective-permute-done((bf16[512,512]{1,0:T(8,128)(2,1)S(1)}, bf16[512,512]{1,0:T(8,128)(2,1)S(1)}, u32[]{:S(2)}, u32[]{:S(2)}) %collective-permute-start.5) | collective-permute-done | bytes 524320 | tf_op jit(solution)/shard_map/weight_dp/ppermute | solution.py:296
  88.2 13.8 %collective-permute-done.6 = bf16[1024,512]{1,0:T(8,128)(2,1)} collective-permute-done((bf16[1024,512]{1,0:T(8,128)(2,1)}, bf16[1024,512]{1,0:T(8,128)(2,1)}, u32[]{:S(2)}, u32[]{:S(2)}) %collective-permute-start.6) | collective-permute-done | bytes 1048608 | tf_op jit(solution)/shard_map/weight_dp/ppermute | solution.py:296
  105.8 4.8 copy.86
  114.0 10.1 %add_convert_fusion.q_ref.k_ref.v_ref = bf16[2048,768]{1,0:T(8,128)(2,1)S(1)} fusion(f32[768]{0:T(1024)S(1)} %pad_maximum_fusion.7, bf16[2048,2048]{1,0:T(8,128)(2,1)} %all-gather.4.cloned.1.call-done, bf16[2048,768]{0,1:T(8,128)(2,1)} %bitcast.175), kind=kOutput, calls=%fused_computation.5 | convolution fusion | flops 6445596672 | bytes 14683136 | tf_op jit(solution)/shard_map/dot_general | solution.py:400
  124.1 16.5 %shard_map.758 = (bf16[2048,256]{1,0:T(8,128)(2,1)}, f32[2,1,2048]{2,1,0:T(1,128)S(1)}) custom-call(s32[2]{0:T(128)S(1)} %get-tuple-element.129.bounds_ref, bf16[2048,768]{1,0:T(8,128)(2,1)S(1)} %add_convert_fusion.q_ref.k_ref.v_ref, bf16[2048,768]{1,0:T(8,128)(2,1)S(1)} %add_convert_fusion.q_ref.k_ref.v_ref, ...), custom_call_target="tpu_custom_call" | custom-call | flops 4294967296 | bytes 4194304 | tf_op jit(solution)/shard_map/pallas_call | solution.py:73
  140.6 10.1 %all-to-all-start = ((bf16[8,256,256]{2,1,0:T(8,128)(2,1)}), bf16[8,256,256]{2,1,0:T(8,128)(2,1)S(1)}, u32[]{:S(2)}, u32[]{:S(2)}) async-start(bf16[8,256,256]{2,1,0:T(8,128)(2,1)} %bitcast.4), calls=%async_computation | async-start | bytes 2097152 | tf_op jit(solution)/shard_map/all_to_all | solution.py:455
  160.5 45.1 %all-to-all-done = bf16[8,256,256]{2,1,0:T(8,128)(2,1)S(1)} async-done(((bf16[8,256,256]{2,1,0:T(8,128)(2,1)}), bf16[8,256,256]{2,1,0:T(8,128)(2,1)S(1)}, u32[]{:S(2)}, u32[]{:S(2)}) %all-to-all-start) | async-done | bytes 1048608 | tf_op jit(solution)/shard_map/all_to_all | solution.py:455
  205.8 3.8 fusion.109
  213.3 10.5 %all-gather.6.cloned.1.call-done = bf16[2048,2048]{1,0:T(8,128)(2,1)} async-done(((bf16[256,2048]{1,0:T(8,128)(2,1)}), bf16[2048,2048]{1,0:T(8,128)(2,1)}) %all-gather.6.cloned.1.call-update) | async-done | bytes 8388624 | tf_op jit(solution)/shard_map/all_gather | solution.py:450
  225.7 4.3 constant_dynamic-slice_fusion.17
  231.4 5.0 fusion.46
  244.2 8.0 %collective-permute-done.10 = bf16[256,2048]{1,0:T(8,128)(2,1)} collective-permute-done((bf16[256,2048]{1,0:T(8,128)(2,1)}, bf16[256,2048]{1,0:T(8,128)(2,1)}, u32[]{:S(2)}, u32[]{:S(2)}) %collective-permute-start.10) | collective-permute-done | bytes 1048608 | tf_op jit(solution)/shard_map/mixed_ring1/ppermute | solution.py:241
  255.3 4.9 fusion.62
  260.2 6.7 fusion.31
  270.0 9.3 %collective-permute-done.11 = bf16[256,2048]{1,0:T(8,128)(2,1)S(1)} collective-permute-done((bf16[256,2048]{1,0:T(8,128)(2,1)}, bf16[256,2048]{1,0:T(8,128)(2,1)S(1)}, u32[]{:S(2)}, u32[]{:S(2)}) %collective-permute-start.11) | collective-permute-done | bytes 1048608 | tf_op jit(solution)/shard_map/mixed_ring2/ppermute | solution.py:241
  284.3 6.4 fusion.45
  290.8 4.6 convolution_convert_fusion.4
  295.8 10.4 %collective-permute-done.13 = bf16[256,2048]{1,0:T(8,128)(2,1)S(1)} collective-permute-done((bf16[256,2048]{1,0:T(8,128)(2,1)S(1)}, bf16[256,2048]{1,0:T(8,128)(2,1)S(1)}, u32[]{:S(2)}, u32[]{:S(2)}) %collective-permute-start.13) | collective-permute-done | bytes 1048608 | tf_op jit(solution)/shard_map/mixed_ring3/ppermute | solution.py:241
  306.5 20.9 %collective-permute-done.16 = bf16[256,2048]{1,0:T(8,128)(2,1)S(1)} collective-permute-done((bf16[256,2048]{1,0:T(8,128)(2,1)S(1)}, bf16[256,2048]{1,0:T(8,128)(2,1)S(1)}, u32[]{:S(2)}, u32[]{:S(2)}) %collective-permute-start.16) | collective-permute-done | bytes 1048608 | tf_op jit(solution)/shard_map/grad_mixed_ring1/ppermute | solution.py:241
  331.2 7.6 %multiply_convert_fusion.4 = (bf16[512,1024]{1,0:T(8,128)(2,1)S(1)}, bf16[512,1024]{1,0:T(8,128)(2,1)S(1)}, bf16[512,1024]{1,0:T(8,128)(2,1)S(1)}, bf16[512,1024]{1,0:T(8,128)(2,1)S(1)}, f32[512,1024]{1,0:T(8,128)}) fusion(f32[1024]{0:T(1024)S(1)} %copy-done.63, f32[512,1024]{1,0:T(8,128)} %copy-done.66, f32[512,1024]{1,0:T(8,128)} %fusion.62, ...), kind=kOutput, calls=%fused_computation.133 | convolution fusion | flops 2168455168 | bytes 18878464 | tf_op jit(solution)/shard_map/mixed_ring3/dot_general | solution.py:400
  338.8 8.2 %fusion.38 = bf16[512,1024]{1,0:T(8,128)(2,1)S(1)} fusion(f32[512,1024]{1,0:T(8,128)} %get-tuple-element.173, bf16[1024,2048]{1,0:T(8,128)(2,1)} %param.83, bf16[256,2048]{1,0:T(8,128)(2,1)S(1)} %get-tuple-element.136, bf16[256,2048]{1,0:T(8,128)(2,1)S(1)} %get-tuple-element.137, f32[1024]{0:T(1024)S(1)} %copy-done.63), kind=kOutput, calls=%fused_computation.73 | convolution fusion | flops 2162688000 | bytes 9441280 | tf_op jit(solution)/shard_map/mixed_ring3/dot_general | solution.py:400
  356.5 11.0 %multiply_convert_fusion.1 = bf16[1024,2048]{1,0:T(8,128)(2,1)} fusion(bf16[2048,1024]{1,0:T(8,128)(2,1)S(1)} %bitcast.174, bf16[2048,2048]{1,0:T(8,128)(2,1)S(1)} %bitcast.172, f32[]{:T(128)S(6)} %div.69), kind=kOutput, calls=%fused_computation.2 | convolution fusion | flops 8594128896 | bytes 16777220 | tf_op jit(solution)/shard_map/contract_gradient/dot_general | solution.py:400
  367.5 10.9 %multiply_convert_fusion = bf16[2048,1024]{1,0:T(8,128)(2,1)} fusion(bf16[2048,2048]{1,0:T(8,128)(2,1)S(1)} %bitcast.173, bf16[2048,1024]{1,0:T(8,128)(2,1)S(1)} %bitcast.168, f32[]{:T(128)S(6)} %div.69), kind=kOutput, calls=%fused_computation.1 | convolution fusion | flops 8594128896 | bytes 16777220 | tf_op jit(solution)/shard_map/expand_gradient/dot_general | solution.py:400
  378.4 4.0 collective-permute-done.21
  397.7 6.0 convolution_convert_fusion
  407.5 30.6 %collective-permute-done.22 = bf16[512,2048]{1,0:T(8,128)(2,1)} collective-permute-done((bf16[512,2048]{1,0:T(8,128)(2,1)}, bf16[512,2048]{1,0:T(8,128)(2,1)}, u32[]{:S(2)}, u32[]{:S(2)}) %collective-permute-start.22) | collective-permute-done | bytes 2097184 | tf_op jit(solution)/shard_map/contract_dp/ppermute | solution.py:296
  446.0 3.8 convolution_convert_fusion.2
  449.7 14.7 %collective-permute-done.23 = bf16[256,2048]{1,0:T(8,128)(2,1)} collective-permute-done((bf16[256,2048]{1,0:T(8,128)(2,1)S(1)}, bf16[256,2048]{1,0:T(8,128)(2,1)}, u32[]{:S(2)}, u32[]{:S(2)}) %collective-permute-start.23) | collective-permute-done | bytes 1048608 | tf_op jit(solution)/shard_map/contract_dp/ppermute | solution.py:296
  475.1 6.6 convolution_convert_fusion.3
  481.7 4.8 fusion.2
  489.5 6.2 convolution_convert_fusion.12.grad_ref
  502.0 21.6 %shard_map.759 = bf16[2048,768]{1,0:T(8,128)(2,1)S(1)} custom-call(s32[2]{0:T(128)S(1)} %get-tuple-element.129.bounds_ref, bf16[2048,768]{1,0:T(8,128)(2,1)} %copy-done.3, bf16[2048,768]{1,0:T(8,128)(2,1)} %copy-done.3, bf16[2048,768]{1,0:T(8,128)(2,1)} %copy-done.3, bf16[2048,256]{1,0:T(8,128)(2,1)S(1)} %convolution_convert_fusion.12.grad_ref, ...), custom_call_target="tpu_custom_call" | custom-call | flops 10737418240 | bytes 8388608 | tf_op jit(solution)/shard_map/pallas_call | solution.py:174
  525.3 16.7 %all-reduce.3.cloned.1.call-done = bf16[256,2048]{1,0:T(8,128)(2,1)} async-done(((bf16[256,2048]{1,0:T(8,128)(2,1)}), bf16[256,2048]{1,0:T(8,128)(2,1)}) %all-reduce.3.cloned.1.call-update) | async-done | bytes 1048592 | tf_op jit(solution)/shard_map/output_dp/psum | solution.py:552
  545.0 3.8 convolution_convert_fusion.9
  565.2 14.7 %collective-permute-done.34 = bf16[256,2048]{1,0:T(8,128)(2,1)S(1)} collective-permute-done((bf16[256,2048]{1,0:T(8,128)(2,1)S(1)}, bf16[256,2048]{1,0:T(8,128)(2,1)S(1)}, u32[]{:S(2)}, u32[]{:S(2)}) %collective-permute-start.34) | collective-permute-done | bytes 1048608 | tf_op jit(solution)/shard_map/grad_normed_ring1/ppermute | solution.py:241
  582.6 8.2 %multiply_convert_fusion.2 = bf16[2048,768]{1,0:T(8,128)(2,1)} fusion(bf16[2048,2048]{1,0:T(8,128)(2,1)S(1)} %bitcast.189, bf16[2048,768]{1,0:T(8,128)(2,1)S(1)} %copy-done.2, f32[]{:T(128)S(6)} %div.69), kind=kOutput, calls=%fused_computation.3 | convolution fusion | flops 6445596672 | bytes 14680068 | tf_op jit(solution)/shard_map/projection_gradient/dot_general | solution.py:400
  591.3 15.5 %collective-permute-done.37 = bf16[256,2048]{1,0:T(8,128)(2,1)S(1)} collective-permute-done((bf16[256,2048]{1,0:T(8,128)(2,1)S(1)}, bf16[256,2048]{1,0:T(8,128)(2,1)S(1)}, u32[]{:S(2)}, u32[]{:S(2)}) %collective-permute-start.37) | collective-permute-done | bytes 1048608 | tf_op jit(solution)/shard_map/grad_normed_ring2/ppermute | solution.py:241
  609.9 4.7 copy.87
  615.0 18.6 %collective-permute-done.48 = bf16[512,2048]{1,0:T(8,128)(2,1)} collective-permute-done((bf16[512,2048]{1,0:T(8,128)(2,1)}, bf16[512,2048]{1,0:T(8,128)(2,1)}, u32[]{:S(2)}, u32[]{:S(2)}) %collective-permute-start.48) | collective-permute-done | bytes 2097184 | tf_op jit(solution)/shard_map/contract_dp/ppermute | solution.py:296
  643.4 3.8 fusion.16
  647.8 4.3 fusion.15
  657.8 4.1 collective-permute-start.43
  661.9 4.5 broadcast_in_dim.151
  691.0 15.7 %all-reduce.5.cloned.1.call-done = bf16[2048,3,256]{0,2,1:T(8,128)(2,1)} async-done(((bf16[2048,3,256]{0,2,1:T(8,128)(2,1)}), bf16[2048,3,256]{0,2,1:T(8,128)(2,1)}) %all-reduce.5.cloned.1.call-update) | async-done | bytes 3145744 | tf_op jit(solution)/shard_map/projection_dp/psum | solution.py:594
  706.7 5.4 copy.88
  (384 shorter events, 190.2 us)
Async XLA Ops:
  7.2 106.7 %all-gather.4.cloned.1.call-start = ((), (), s32[]{:S(2)}) async-start(), calls=%async_computation.1 | async-start | bytes 9437184 | tf_op jit(solution)/shard_map/all_gather | solution.py:422
  12.0 211.8 %all-gather.6.cloned.1.call-start = ((), (), s32[]{:S(2)}) async-start(), calls=%async_computation.2 | async-start | bytes 9437184 | tf_op jit(solution)/shard_map/all_gather | solution.py:450
  12.1 10.4 %collective-permute-start = (bf16[256,512]{1,0:T(8,128)(2,1)S(1)}, bf16[256,512]{1,0:T(8,128)(2,1)S(1)}, u32[]{:S(2)}, u32[]{:S(2)}) collective-permute-start(bf16[256,512]{1,0:T(8,128)(2,1)S(1)} %constant_dynamic-slice_fusion.18), channel_id=1, source_target_pairs={{0,2},{1,3},{2,6},{3,7},{6,4},{7,5},{4,0},{5,1},{8,10},{9,11},{10,... | collective-permute-start | bytes 786440 | tf_op jit(solution)/shard_map/weight_ring/ppermute | solution.py:241
  23.2 23.3 %collective-permute-start.1 = (bf16[512,512]{1,0:T(8,128)(2,1)S(1)}, bf16[512,512]{1,0:T(8,128)(2,1)S(1)}, u32[]{:S(2)}, u32[]{:S(2)}) collective-permute-start(bf16[512,512]{1,0:T(8,128)(2,1)S(1)} %get-tuple-element.151), channel_id=1, source_target_pairs={{0,8},{8,0},{16,24},{24,16},{1,9},{9,1},{17,25},{25,17},{2,10},{10... | collective-permute-start | bytes 1572872 | tf_op jit(solution)/shard_map/weight_dp/ppermute | solution.py:296
  24.8 19.6 %collective-permute-start.3 = (bf16[256,512]{1,0:T(8,128)(2,1)S(1)}, bf16[256,512]{1,0:T(8,128)(2,1)S(1)}, u32[]{:S(2)}, u32[]{:S(2)}) collective-permute-start(bf16[256,512]{1,0:T(8,128)(2,1)S(1)} %collective-permute-done), channel_id=1, source_target_pairs={{0,2},{1,3},{2,6},{3,7},{6,4},{7,5},{4,0},{5,1},{8,10},{9,11},{10,... | collective-permute-start | bytes 786440 | tf_op jit(solution)/shard_map/weight_ring/ppermute | solution.py:241
  44.4 20.9 %collective-permute-start.4 = (bf16[256,512]{1,0:T(8,128)(2,1)S(1)}, bf16[256,512]{1,0:T(8,128)(2,1)S(1)}, u32[]{:S(2)}, u32[]{:S(2)}) collective-permute-start(bf16[256,512]{1,0:T(8,128)(2,1)S(1)} %collective-permute-done.3), channel_id=1, source_target_pairs={{0,2},{1,3},{2,6},{3,7},{6,4},{7,5},{4,0},{5,1},{8,10},{9,11},{10,... | collective-permute-start | bytes 786440 | tf_op jit(solution)/shard_map/weight_ring/ppermute | solution.py:241
  47.5 35.3 %collective-permute-start.2 = (bf16[1024,512]{1,0:T(8,128)(2,1)}, bf16[1024,512]{1,0:T(8,128)(2,1)}, u32[]{:S(2)}, u32[]{:S(2)}) collective-permute-start(bf16[1024,512]{1,0:T(8,128)(2,1)} %pad_maximum_fusion.3), channel_id=1, source_target_pairs={{0,16},{8,24},{16,0},{24,8},{1,17},{9,25},{17,1},{25,9},{2,18},{10... | collective-permute-start | bytes 3145736 | tf_op jit(solution)/shard_map/weight_dp/ppermute | solution.py:296
  65.4 14.9 %collective-permute-start.5 = (bf16[512,512]{1,0:T(8,128)(2,1)S(1)}, bf16[512,512]{1,0:T(8,128)(2,1)S(1)}, u32[]{:S(2)}, u32[]{:S(2)}) collective-permute-start(bf16[512,512]{1,0:T(8,128)(2,1)S(1)} %constant_dynamic-update-slice_fusion.2), channel_id=1, source_target_pairs={{0,16},{8,24},{16,0},{24,8},{1,17},{9,25},{17,1},{25,9},{2,18},{10... | collective-permute-start | bytes 1572872 | tf_op jit(solution)/shard_map/weight_dp/ppermute | solution.py:296
  81.3 20.8 %collective-permute-start.6 = (bf16[1024,512]{1,0:T(8,128)(2,1)}, bf16[1024,512]{1,0:T(8,128)(2,1)}, u32[]{:S(2)}, u32[]{:S(2)}) collective-permute-start(bf16[1024,512]{1,0:T(8,128)(2,1)} %pad_maximum_fusion.4), channel_id=1, source_target_pairs={{0,8},{8,0},{16,24},{24,16},{1,9},{9,1},{17,25},{25,17},{2,10},{10... | collective-permute-start | bytes 3145736 | tf_op jit(solution)/shard_map/weight_dp/ppermute | solution.py:296
  105.8 8.1 %collective-permute-start.7 = (bf16[1024,2048]{1,0:T(8,128)(2,1)}, bf16[1024,2048]{1,0:T(8,128)(2,1)}, u32[]{:S(2)}, u32[]{:S(2)}) collective-permute-start(bf16[1024,2048]{1,0:T(8,128)(2,1)} %slice_dynamic-update-slice_fusion), channel_id=1, source_target_pairs={{0,1},{1,0},{2,3},{3,2},{4,5},{5,4},{6,7},{7,6},{8,9},{9,8},{10,11... | collective-permute-start | bytes 12582920 | tf_op jit(solution)/shard_map/ppermute | solution.py:245
  140.6 65.0 %all-to-all-start = ((bf16[8,256,256]{2,1,0:T(8,128)(2,1)}), bf16[8,256,256]{2,1,0:T(8,128)(2,1)S(1)}, u32[]{:S(2)}, u32[]{:S(2)}) async-start(bf16[8,256,256]{2,1,0:T(8,128)(2,1)} %bitcast.4), calls=%async_computation | async-start | bytes 2097152 | tf_op jit(solution)/shard_map/all_to_all | solution.py:455
  150.7 317.4 %all-gather.8.cloned.1.call-start = ((), (), s32[]{:S(2)}) async-start(), calls=%async_computation.3 | async-start | bytes 9437184 | tf_op jit(solution)/shard_map/grad_hidden_gather/all_gather | solution.py:522
  225.4 26.8 %collective-permute-start.10 = (bf16[256,2048]{1,0:T(8,128)(2,1)}, bf16[256,2048]{1,0:T(8,128)(2,1)}, u32[]{:S(2)}, u32[]{:S(2)}) collective-permute-start(bf16[256,2048]{1,0:T(8,128)(2,1)} %add_convert_fusion.14), channel_id=1, source_target_pairs={{0,2},{1,3},{2,6},{3,7},{6,4},{7,5},{4,0},{5,1},{8,10},{9,11},{10,... | collective-permute-start | bytes 3145736 | tf_op jit(solution)/shard_map/mixed_ring1/ppermute | solution.py:241
  243.3 139.1 %collective-permute-start.9 = (bf16[256,2048]{1,0:T(8,128)(2,1)}, bf16[256,2048]{1,0:T(8,128)(2,1)S(1)}, u32[]{:S(2)}, u32[]{:S(2)}) collective-permute-start(bf16[256,2048]{1,0:T(8,128)(2,1)} %slice.217), channel_id=1, source_target_pairs={{0,1},{1,0},{2,3},{3,2},{4,5},{5,4},{6,7},{7,6},{8,9},{9,8},{10,11... | collective-permute-start | bytes 3145736 | tf_op jit(solution)/shard_map/grad_mixed_own/ppermute | solution.py:245
  252.3 27.0 %collective-permute-start.11 = (bf16[256,2048]{1,0:T(8,128)(2,1)}, bf16[256,2048]{1,0:T(8,128)(2,1)S(1)}, u32[]{:S(2)}, u32[]{:S(2)}) collective-permute-start(bf16[256,2048]{1,0:T(8,128)(2,1)} %collective-permute-done.10), channel_id=1, source_target_pairs={{0,2},{1,3},{2,6},{3,7},{6,4},{7,5},{4,0},{5,1},{8,10},{9,11},{10,... | collective-permute-start | bytes 3145736 | tf_op jit(solution)/shard_map/mixed_ring2/ppermute | solution.py:241
  269.4 10.2 %collective-permute-start.15 = (bf16[256,2048]{1,0:T(8,128)(2,1)S(1)}, bf16[256,2048]{1,0:T(8,128)(2,1)S(1)}, u32[]{:S(2)}, u32[]{:S(2)}) collective-permute-start(bf16[256,2048]{1,0:T(8,128)(2,1)S(1)} %slice.219), channel_id=1, source_target_pairs={{0,1},{1,0},{2,3},{3,2},{4,5},{5,4},{6,7},{7,6},{8,9},{9,8},{10,11... | collective-permute-start | bytes 3145736 | tf_op jit(solution)/shard_map/grad_mixed_ring1/ppermute | solution.py:245
  279.3 27.0 %collective-permute-start.13 = (bf16[256,2048]{1,0:T(8,128)(2,1)S(1)}, bf16[256,2048]{1,0:T(8,128)(2,1)S(1)}, u32[]{:S(2)}, u32[]{:S(2)}) collective-permute-start(bf16[256,2048]{1,0:T(8,128)(2,1)S(1)} %collective-permute-done.11), channel_id=1, source_target_pairs={{0,2},{1,3},{2,6},{3,7},{6,4},{7,5},{4,0},{5,1},{8,10},{9,11},{10,... | collective-permute-start | bytes 3145736 | tf_op jit(solution)/shard_map/mixed_ring3/ppermute | solution.py:241
  280.0 47.4 %collective-permute-start.16 = (bf16[256,2048]{1,0:T(8,128)(2,1)S(1)}, bf16[256,2048]{1,0:T(8,128)(2,1)S(1)}, u32[]{:S(2)}, u32[]{:S(2)}) collective-permute-start(bf16[256,2048]{1,0:T(8,128)(2,1)S(1)} %add_convert_fusion.13), channel_id=1, source_target_pairs={{0,2},{1,3},{2,6},{3,7},{6,4},{7,5},{4,0},{5,1},{8,10},{9,11},{10,... | collective-permute-start | bytes 3145736 | tf_op jit(solution)/shard_map/grad_mixed_ring1/ppermute | solution.py:241
  295.4 32.0 %collective-permute-start.19 = (bf16[256,2048]{1,0:T(8,128)(2,1)S(1)}, bf16[256,2048]{1,0:T(8,128)(2,1)S(1)}, u32[]{:S(2)}, u32[]{:S(2)}) collective-permute-start(bf16[256,2048]{1,0:T(8,128)(2,1)S(1)} %slice.223), channel_id=1, source_target_pairs={{0,1},{1,0},{2,3},{3,2},{4,5},{5,4},{6,7},{7,6},{8,9},{9,8},{10,11... | collective-permute-start | bytes 3145736 | tf_op jit(solution)/shard_map/grad_mixed_ring2/ppermute | solution.py:245
  306.2 22.9 %collective-permute-start.14 = (bf16[256,2048]{1,0:T(8,128)(2,1)S(1)}, bf16[256,2048]{1,0:T(8,128)(2,1)S(1)}, u32[]{:S(2)}, u32[]{:S(2)}) collective-permute-start(bf16[256,2048]{1,0:T(8,128)(2,1)S(1)} %collective-permute-done.13), channel_id=1, source_target_pairs={{0,1},{1,0},{2,3},{3,2},{4,5},{5,4},{6,7},{7,6},{8,9},{9,8},{10,11... | collective-permute-start | bytes 3145736 | tf_op jit(solution)/shard_map/mixed_ring3/ppermute | solution.py:245
  328.9 25.3 %collective-permute-start.20 = (bf16[256,2048]{1,0:T(8,128)(2,1)}, bf16[256,2048]{1,0:T(8,128)(2,1)}, u32[]{:S(2)}, u32[]{:S(2)}) collective-permute-start(bf16[256,2048]{1,0:T(8,128)(2,1)} %add_convert_fusion.12), channel_id=1, source_target_pairs={{0,2},{1,3},{2,6},{3,7},{6,4},{7,5},{4,0},{5,1},{8,10},{9,11},{10,... | collective-permute-start | bytes 3145736 | tf_op jit(solution)/shard_map/grad_mixed_ring2/ppermute | solution.py:241
  356.2 26.2 %collective-permute-start.21 = (bf16[256,2048]{1,0:T(8,128)(2,1)S(1)}, bf16[256,2048]{1,0:T(8,128)(2,1)S(1)}, u32[]{:S(2)}, u32[]{:S(2)}) collective-permute-start(bf16[256,2048]{1,0:T(8,128)(2,1)S(1)} %add_convert_fusion.11), channel_id=1, source_target_pairs={{0,2},{1,3},{2,6},{3,7},{6,4},{7,5},{4,0},{5,1},{8,10},{9,11},{10,... | collective-permute-start | bytes 3145736 | tf_op jit(solution)/shard_map/grad_mixed_ring3/ppermute | solution.py:241
  387.4 154.6 %all-reduce.3.cloned.1.call-start = ((), (), s32[]{:S(2)}) async-start(), calls=%async_computation.4 | async-start | bytes 2097152 | tf_op jit(solution)/shard_map/output_dp/psum | solution.py:552
  391.1 47.0 %collective-permute-start.22 = (bf16[512,2048]{1,0:T(8,128)(2,1)}, bf16[512,2048]{1,0:T(8,128)(2,1)}, u32[]{:S(2)}, u32[]{:S(2)}) collective-permute-start(bf16[512,2048]{1,0:T(8,128)(2,1)} %constant_dynamic-slice_fusion.7), channel_id=1, source_target_pairs={{0,8},{8,0},{16,24},{24,16},{1,9},{9,1},{17,25},{25,17},{2,10},{10... | collective-permute-start | bytes 6291464 | tf_op jit(solution)/shard_map/contract_dp/ppermute | solution.py:296
  395.4 47.0 %collective-permute-start.24 = (bf16[1024,1024]{1,0:T(8,128)(2,1)S(1)}, bf16[1024,1024]{1,0:T(8,128)(2,1)S(1)}, u32[]{:S(2)}, u32[]{:S(2)}) collective-permute-start(bf16[1024,1024]{1,0:T(8,128)(2,1)S(1)} %constant_dynamic-slice_fusion.2), channel_id=1, source_target_pairs={{0,16},{8,24},{16,0},{24,8},{1,17},{9,25},{17,1},{25,9},{2,18},{10... | collective-permute-start | bytes 6291464 | tf_op jit(solution)/shard_map/expand_dp/ppermute | solution.py:296
  440.8 23.7 %collective-permute-start.23 = (bf16[256,2048]{1,0:T(8,128)(2,1)S(1)}, bf16[256,2048]{1,0:T(8,128)(2,1)}, u32[]{:S(2)}, u32[]{:S(2)}) collective-permute-start(bf16[256,2048]{1,0:T(8,128)(2,1)S(1)} %constant_dynamic-slice_fusion.1), channel_id=1, source_target_pairs={{0,16},{8,24},{16,0},{24,8},{1,17},{9,25},{17,1},{25,9},{2,18},{10... | collective-permute-start | bytes 3145736 | tf_op jit(solution)/shard_map/contract_dp/ppermute | solution.py:296
  444.5 26.7 %collective-permute-start.25 = (bf16[512,1024]{1,0:T(8,128)(2,1)}, bf16[512,1024]{1,0:T(8,128)(2,1)}, u32[]{:S(2)}, u32[]{:S(2)}) collective-permute-start(bf16[512,1024]{1,0:T(8,128)(2,1)} %constant_dynamic-slice_fusion.3), channel_id=1, source_target_pairs={{0,8},{8,0},{16,24},{24,16},{1,9},{9,1},{17,25},{25,17},{2,10},{10... | collective-permute-start | bytes 3145736 | tf_op jit(solution)/shard_map/expand_dp/ppermute | solution.py:296
  474.9 11.7 %collective-permute-start.29 = (bf16[256,2048]{1,0:T(8,128)(2,1)}, bf16[256,2048]{1,0:T(8,128)(2,1)}, u32[]{:S(2)}, u32[]{:S(2)}) collective-permute-start(bf16[256,2048]{1,0:T(8,128)(2,1)} %slice.204), channel_id=1, source_target_pairs={{0,1},{1,0},{2,3},{3,2},{4,5},{5,4},{6,7},{7,6},{8,9},{9,8},{10,11... | collective-permute-start | bytes 3145736 | tf_op jit(solution)/shard_map/branch_ring1/ppermute | solution.py:245
  486.5 220.2 %all-reduce.5.cloned.1.call-start = ((), (), s32[]{:S(2)}) async-start(), calls=%async_computation.5 | async-start | bytes 6291456 | tf_op jit(solution)/shard_map/projection_dp/psum | solution.py:594
  489.5 55.5 %collective-permute-start.30 = (bf16[256,2048]{1,0:T(8,128)(2,1)}, bf16[256,2048]{1,0:T(8,128)(2,1)}, u32[]{:S(2)}, u32[]{:S(2)}) collective-permute-start(bf16[256,2048]{1,0:T(8,128)(2,1)} %add_convert_fusion.8), channel_id=1, source_target_pairs={{0,2},{1,3},{2,6},{3,7},{6,4},{7,5},{4,0},{5,1},{8,10},{9,11},{10,... | collective-permute-start | bytes 3145736 | tf_op jit(solution)/shard_map/branch_ring1/ppermute | solution.py:241
  495.8 61.5 %collective-permute-start.35 = (bf16[256,2048]{1,0:T(8,128)(2,1)}, bf16[256,2048]{1,0:T(8,128)(2,1)}, u32[]{:S(2)}, u32[]{:S(2)}) collective-permute-start(bf16[256,2048]{1,0:T(8,128)(2,1)} %add_convert_fusion.10), channel_id=1, source_target_pairs={{0,16},{8,24},{16,0},{24,8},{1,17},{9,25},{17,1},{25,9},{2,18},{10... | collective-permute-start | bytes 3145736 | tf_op jit(solution)/shard_map/contract_dp/ppermute | solution.py:296
  497.4 59.9 %collective-permute-start.36 = (bf16[512,1024]{1,0:T(8,128)(2,1)}, bf16[512,1024]{1,0:T(8,128)(2,1)}, u32[]{:S(2)}, u32[]{:S(2)}) collective-permute-start(bf16[512,1024]{1,0:T(8,128)(2,1)} %add_convert_fusion.9), channel_id=1, source_target_pairs={{0,8},{8,0},{16,24},{24,16},{1,9},{9,1},{17,25},{25,17},{2,10},{10... | collective-permute-start | bytes 3145736 | tf_op jit(solution)/shard_map/expand_dp/ppermute | solution.py:296
  499.9 140.0 %collective-permute-start.28 = (bf16[256,2048]{1,0:T(8,128)(2,1)}, bf16[256,2048]{1,0:T(8,128)(2,1)}, u32[]{:S(2)}, u32[]{:S(2)}) collective-permute-start(bf16[256,2048]{1,0:T(8,128)(2,1)} %slice.202), channel_id=1, source_target_pairs={{0,1},{1,0},{2,3},{3,2},{4,5},{5,4},{6,7},{7,6},{8,9},{9,8},{10,11... | collective-permute-start | bytes 3145736 | tf_op jit(solution)/shard_map/branch_ring2/ppermute | solution.py:245
  552.7 28.7 %collective-permute-start.32 = (bf16[256,2048]{1,0:T(8,128)(2,1)S(1)}, bf16[256,2048]{1,0:T(8,128)(2,1)S(1)}, u32[]{:S(2)}, u32[]{:S(2)}) collective-permute-start(bf16[256,2048]{1,0:T(8,128)(2,1)S(1)} %constant_dynamic-slice_fusion.5), channel_id=1, source_target_pairs={{0,1},{1,0},{2,3},{3,2},{4,5},{5,4},{6,7},{7,6},{8,9},{9,8},{10,11... | collective-permute-start | bytes 3145736 | tf_op jit(solution)/shard_map/ppermute | solution.py:245
  553.7 26.3 %collective-permute-start.34 = (bf16[256,2048]{1,0:T(8,128)(2,1)S(1)}, bf16[256,2048]{1,0:T(8,128)(2,1)S(1)}, u32[]{:S(2)}, u32[]{:S(2)}) collective-permute-start(bf16[256,2048]{1,0:T(8,128)(2,1)S(1)} %add_convert_fusion.7), channel_id=1, source_target_pairs={{0,2},{1,3},{2,6},{3,7},{6,4},{7,5},{4,0},{5,1},{8,10},{9,11},{10,... | collective-permute-start | bytes 3145736 | tf_op jit(solution)/shard_map/grad_normed_ring1/ppermute | solution.py:241
  557.4 49.5 %collective-permute-start.31 = (bf16[256,2048]{1,0:T(8,128)(2,1)S(1)}, bf16[256,2048]{1,0:T(8,128)(2,1)S(1)}, u32[]{:S(2)}, u32[]{:S(2)}) collective-permute-start(bf16[256,2048]{1,0:T(8,128)(2,1)S(1)} %constant_dynamic-slice_fusion.4), channel_id=1, source_target_pairs={{0,1},{1,0},{2,3},{3,2},{4,5},{5,4},{6,7},{7,6},{8,9},{9,8},{10,11... | collective-permute-start | bytes 3145736 | tf_op jit(solution)/shard_map/ppermute | solution.py:245
  560.7 54.0 %collective-permute-start.47 = (bf16[1024,1024]{1,0:T(8,128)(2,1)}, bf16[1024,1024]{1,0:T(8,128)(2,1)}, u32[]{:S(2)}, u32[]{:S(2)}) collective-permute-start(bf16[1024,1024]{1,0:T(8,128)(2,1)} %pad_maximum_fusion.1), channel_id=1, source_target_pairs={{0,16},{8,24},{16,0},{24,8},{1,17},{9,25},{17,1},{25,9},{2,18},{10... | collective-permute-start | bytes 6291464 | tf_op jit(solution)/shard_map/expand_dp/ppermute | solution.py:296
  580.0 53.6 %collective-permute-start.48 = (bf16[512,2048]{1,0:T(8,128)(2,1)}, bf16[512,2048]{1,0:T(8,128)(2,1)}, u32[]{:S(2)}, u32[]{:S(2)}) collective-permute-start(bf16[512,2048]{1,0:T(8,128)(2,1)} %pad_maximum_fusion.2), channel_id=1, source_target_pairs={{0,8},{8,0},{16,24},{24,16},{1,9},{9,1},{17,25},{25,17},{2,10},{10... | collective-permute-start | bytes 6291464 | tf_op jit(solution)/shard_map/contract_dp/ppermute | solution.py:296
  582.0 24.9 %collective-permute-start.37 = (bf16[256,2048]{1,0:T(8,128)(2,1)S(1)}, bf16[256,2048]{1,0:T(8,128)(2,1)S(1)}, u32[]{:S(2)}, u32[]{:S(2)}) collective-permute-start(bf16[256,2048]{1,0:T(8,128)(2,1)S(1)} %add_convert_fusion.6), channel_id=1, source_target_pairs={{0,2},{1,3},{2,6},{3,7},{6,4},{7,5},{4,0},{5,1},{8,10},{9,11},{10,... | collective-permute-start | bytes 3145736 | tf_op jit(solution)/shard_map/grad_normed_ring2/ppermute | solution.py:241
  606.9 73.6 %collective-permute-start.27 = (bf16[256,2048]{1,0:T(8,128)(2,1)}, bf16[256,2048]{1,0:T(8,128)(2,1)}, u32[]{:S(2)}, u32[]{:S(2)}) collective-permute-start(bf16[256,2048]{1,0:T(8,128)(2,1)} %slice.200), channel_id=1, source_target_pairs={{0,1},{1,0},{2,3},{3,2},{4,5},{5,4},{6,7},{7,6},{8,9},{9,8},{10,11... | collective-permute-start | bytes 3145736 | tf_op jit(solution)/shard_map/branch_ring3/ppermute | solution.py:245
  608.4 31.5 %collective-permute-start.38 = (bf16[256,2048]{1,0:T(8,128)(2,1)}, bf16[256,2048]{1,0:T(8,128)(2,1)}, u32[]{:S(2)}, u32[]{:S(2)}) collective-permute-start(bf16[256,2048]{1,0:T(8,128)(2,1)} %add_convert_fusion.5), channel_id=1, source_target_pairs={{0,2},{1,3},{2,6},{3,7},{6,4},{7,5},{4,0},{5,1},{8,10},{9,11},{10,... | collective-permute-start | bytes 3145736 | tf_op jit(solution)/shard_map/grad_normed_ring3/ppermute | solution.py:241
  614.7 97.4 %collective-permute-start.26 = (bf16[256,2048]{1,0:T(8,128)(2,1)}, bf16[256,2048]{1,0:T(8,128)(2,1)}, u32[]{:S(2)}, u32[]{:S(2)}) collective-permute-start(bf16[256,2048]{1,0:T(8,128)(2,1)} %slice.198), channel_id=1, source_target_pairs={{0,1},{1,0},{2,3},{3,2},{4,5},{5,4},{6,7},{7,6},{8,9},{9,8},{10,11... | collective-permute-start | bytes 3145736 | tf_op jit(solution)/shard_map/branch_own/ppermute | solution.py:245
  633.5 9.8 %collective-permute-start.41 = (bf16[256,2048]{1,0:T(8,128)(2,1)}, bf16[256,2048]{1,0:T(8,128)(2,1)S(1)}, u32[]{:S(2)}, u32[]{:S(2)}) collective-permute-start(bf16[256,2048]{1,0:T(8,128)(2,1)} %constant_dynamic-slice_fusion.8), channel_id=1, source_target_pairs={{0,1},{1,0},{2,3},{3,2},{4,5},{5,4},{6,7},{7,6},{8,9},{9,8},{10,11... | collective-permute-start | bytes 3145736 | tf_op jit(solution)/shard_map/grad_normed_own/ppermute | solution.py:245
  643.1 37.3 %collective-permute-start.39 = (bf16[256,2048]{1,0:T(8,128)(2,1)}, bf16[256,2048]{1,0:T(8,128)(2,1)}, u32[]{:S(2)}, u32[]{:S(2)}) collective-permute-start(bf16[256,2048]{1,0:T(8,128)(2,1)} %add_convert_fusion.4), channel_id=1, source_target_pairs={{0,2},{1,3},{2,6},{3,7},{6,4},{7,5},{4,0},{5,1},{8,10},{9,11},{10,... | collective-permute-start | bytes 3145736 | tf_op jit(solution)/shard_map/branch_ring2/ppermute | solution.py:241
  647.3 10.4 %collective-permute-start.42 = (f32[6,2048]{1,0:T(8,128)S(1)}, f32[6,2048]{1,0:T(8,128)S(1)}, u32[]{:S(2)}, u32[]{:S(2)}) collective-permute-start(f32[6,2048]{1,0:T(8,128)S(1)} %broadcast_multiply_fusion), channel_id=1, source_target_pairs={{0,1},{1,0},{2,3},{3,2},{4,5},{5,4},{6,7},{7,6},{8,9},{9,8},{10,11... | collective-permute-start | bytes 147464 | tf_op jit(solution)/shard_map/small_sums/ppermute | solution.py:359
  657.8 13.6 %collective-permute-start.43 = (f32[6,2048]{1,0:T(8,128)S(1)}, f32[6,2048]{1,0:T(8,128)S(1)}, u32[]{:S(2)}, u32[]{:S(2)}) collective-permute-start(f32[6,2048]{1,0:T(8,128)S(1)} %fusion.185), channel_id=1, source_target_pairs={{0,2},{1,3},{2,0},{3,1},{4,6},{5,7},{6,4},{7,5},{8,10},{9,11},{10,... | collective-permute-start | bytes 147464 | tf_op jit(solution)/shard_map/small_sums/ppermute | solution.py:359
  677.9 7.6 %collective-permute-start.45 = (f32[3072]{0:T(1024)S(1)}, f32[3072]{0:T(1024)S(1)}, u32[]{:S(2)}, u32[]{:S(2)}) collective-permute-start(f32[3072]{0:T(1024)S(1)} %pad_maximum_fusion.6), channel_id=1, source_target_pairs={{0,8},{8,0},{16,24},{24,16},{1,9},{9,1},{17,25},{25,17},{2,10},{10... | collective-permute-start | bytes 36872 | tf_op jit(solution)/shard_map/small_sums/ppermute | solution.py:359
  683.9 28.2 %collective-permute-start.40 = (bf16[256,2048]{1,0:T(8,128)(2,1)}, bf16[256,2048]{1,0:T(8,128)(2,1)}, u32[]{:S(2)}, u32[]{:S(2)}) collective-permute-start(bf16[256,2048]{1,0:T(8,128)(2,1)} %add_convert_fusion.3), channel_id=1, source_target_pairs={{0,2},{1,3},{2,6},{3,7},{6,4},{7,5},{4,0},{5,1},{8,10},{9,11},{10,... | collective-permute-start | bytes 3145736 | tf_op jit(solution)/shard_map/branch_ring3/ppermute | solution.py:241
  (80 other events, 592.2 us)
Sparse Core Ops, SparseCore 0:
  12.1 100.8 all-gather.3
  114.6 109.1 all-gather.5
  387.5 80.4 all-gather.7
  486.6 55.3 all-reduce.2
  614.8 91.8 all-reduce.4

commit v3 on v2

--- a/solution.py
+++ b/solution.py
@@ -300,41 +300,72 @@
     return [1 << i for i in range((lax.axis_size("dp") - 1).bit_length())]
 
 
-def tied(ties):
-    left = list(ties)
-
-    def tie(value):
-        return after(value, *left.pop(0)) if left else value
-
-    return tie
-
-
-def dp_halves(value, bits, axis, ties):
-    tie = tied(ties)
+def sum_job(value, bits, axis=0):
     me = lax.axis_index("dp")
-    stages = [value]
     for bit in bits:
         half = value.shape[axis] // 2
         up = (me & bit) != 0
         keep = lax.dynamic_slice_in_dim(value, jnp.where(up, half, 0), half, axis)
         give = lax.dynamic_slice_in_dim(value, jnp.where(up, 0, half), half, axis)
-        got = tie(flip_dp(give, bit))
+        (got,) = yield [(give, bit)]
         value = (keep.astype(jnp.float32) + got.astype(jnp.float32)).astype(value.dtype)
-        stages.append(value)
-    return stages
+    blocks = [(0, value)]
+    wave = [(0, value, bits[::-1])]
+    while wave:
+        sends = [
+            (mask ^ bit, block, bit, left[place + 1 :])
+            for mask, block, left in wave
+            for place, bit in enumerate(left)
+        ]
+        if not sends:
+            break
+        got = yield [(block, bit) for _, block, bit, _ in sends]
+        wave = [(mask, block, left) for (mask, _, _, left), block in zip(sends, got)]
+        blocks += [(mask, block) for mask, block, _ in wave]
+    return blocks
+
+
+class Exchange:
+    def __init__(self):
+        self.jobs = {}
+        self.done = {}
+        self.flying = {}
+
+    def add(self, name, job):
+        self.jobs[name] = job
+        self._advance(name, None)
+
+    def _advance(self, name, got):
+        try:
+            sends = self.jobs[name].send(got)
+        except StopIteration as stop:
+            self.done[name] = stop.value
+            del self.jobs[name]
+            return
+        with jax.named_scope("dp_" + name):
+            self.flying[name] = [flip_dp(value, bit) for value, bit in sends]
+
+    def hop(self, *ties):
+        names = list(self.flying)
+        flat = [value for name in names for value in self.flying[name]]
+        flat = lax.optimization_barrier(tuple(flat) + ties)
+        place = 0
+        for name in names:
+            count = len(self.flying.pop(name))
+            self._advance(name, list(flat[place : place + count]))
+            place += count
+        return flat[place:] if len(ties) != 1 else flat[-1]
 
 
 def dp_blocks(value, bits, ties):
-    tie = tied(ties)
-    blocks = [(0, value)]
-    first = None
+    blocks = [(0, value, 0)]
     for bit in bits:
-        got = tie(flip_dp(jnp.concatenate([block for _, block in blocks], axis=0), bit))
-        first = got if first is None else first
-        blocks += [
-            (mask ^ bit, piece) for (mask, _), piece in zip(blocks, jnp.split(got, len(blocks)))
-        ]
-    return blocks, first
+        for mask, block, hops in list(blocks):
+            got = flip_dp(block, bit)
+            if hops < len(ties):
+                got = after(got, *ties[hops])
+            blocks.append((mask ^ bit, got, hops + 1))
+    return [(mask, block) for mask, block, _ in blocks]
 
 
 def cut_place(mask, bits, size):
@@ -346,9 +377,8 @@
     return place
 
 
-def put(full, block, rows, column=0):
-    block = block.astype(full.dtype).reshape(block.shape[:1] + full.shape[1:2] + (-1,)) if full.ndim == 3 else block.astype(full.dtype)
-    return lax.dynamic_update_slice(full, block, (rows, column) + (0,) * (full.ndim - 2))
+def put(full, block, row, column=0):
+    return lax.dynamic_update_slice(full, block.astype(full.dtype), (row, column))
 
 
 def small_sum(value, axes):
@@ -435,7 +465,7 @@
     weight_own = jnp.zeros((2 * half, features), bf16)
     with jax.named_scope("weight_dp"):
         for start, order in ((0, bits), (half, bits[::-1])):
-            for mask, block in dp_blocks(pieces[start : start + half], order, [])[0]:
+            for mask, block in dp_blocks(pieces[start : start + half], order, []):
                 weight_own = put(weight_own, block, start, (group ^ mask) * columns)
     weight_other = swap_cores(weight_own)
 
@@ -521,106 +551,56 @@
     with jax.named_scope("grad_hidden_gather"):
         grad_hidden_all = lax.all_gather(grad_hidden_low, "tensor", axis=0, tiled=True)
 
-    with jax.named_scope("contract_dp"):
-        contract_half = dp_halves(contract_local, bits[:1], 0, [(grad_hidden_low,)])[-1]
-        contract_cut = dp_halves(contract_half, bits[1:], 0, [(grad_hidden_all,)])[-1]
-    with jax.named_scope("expand_dp"):
-        expand_half = dp_halves(expand_local, bits[::-1][:1], 0, [(grad_hidden_low,)])[-1]
-        expand_cut = dp_halves(expand_half, bits[::-1][1:], 0, [(grad_hidden_all,)])[-1]
-    grad_hidden_all = after(grad_hidden_all, contract_cut, expand_cut)
-    with jax.named_scope("grad_context"):
-        grad_context = dot(grad_hidden_all, output_weight, 1, 1).astype(bf16)
-
+    exchange = Exchange()
+    exchange.add("contract", sum_job(contract_local, bits))
+    exchange.add("expand", sum_job(expand_local, bits[::-1]))
     branch_terms = [
         dot(after(block, grad_hidden_low), contract_weight, 1, 0).astype(bf16) for block in activated
     ]
-
-    def branch_part(step):
-        block = after(branch_terms[step], grad_hidden_all)
-        return block[:shard_rows], block[shard_rows:]
-
-    def branch_total(step):
-        mine, other = branch_part(step)
-        return mine.astype(f32) + swap_cores(other).astype(f32)
-
+    branch_totals = [
+        block[:shard_rows].astype(f32) + swap_cores(block[shard_rows:]).astype(f32)
+        for block in branch_terms
+    ]
+    branch_sent = branch_totals[1].astype(bf16)
+    grad_hidden_low = exchange.hop(grad_hidden_low)
+    for _ in bits[1:]:
+        grad_hidden_low = exchange.hop(grad_hidden_low, *branch_terms, branch_sent)[0]
+    grad_hidden_all, branch_sent = lax.optimization_barrier(
+        (after(grad_hidden_all, grad_hidden_low), branch_sent)
+    )
     with jax.named_scope("branch_ring1"):
-        branch_arrived = ring_step(branch_total(1).astype(bf16))
-
-    with jax.named_scope("output_gradient"):
-        output_local = (share * dot(context, grad_hidden_all, 0, 0)).astype(bf16)
-    with jax.named_scope("output_dp"):
-        output_gradient = lax.psum(output_local, "dp")
+        branch_arrived = ring_step(branch_sent)
+    with jax.named_scope("grad_context"):
+        grad_context = dot(grad_hidden_all, output_weight, 1, 1).astype(bf16)
+
+    def branch_step(step):
+        with jax.named_scope(f"branch_ring{step}"):
+            total = branch_totals[step] + branch_arrived.astype(f32)
+            return ring_step(total.astype(bf16))
+
     projected_grad = attend_back(own_bounds, projected, grad_context, context, totals, local_heads)
     projected_grad, branch_arrived = lax.optimization_barrier((projected_grad, branch_arrived))
-
-    normed_terms = []
+    branch_arrived = branch_step(2)
     with jax.named_scope("normed_terms"):
-        for step in range(chips):
-            rows = lax.dynamic_slice_in_dim(
-                projected_grad, ring_chip(step) * 2 * shard_rows, 2 * shard_rows
-            )
-            normed_terms.append(dot(rows, weight_flat, 1, 1).astype(bf16))
-    projected_late = after(projected_grad, *normed_terms)
+        normed_terms = dot(projected_grad, weight_flat, 1, 1).astype(bf16)
+    normed_terms, branch_arrived = exchange.hop(normed_terms, branch_arrived)
+    projected_late = after(projected_grad, normed_terms)
+    with jax.named_scope("grad_normed_scatter"):
+        grad_normed = lax.psum_scatter(
+            normed_terms, "tensor", scatter_dimension=0, tiled=True
+        ).astype(f32)
+
     with jax.named_scope("projection_gradient"):
         projection_local = (share * dot(normed, projected_late, 0, 0)).astype(bf16)
-
-    def normed_total(step):
-        mine = lax.dynamic_slice_in_dim(normed_terms[step], core * shard_rows, shard_rows)
-        other = lax.dynamic_slice_in_dim(normed_terms[step], (1 - core) * shard_rows, shard_rows)
-        return mine.astype(f32) + swap_cores(other).astype(f32)
-
-
-    normed_arrivals = []
-
-    def normed_step(step, *meanwhile):
-        total = normed_total(step)
-        if normed_arrivals:
-            total = total + after(normed_arrivals[-1], *meanwhile).astype(f32)
-        with jax.named_scope(f"grad_normed_ring{step}"):
-            normed_arrivals.append(ring_step(total.astype(bf16)))
-
-    with jax.named_scope("contract_dp"):
-        contract_blocks, contract_first = dp_blocks(
-            contract_cut, bits[::-1], [(projected_late,), (projected_late,)]
-        )
-    with jax.named_scope("expand_dp"):
-        expand_blocks, expand_first = dp_blocks(
-            expand_cut, bits, [(projected_late,), (projected_late,)]
-        )
-    for step in range(1, chips):
-        normed_step(step, *((contract_first, expand_first) if step == 2 else ()))
-    last = normed_arrivals[-1]
-    with jax.named_scope("projection_dp"):
-        projection_gradient = lax.psum(
-            after(projection_local, normed_arrivals[0], output_gradient), "dp"
-        )
-    projection_gradient = projection_gradient.reshape(features, 3, local_width).astype(f32)
-    output_gradient = output_gradient.astype(f32)
-    with jax.named_scope("grad_normed_own"):
-        grad_normed = normed_total(0) + last.astype(f32)
-
-    branch_arrived = after(branch_arrived, last)
-    for step in range(2, chips):
-        with jax.named_scope(f"branch_ring{step}"):
-            total = branch_total(step) + branch_arrived.astype(f32)
-            branch_arrived = ring_step(total.astype(bf16))
-    with jax.named_scope("branch_own"):
-        branch = branch_total(0) + branch_arrived.astype(f32)
-    layer_output = (local_live * (hidden + branch + contract_bias)).astype(bf16)
-    input_gradient = (
-        grad_hidden + normalize_back(grad_normed, attention_gain, unit_one, inverse_one)
-    ).astype(bf16)
-
-    contract_gradient = jnp.zeros(contract_local.shape, f32)
-    for mask, block in contract_blocks:
-        contract_gradient = put(
-            contract_gradient, after(block, last), cut_place(mask, bits, contract_local.shape[0])
-        )
-    expand_gradient = jnp.zeros(expand_local.shape, f32)
-    for mask, block in expand_blocks:
-        expand_gradient = put(
-            expand_gradient, after(block, last), cut_place(mask, bits[::-1], expand_local.shape[0])
-        )
+    with jax.named_scope("output_gradient"):
+        output_local = (share * dot(context, after(grad_hidden_all, normed_terms), 0, 0)).astype(
+            bf16
+        )
+    cut = projection_local.shape[0] // 2
+    projection_orders = ((0, bits), (cut, bits[::-1]))
+    for start, order in projection_orders:
+        exchange.add(f"projection{start}", sum_job(projection_local[start : start + cut], order))
+    exchange.add("output", sum_job(output_local, bits))
     sums_by_row = share * jnp.stack(
         [
             jnp.sum(grad_normed * unit_one, axis=0),
@@ -640,12 +620,55 @@
         ]
     )
     own_columns = features // tensor_size
+    for _ in bits[1:]:
+        exchange.hop()
+    branch_arrived = exchange.hop(branch_arrived)
+    sums_by_row, branch_arrived = lax.optimization_barrier((sums_by_row, branch_arrived))
+    for step in range(3, chips):
+        branch_arrived = branch_step(step)
+    branch = branch_totals[0] + branch_arrived.astype(f32)
+    layer_output = (local_live * (hidden + branch + contract_bias)).astype(bf16)
+    exchange.hop()
+    while exchange.flying:
+        sums_by_row = exchange.hop(sums_by_row)
     with jax.named_scope("small_sums"):
-        sums_by_row = small_sum(sums_by_row, ("tensor",))
+        sums = small_sum(jnp.concatenate([sums_by_row.reshape(-1), sums_by_width]), ("dp",))
+        sums_by_width = sums[sums_by_row.size :]
+        sums_by_row = small_sum(
+            sums[: sums_by_row.size].reshape(sums_by_row.shape), ("tensor",)
+        )
         sums_by_row = lax.dynamic_slice_in_dim(sums_by_row, rank * own_columns, own_columns, 1)
-        sums = small_sum(jnp.concatenate([sums_by_row.reshape(-1), sums_by_width]), ("dp",))
-    sums_by_row = sums[: 6 * own_columns].reshape(6, own_columns)
-    sums_by_width = sums[6 * own_columns :]
+    projection_parts = [
+        (start, order, exchange.done[f"projection{start}"]) for start, order in projection_orders
+    ]
+    zero = after(jnp.zeros((), f32), normed_terms)
+    input_gradient = (
+        grad_hidden + normalize_back(grad_normed, attention_gain, unit_one, inverse_one)
+    ).astype(bf16)
+
+    contract_gradient = jnp.broadcast_to(zero, contract_local.shape)
+    for mask, block in exchange.done["contract"]:
+        contract_gradient = put(
+            contract_gradient, block, cut_place(mask, bits, contract_local.shape[0])
+        )
+    expand_gradient = jnp.broadcast_to(zero, expand_local.shape)
+    for mask, block in exchange.done["expand"]:
+        expand_gradient = put(
+            expand_gradient, block, cut_place(mask, bits[::-1], expand_local.shape[0])
+        )
+    projection_gradient = jnp.broadcast_to(zero.astype(bf16), projection_local.shape)
+    for start, order, blocks in projection_parts:
+        for mask, block in blocks:
+            projection_gradient = put(
+                projection_gradient, block, start + cut_place(mask, order, cut)
+            )
+    projection_gradient = projection_gradient.reshape(features, 3, local_width).astype(f32)
+    output_gradient = jnp.broadcast_to(zero, output_local.shape)
+    for mask, block in exchange.done["output"]:
+        output_gradient = put(
+            output_gradient, block, cut_place(mask, bits, output_local.shape[0])
+        )
+
     query_value_gradient = sums_by_width[: 2 * local_width].reshape(2, local_width)
     expand_bias_gradient = sums_by_width[2 * local_width :]
     return (

time: 732 us -> 713 us (0.974)
  waiting for transfers between devices: 316 us -> 269 us
  starting transfers between devices: 51 us -> 68.4 us
  other arithmetic: 75.9 us -> 84.6 us
    psum x2 -> x0, waiting for transfers between devices: 32.4 us -> none  [the longest x1 16.7 us: shards(): output_gradient = lax.psum(output_local, 'dp')]
    ppermute x15 -> x12, waiting for transfers between devices: 127 us -> 99.5 us  [ring_step(): return lax.ppermute(value, 'tensor', pairs)]
    ppermute x12 -> x31, starting transfers between devices: 17.3 us -> 35.3 us  [flip_dp(): return lax.ppermute(value, 'dp', [(i, i ^ bit) for i in range(size)])]
    dynamic_update_slice x8 -> x13, other arithmetic: 12.2 us -> 26 us  [put(): lax.dynamic_update_slice(full, block.astype(full.dtype), (row, column))]
    ppermute x12 -> x31, waiting for transfers between devices: 91.1 us -> 104 us  [flip_dp(): return lax.ppermute(value, 'dp', [(i, i ^ bit) for i in range(size)])]
    dynamic_update_slice x7 -> x14, local copies, waits for them, and re-layouts: 9.96 us -> 18.6 us  [put(): lax.dynamic_update_slice(full, block.astype(full.dtype), (row, column))]
    concatenate x4 -> x0, other arithmetic: 8.38 us -> none  [dp_blocks(): jnp.concatenate([block for _, block in blocks], axis=0)]
    dot_general x28 -> x25, matrix products: 142 us -> 139 us  [dot(): lax.dot_general(a, b, (((a_axis,), (b_axis,)), ((), ())), preferred_eleme...]
  transfers between devices with their start and end apart: 55 -> 66, of which waited for: 25 -> 28; matrix products, arithmetic and copies ran while one was open for 37% -> 40% of each run, Pallas kernels for 5% -> 5%
where the time goes in v3:
time: 713 us; the launch traced here: 704 us
  waiting for transfers between devices  269 us (38%)
  matrix products  139 us (19%)
  other arithmetic  84.6 us (12%)
  local copies, waits for them, and re-layouts  79.8 us (11%)
  starting transfers between devices  68.4 us (10%)
  Pallas kernels  38.2 us (5%)
  between operations  25 us (4%)
    dot_general x25, matrix products, dot(): lax.dot_general(a, b, (((a_axis,), (b_axis,)), ((), ())), preferred_eleme...  139 us
    ppermute x31, waiting for transfers between devices, flip_dp(): return lax.ppermute(value, 'dp', [(i, i ^ bit) for i in range(size)])  104 us
    ppermute x12, waiting for transfers between devices, ring_step(): return lax.ppermute(value, 'tensor', pairs)  99.5 us
    all_to_all x1, waiting for transfers between devices, shards(): lax.all_to_all(context.reshape(tensor_size, shard_rows, local_width), 'te...  45.1 us
    ppermute x31, starting transfers between devices, flip_dp(): return lax.ppermute(value, 'dp', [(i, i ^ bit) for i in range(size)])  35.3 us
    dynamic_update_slice x13, other arithmetic, put(): lax.dynamic_update_slice(full, block.astype(full.dtype), (row, column))  26 us
    pallas_call x1, Pallas kernels, attend_back(): pl.pallas_call(functools.partial(attend_back_kernel, block, local_heads),...  21.8 us
    dynamic_update_slice x14, local copies, waits for them, and re-layouts, put(): lax.dynamic_update_slice(full, block.astype(full.dtype), (row, column))  18.6 us
  transfers between devices with their start and end apart: 66, of which 28 were waited for; matrix products, arithmetic and copies ran while one was open for 40% of the time, Pallas kernels for 5%

profile of v3, /device:TPU:0, one launch (start us, length us, event | category | flops | bytes accessed | tf_op | source)
XLA Modules:
  0.0 704.2 jit_solution(17597624028693322563)
XLA Ops:
  15.7 7.3 %collective-permute-done = bf16[256,512]{1,0:T(8,128)(2,1)S(1)} collective-permute-done((bf16[256,512]{1,0:T(8,128)(2,1)S(1)}, bf16[256,512]{1,0:T(8,128)(2,1)S(1)}, u32[]{:S(2)}, u32[]{:S(2)}) %collective-permute-start) | collective-permute-done | bytes 262176 | tf_op jit(solution)/shard_map/weight_ring/ppermute | solution.py:241
  28.8 14.2 %collective-permute-done.4 = bf16[256,512]{1,0:T(8,128)(2,1)S(1)} collective-permute-done((bf16[256,512]{1,0:T(8,128)(2,1)S(1)}, bf16[256,512]{1,0:T(8,128)(2,1)S(1)}, u32[]{:S(2)}, u32[]{:S(2)}) %collective-permute-start.4) | collective-permute-done | bytes 262176 | tf_op jit(solution)/shard_map/weight_ring/ppermute | solution.py:241
  46.2 17.1 %collective-permute-done.5 = bf16[256,512]{1,0:T(8,128)(2,1)S(1)} collective-permute-done((bf16[256,512]{1,0:T(8,128)(2,1)S(1)}, bf16[256,512]{1,0:T(8,128)(2,1)S(1)}, u32[]{:S(2)}, u32[]{:S(2)}) %collective-permute-start.5) | collective-permute-done | bytes 262176 | tf_op jit(solution)/shard_map/weight_ring/ppermute | solution.py:241
  67.2 11.1 %collective-permute-done.6 = bf16[512,512]{1,0:T(8,128)(2,1)S(1)} collective-permute-done((bf16[512,512]{1,0:T(8,128)(2,1)S(1)}, bf16[512,512]{1,0:T(8,128)(2,1)S(1)}, u32[]{:S(2)}, u32[]{:S(2)}) %collective-permute-start.6) | collective-permute-done | bytes 524320 | tf_op jit(solution)/shard_map/weight_dp/ppermute | solution.py:296
  78.2 9.9 %collective-permute-done.2 = bf16[512,512]{1,0:T(8,128)(2,1)} collective-permute-done((bf16[512,512]{1,0:T(8,128)(2,1)S(1)}, bf16[512,512]{1,0:T(8,128)(2,1)}, u32[]{:S(2)}, u32[]{:S(2)}) %collective-permute-start.2) | collective-permute-done | bytes 524320 | tf_op jit(solution)/shard_map/weight_dp/ppermute | solution.py:296
  90.0 3.7 collective-permute-done.3
  99.7 4.9 copy.77
  107.2 10.1 %add_convert_fusion.q_ref.k_ref.v_ref = bf16[2048,768]{1,0:T(8,128)(2,1)S(1)} fusion(f32[768]{0:T(1024)S(1)} %pad_maximum_fusion.3, bf16[2048,2048]{1,0:T(8,128)(2,1)} %all-gather.4.cloned.1.call-done, bf16[2048,768]{0,1:T(8,128)(2,1)} %bitcast.177), kind=kOutput, calls=%fused_computation.6 | convolution fusion | flops 6445596672 | bytes 14683136 | tf_op jit(solution)/shard_map/dot_general | solution.py:430
  117.3 16.4 %shard_map.686 = (bf16[2048,256]{1,0:T(8,128)(2,1)}, f32[2,1,2048]{2,1,0:T(1,128)S(1)}) custom-call(s32[2]{0:T(128)S(1)} %get-tuple-element.154.bounds_ref, bf16[2048,768]{1,0:T(8,128)(2,1)S(1)} %add_convert_fusion.q_ref.k_ref.v_ref, bf16[2048,768]{1,0:T(8,128)(2,1)S(1)} %add_convert_fusion.q_ref.k_ref.v_ref, ...), custom_call_target="tpu_custom_call" | custom-call | flops 4294967296 | bytes 4194304 | tf_op jit(solution)/shard_map/pallas_call | solution.py:73
  133.7 15.2 %all-to-all-start = ((bf16[8,256,256]{2,1,0:T(8,128)(2,1)}), bf16[8,256,256]{2,1,0:T(8,128)(2,1)S(1)}, u32[]{:S(2)}, u32[]{:S(2)}) async-start(bf16[8,256,256]{2,1,0:T(8,128)(2,1)} %bitcast.4), calls=%async_computation | async-start | bytes 2097152 | tf_op jit(solution)/shard_map/all_to_all | solution.py:485
  158.8 45.1 %all-to-all-done = bf16[8,256,256]{2,1,0:T(8,128)(2,1)S(1)} async-done(((bf16[8,256,256]{2,1,0:T(8,128)(2,1)}), bf16[8,256,256]{2,1,0:T(8,128)(2,1)S(1)}, u32[]{:S(2)}, u32[]{:S(2)}) %all-to-all-start) | async-done | bytes 1048608 | tf_op jit(solution)/shard_map/all_to_all | solution.py:485
  207.6 3.8 fusion.133
  213.5 8.8 %all-gather.6.cloned.1.call-done = bf16[2048,2048]{1,0:T(8,128)(2,1)} async-done(((bf16[256,2048]{1,0:T(8,128)(2,1)}), bf16[2048,2048]{1,0:T(8,128)(2,1)}) %all-gather.6.cloned.1.call-update) | async-done | bytes 8388624 | tf_op jit(solution)/shard_map/all_gather | solution.py:480
  224.3 5.8 constant_dynamic-slice_fusion.17
  231.4 5.0 fusion.47
  244.3 6.4 collective-permute-done.12
  257.0 6.8 fusion.31
  266.3 11.2 %collective-permute-done.13 = bf16[256,2048]{1,0:T(8,128)(2,1)S(1)} collective-permute-done((bf16[256,2048]{1,0:T(8,128)(2,1)S(1)}, bf16[256,2048]{1,0:T(8,128)(2,1)S(1)}, u32[]{:S(2)}, u32[]{:S(2)}) %collective-permute-start.13) | collective-permute-done | bytes 1048608 | tf_op jit(solution)/shard_map/mixed_ring2/ppermute | solution.py:241
  284.0 6.4 fusion.45
  290.5 4.6 convolution_convert_fusion.5
  295.9 8.9 %collective-permute-done.15 = bf16[256,2048]{1,0:T(8,128)(2,1)S(1)} collective-permute-done((bf16[256,2048]{1,0:T(8,128)(2,1)S(1)}, bf16[256,2048]{1,0:T(8,128)(2,1)S(1)}, u32[]{:S(2)}, u32[]{:S(2)}) %collective-permute-start.15) | collective-permute-done | bytes 1048608 | tf_op jit(solution)/shard_map/mixed_ring3/ppermute | solution.py:241
  305.1 21.8 %collective-permute-done.18 = bf16[256,2048]{1,0:T(8,128)(2,1)S(1)} collective-permute-done((bf16[256,2048]{1,0:T(8,128)(2,1)S(1)}, bf16[256,2048]{1,0:T(8,128)(2,1)S(1)}, u32[]{:S(2)}, u32[]{:S(2)}) %collective-permute-start.18) | collective-permute-done | bytes 1048608 | tf_op jit(solution)/shard_map/grad_mixed_ring1/ppermute | solution.py:241
  330.6 8.0 %multiply_convert_fusion.4 = (bf16[512,1024]{1,0:T(8,128)(2,1)}, bf16[512,1024]{1,0:T(8,128)(2,1)S(1)}, bf16[512,1024]{1,0:T(8,128)(2,1)S(1)}, bf16[512,1024]{1,0:T(8,128)(2,1)S(1)}, f32[512,1024]{1,0:T(8,128)S(1)}) fusion(f32[1024]{0:T(1024)S(1)} %copy-done.51, f32[512,1024]{1,0:T(8,128)} %copy-done.53, f32[512,1024]{1,0:T(8,128)} %fusion.63, ...), kind=kOutput, calls=%fused_computation.128 | convolution fusion | flops 2168455168 | bytes 18878464 | tf_op jit(solution)/shard_map/mixed_ring3/dot_general | solution.py:430
  338.6 6.8 fusion.38
  350.7 3.9 collective-permute-done.22
  356.7 10.9 %multiply_convert_fusion.1 = bf16[1024,2048]{1,0:T(8,128)(2,1)} fusion(bf16[2048,1024]{1,0:T(8,128)(2,1)S(1)} %bitcast.176, bf16[2048,2048]{1,0:T(8,128)(2,1)S(1)} %bitcast.174, f32[]{:T(128)S(6)} %div.65), kind=kOutput, calls=%fused_computation.2 | convolution fusion | flops 8594128896 | bytes 16777220 | tf_op jit(solution)/shard_map/contract_gradient/dot_general | solution.py:430
  367.6 10.9 %multiply_convert_fusion = bf16[2048,1024]{1,0:T(8,128)(2,1)} fusion(bf16[2048,2048]{1,0:T(8,128)(2,1)S(1)} %bitcast.175, bf16[2048,1024]{1,0:T(8,128)(2,1)S(1)} %bitcast.171, f32[]{:T(128)S(6)} %div.65), kind=kOutput, calls=%fused_computation.1 | convolution fusion | flops 8594128896 | bytes 16777220 | tf_op jit(solution)/shard_map/expand_gradient/dot_general | solution.py:430
  398.5 5.0 convolution_convert_fusion.1
  412.9 26.9 %collective-permute-done.26 = bf16[512,2048]{1,0:T(8,128)(2,1)} collective-permute-done((bf16[512,2048]{1,0:T(8,128)(2,1)}, bf16[512,2048]{1,0:T(8,128)(2,1)}, u32[]{:S(2)}, u32[]{:S(2)}) %collective-permute-start.26) | collective-permute-done | bytes 2097184 | tf_op jit(solution)/shard_map/dp_contract/ppermute | solution.py:296
  455.1 12.0 %collective-permute-done.29 = bf16[512,1024]{1,0:T(8,128)(2,1)S(1)} collective-permute-done((bf16[512,1024]{1,0:T(8,128)(2,1)S(1)}, bf16[512,1024]{1,0:T(8,128)(2,1)S(1)}, u32[]{:S(2)}, u32[]{:S(2)}) %collective-permute-start.29) | collective-permute-done | bytes 1048608 | tf_op jit(solution)/shard_map/dp_expand/ppermute | solution.py:296
  476.6 5.8 convolution_convert_fusion.9.grad_ref
  482.4 21.8 %shard_map.687 = bf16[2048,768]{1,0:T(8,128)(2,1)S(1)} custom-call(s32[2]{0:T(128)S(1)} %get-tuple-element.154.bounds_ref, bf16[2048,768]{1,0:T(8,128)(2,1)} %copy-done.4, bf16[2048,768]{1,0:T(8,128)(2,1)} %copy-done.4, bf16[2048,768]{1,0:T(8,128)(2,1)} %copy-done.4, bf16[2048,256]{1,0:T(8,128)(2,1)S(1)} %convolution_convert_fusion.9.grad_ref, ...), custom_call_target="tpu_custom_call" | custom-call | flops 10737418240 | bytes 8388608 | tf_op jit(solution)/shard_map/pallas_call | solution.py:174
  504.9 4.2 add_convert_fusion.4
  510.2 8.9 %convolution_convert_fusion = bf16[2048,2048]{1,0:T(8,128)(2,1)} fusion(bf16[2048,768]{1,0:T(8,128)(2,1)S(1)} %shard_map.687, bf16[2048,768]{0,1:T(8,128)(2,1)S(1)} %bitcast.178), kind=kOutput, calls=%fused_computation.3 | convolution fusion | flops 6446645248 | bytes 14680064 | tf_op jit(solution)/shard_map/normed_terms/dot_general | solution.py:430
  519.1 5.4 collective-permute-done.31
  524.5 5.7 collective-permute-done.37
  537.9 7.0 fusion.5
  544.9 4.6 collective-permute-start.42
  549.5 9.6 %multiply_convert_fusion.2 = bf16[2048,768]{0,1:T(8,128)(2,1)S(1)} fusion(bf16[2048,2048]{1,0:T(8,128)(2,1)} %all-gather.4.cloned.1.call-done, bf16[2048,768]{1,0:T(8,128)(2,1)S(1)} %copy-done.3, f32[]{:T(128)S(6)} %div.65), kind=kOutput, calls=%fused_computation.5 | convolution fusion | flops 6445596672 | bytes 14680068 | tf_op jit(solution)/shard_map/projection_gradient/dot_general | solution.py:430
  563.8 4.5 broadcast_in_dim.160
  573.8 4.5 broadcast_in_dim.159
  586.7 10.3 %collective-permute-done.38 = bf16[256,2048]{1,0:T(8,128)(2,1)S(1)} collective-permute-done((bf16[256,2048]{1,0:T(8,128)(2,1)}, bf16[256,2048]{1,0:T(8,128)(2,1)S(1)}, u32[]{:S(2)}, u32[]{:S(2)}) %collective-permute-start.38) | collective-permute-done | bytes 1048608 | tf_op jit(solution)/shard_map/dp_contract/ppermute | solution.py:296
  605.1 9.6 %collective-permute-done.45 = bf16[64,2048]{1,0:T(8,128)(2,1)S(1)} collective-permute-done((bf16[64,2048]{1,0:T(8,128)(2,1)S(1)}, bf16[64,2048]{1,0:T(8,128)(2,1)S(1)}, u32[]{:S(2)}, u32[]{:S(2)}) %collective-permute-start.45) | collective-permute-done | bytes 262176 | tf_op jit(solution)/shard_map/dp_output/ppermute | solution.py:296
  625.9 5.3 collective-permute-done.52
  633.8 3.9 collective-permute-done.51
  661.9 4.1 fusion.15
  678.3 5.7 collective-permute-done.59
  686.5 5.4 copy.78
  (378 shorter events, 224.3 us)
Async XLA Ops:
  7.2 99.9 %all-gather.4.cloned.1.call-start = ((), (), s32[]{:S(2)}) async-start(), calls=%async_computation.2 | async-start | bytes 9437184 | tf_op jit(solution)/shard_map/all_gather | solution.py:452
  12.6 209.8 %all-gather.6.cloned.1.call-start = ((), (), s32[]{:S(2)}) async-start(), calls=%async_computation.3 | async-start | bytes 9437184 | tf_op jit(solution)/shard_map/all_gather | solution.py:480
  23.1 20.0 %collective-permute-start.4 = (bf16[256,512]{1,0:T(8,128)(2,1)S(1)}, bf16[256,512]{1,0:T(8,128)(2,1)S(1)}, u32[]{:S(2)}, u32[]{:S(2)}) collective-permute-start(bf16[256,512]{1,0:T(8,128)(2,1)S(1)} %collective-permute-done), channel_id=1, source_target_pairs={{0,2},{1,3},{2,6},{3,7},{6,4},{7,5},{4,0},{5,1},{8,10},{9,11},{10,... | collective-permute-start | bytes 786440 | tf_op jit(solution)/shard_map/weight_ring/ppermute | solution.py:241
  27.3 38.1 %collective-permute-start.1 = (bf16[512,512]{1,0:T(8,128)(2,1)S(1)}, bf16[512,512]{1,0:T(8,128)(2,1)S(1)}, u32[]{:S(2)}, u32[]{:S(2)}) collective-permute-start(bf16[512,512]{1,0:T(8,128)(2,1)S(1)} %get-tuple-element.174), channel_id=1, source_target_pairs={{0,8},{8,0},{16,24},{24,16},{1,9},{9,1},{17,25},{25,17},{2,10},{10... | collective-permute-start | bytes 1572872 | tf_op jit(solution)/shard_map/weight_dp/ppermute | solution.py:296
  43.0 20.3 %collective-permute-start.5 = (bf16[256,512]{1,0:T(8,128)(2,1)S(1)}, bf16[256,512]{1,0:T(8,128)(2,1)S(1)}, u32[]{:S(2)}, u32[]{:S(2)}) collective-permute-start(bf16[256,512]{1,0:T(8,128)(2,1)S(1)} %collective-permute-done.4), channel_id=1, source_target_pairs={{0,2},{1,3},{2,6},{3,7},{6,4},{7,5},{4,0},{5,1},{8,10},{9,11},{10,... | collective-permute-start | bytes 786440 | tf_op jit(solution)/shard_map/weight_ring/ppermute | solution.py:241
  63.4 24.7 %collective-permute-start.2 = (bf16[512,512]{1,0:T(8,128)(2,1)S(1)}, bf16[512,512]{1,0:T(8,128)(2,1)}, u32[]{:S(2)}, u32[]{:S(2)}) collective-permute-start(bf16[512,512]{1,0:T(8,128)(2,1)S(1)} %get-tuple-element.174), channel_id=1, source_target_pairs={{0,16},{8,24},{16,0},{24,8},{1,17},{9,25},{17,1},{25,9},{2,18},{10... | collective-permute-start | bytes 1572872 | tf_op jit(solution)/shard_map/weight_dp/ppermute | solution.py:296
  65.4 28.3 %collective-permute-start.3 = (bf16[512,512]{1,0:T(8,128)(2,1)S(1)}, bf16[512,512]{1,0:T(8,128)(2,1)}, u32[]{:S(2)}, u32[]{:S(2)}) collective-permute-start(bf16[512,512]{1,0:T(8,128)(2,1)S(1)} %collective-permute-done.1), channel_id=1, source_target_pairs={{0,16},{8,24},{16,0},{24,8},{1,17},{9,25},{17,1},{25,9},{2,18},{10... | collective-permute-start | bytes 1572872 | tf_op jit(solution)/shard_map/weight_dp/ppermute | solution.py:296
  65.5 31.8 %collective-permute-start.7 = (bf16[512,512]{1,0:T(8,128)(2,1)S(1)}, bf16[512,512]{1,0:T(8,128)(2,1)S(1)}, u32[]{:S(2)}, u32[]{:S(2)}) collective-permute-start(bf16[512,512]{1,0:T(8,128)(2,1)S(1)} %constant_dynamic-update-slice_fusion.12), channel_id=1, source_target_pairs={{0,8},{8,0},{16,24},{24,16},{1,9},{9,1},{17,25},{25,17},{2,10},{10... | collective-permute-start | bytes 1572872 | tf_op jit(solution)/shard_map/weight_dp/ppermute | solution.py:296
  78.2 19.9 %collective-permute-start.8 = (bf16[512,512]{1,0:T(8,128)(2,1)S(1)}, bf16[512,512]{1,0:T(8,128)(2,1)S(1)}, u32[]{:S(2)}, u32[]{:S(2)}) collective-permute-start(bf16[512,512]{1,0:T(8,128)(2,1)S(1)} %collective-permute-done.6), channel_id=1, source_target_pairs={{0,8},{8,0},{16,24},{24,16},{1,9},{9,1},{17,25},{25,17},{2,10},{10... | collective-permute-start | bytes 1572872 | tf_op jit(solution)/shard_map/weight_dp/ppermute | solution.py:296
  133.7 70.2 %all-to-all-start = ((bf16[8,256,256]{2,1,0:T(8,128)(2,1)}), bf16[8,256,256]{2,1,0:T(8,128)(2,1)S(1)}, u32[]{:S(2)}, u32[]{:S(2)}) async-start(bf16[8,256,256]{2,1,0:T(8,128)(2,1)} %bitcast.4), calls=%async_computation | async-start | bytes 2097152 | tf_op jit(solution)/shard_map/all_to_all | solution.py:485
  148.9 327.6 %all-gather.8.cloned.1.call-start = ((), (), s32[]{:S(2)}) async-start(), calls=%async_computation.4 | async-start | bytes 9437184 | tf_op jit(solution)/shard_map/grad_hidden_gather/all_gather | solution.py:552
  224.0 26.7 %collective-permute-start.12 = (bf16[256,2048]{1,0:T(8,128)(2,1)}, bf16[256,2048]{1,0:T(8,128)(2,1)S(1)}, u32[]{:S(2)}, u32[]{:S(2)}) collective-permute-start(bf16[256,2048]{1,0:T(8,128)(2,1)} %add_convert_fusion.11), channel_id=1, source_target_pairs={{0,2},{1,3},{2,6},{3,7},{6,4},{7,5},{4,0},{5,1},{8,10},{9,11},{10,... | collective-permute-start | bytes 3145736 | tf_op jit(solution)/shard_map/mixed_ring1/ppermute | solution.py:241
  243.4 138.0 %collective-permute-start.11 = (bf16[256,2048]{1,0:T(8,128)(2,1)}, bf16[256,2048]{1,0:T(8,128)(2,1)}, u32[]{:S(2)}, u32[]{:S(2)}) collective-permute-start(bf16[256,2048]{1,0:T(8,128)(2,1)} %slice.216), channel_id=1, source_target_pairs={{0,1},{1,0},{2,3},{3,2},{4,5},{5,4},{6,7},{7,6},{8,9},{9,8},{10,11... | collective-permute-start | bytes 3145736 | tf_op jit(solution)/shard_map/grad_mixed_own/ppermute | solution.py:245
  250.7 26.8 %collective-permute-start.13 = (bf16[256,2048]{1,0:T(8,128)(2,1)S(1)}, bf16[256,2048]{1,0:T(8,128)(2,1)S(1)}, u32[]{:S(2)}, u32[]{:S(2)}) collective-permute-start(bf16[256,2048]{1,0:T(8,128)(2,1)S(1)} %collective-permute-done.12), channel_id=1, source_target_pairs={{0,2},{1,3},{2,6},{3,7},{6,4},{7,5},{4,0},{5,1},{8,10},{9,11},{10,... | collective-permute-start | bytes 3145736 | tf_op jit(solution)/shard_map/mixed_ring2/ppermute | solution.py:241
  277.5 17.6 %collective-permute-start.17 = (bf16[256,2048]{1,0:T(8,128)(2,1)S(1)}, bf16[256,2048]{1,0:T(8,128)(2,1)S(1)}, u32[]{:S(2)}, u32[]{:S(2)}) collective-permute-start(bf16[256,2048]{1,0:T(8,128)(2,1)S(1)} %slice.218), channel_id=1, source_target_pairs={{0,1},{1,0},{2,3},{3,2},{4,5},{5,4},{6,7},{7,6},{8,9},{9,8},{10,11... | collective-permute-start | bytes 3145736 | tf_op jit(solution)/shard_map/grad_mixed_ring1/ppermute | solution.py:245
  277.5 27.3 %collective-permute-start.15 = (bf16[256,2048]{1,0:T(8,128)(2,1)S(1)}, bf16[256,2048]{1,0:T(8,128)(2,1)S(1)}, u32[]{:S(2)}, u32[]{:S(2)}) collective-permute-start(bf16[256,2048]{1,0:T(8,128)(2,1)S(1)} %collective-permute-done.13), channel_id=1, source_target_pairs={{0,2},{1,3},{2,6},{3,7},{6,4},{7,5},{4,0},{5,1},{8,10},{9,11},{10,... | collective-permute-start | bytes 3145736 | tf_op jit(solution)/shard_map/mixed_ring3/ppermute | solution.py:241
  295.6 31.3 %collective-permute-start.18 = (bf16[256,2048]{1,0:T(8,128)(2,1)S(1)}, bf16[256,2048]{1,0:T(8,128)(2,1)S(1)}, u32[]{:S(2)}, u32[]{:S(2)}) collective-permute-start(bf16[256,2048]{1,0:T(8,128)(2,1)S(1)} %add_convert_fusion.10), channel_id=1, source_target_pairs={{0,2},{1,3},{2,6},{3,7},{6,4},{7,5},{4,0},{5,1},{8,10},{9,11},{10,... | collective-permute-start | bytes 3145736 | tf_op jit(solution)/shard_map/grad_mixed_ring1/ppermute | solution.py:241
  295.7 31.2 %collective-permute-start.21 = (bf16[256,2048]{1,0:T(8,128)(2,1)S(1)}, bf16[256,2048]{1,0:T(8,128)(2,1)S(1)}, u32[]{:S(2)}, u32[]{:S(2)}) collective-permute-start(bf16[256,2048]{1,0:T(8,128)(2,1)S(1)} %slice.222), channel_id=1, source_target_pairs={{0,1},{1,0},{2,3},{3,2},{4,5},{5,4},{6,7},{7,6},{8,9},{9,8},{10,11... | collective-permute-start | bytes 3145736 | tf_op jit(solution)/shard_map/grad_mixed_ring2/ppermute | solution.py:245
  304.8 23.8 %collective-permute-start.16 = (bf16[256,2048]{1,0:T(8,128)(2,1)S(1)}, bf16[256,2048]{1,0:T(8,128)(2,1)S(1)}, u32[]{:S(2)}, u32[]{:S(2)}) collective-permute-start(bf16[256,2048]{1,0:T(8,128)(2,1)S(1)} %collective-permute-done.15), channel_id=1, source_target_pairs={{0,1},{1,0},{2,3},{3,2},{4,5},{5,4},{6,7},{7,6},{8,9},{9,8},{10,11... | collective-permute-start | bytes 3145736 | tf_op jit(solution)/shard_map/mixed_ring3/ppermute | solution.py:245
  328.4 26.2 %collective-permute-start.22 = (bf16[256,2048]{1,0:T(8,128)(2,1)}, bf16[256,2048]{1,0:T(8,128)(2,1)}, u32[]{:S(2)}, u32[]{:S(2)}) collective-permute-start(bf16[256,2048]{1,0:T(8,128)(2,1)} %add_convert_fusion.9), channel_id=1, source_target_pairs={{0,2},{1,3},{2,6},{3,7},{6,4},{7,5},{4,0},{5,1},{8,10},{9,11},{10,... | collective-permute-start | bytes 3145736 | tf_op jit(solution)/shard_map/grad_mixed_ring2/ppermute | solution.py:241
  356.3 25.1 %collective-permute-start.23 = (bf16[256,2048]{1,0:T(8,128)(2,1)S(1)}, bf16[256,2048]{1,0:T(8,128)(2,1)S(1)}, u32[]{:S(2)}, u32[]{:S(2)}) collective-permute-start(bf16[256,2048]{1,0:T(8,128)(2,1)S(1)} %add_convert_fusion.8), channel_id=1, source_target_pairs={{0,2},{1,3},{2,6},{3,7},{6,4},{7,5},{4,0},{5,1},{8,10},{9,11},{10,... | collective-permute-start | bytes 3145736 | tf_op jit(solution)/shard_map/grad_mixed_ring3/ppermute | solution.py:241
  390.2 256.5 %reduce-scatter.2.cloned.1.call-start = ((), (), s32[]{:S(2)}) async-start(), calls=%async_computation.5 | async-start | bytes 9437184 | tf_op jit(solution)/shard_map/grad_normed_scatter/reduce_scatter | solution.py:589
  394.0 45.8 %collective-permute-start.26 = (bf16[512,2048]{1,0:T(8,128)(2,1)}, bf16[512,2048]{1,0:T(8,128)(2,1)}, u32[]{:S(2)}, u32[]{:S(2)}) collective-permute-start(bf16[512,2048]{1,0:T(8,128)(2,1)} %constant_dynamic-slice_fusion.1), channel_id=1, source_target_pairs={{0,8},{8,0},{16,24},{24,16},{1,9},{9,1},{17,25},{25,17},{2,10},{10... | collective-permute-start | bytes 6291464 | tf_op jit(solution)/shard_map/dp_contract/ppermute | solution.py:296
  397.0 45.5 %collective-permute-start.27 = (bf16[1024,1024]{1,0:T(8,128)(2,1)}, bf16[1024,1024]{1,0:T(8,128)(2,1)}, u32[]{:S(2)}, u32[]{:S(2)}) collective-permute-start(bf16[1024,1024]{1,0:T(8,128)(2,1)} %constant_dynamic-slice_fusion.2), channel_id=1, source_target_pairs={{0,16},{8,24},{16,0},{24,8},{1,17},{9,25},{17,1},{25,9},{2,18},{10... | collective-permute-start | bytes 6291464 | tf_op jit(solution)/shard_map/dp_expand/ppermute | solution.py:296
  408.1 45.7 %collective-permute-start.30 = (bf16[256,2048]{1,0:T(8,128)(2,1)S(1)}, bf16[256,2048]{1,0:T(8,128)(2,1)S(1)}, u32[]{:S(2)}, u32[]{:S(2)}) collective-permute-start(bf16[256,2048]{1,0:T(8,128)(2,1)S(1)} %slice.244), channel_id=1, source_target_pairs={{0,1},{1,0},{2,3},{3,2},{4,5},{5,4},{6,7},{7,6},{8,9},{9,8},{10,11... | collective-permute-start | bytes 3145736 | tf_op jit(solution)/shard_map/ppermute | solution.py:245
  408.2 96.7 %collective-permute-start.36 = (bf16[256,2048]{1,0:T(8,128)(2,1)}, bf16[256,2048]{1,0:T(8,128)(2,1)}, u32[]{:S(2)}, u32[]{:S(2)}) collective-permute-start(bf16[256,2048]{1,0:T(8,128)(2,1)} %slice.246), channel_id=1, source_target_pairs={{0,1},{1,0},{2,3},{3,2},{4,5},{5,4},{6,7},{7,6},{8,9},{9,8},{10,11... | collective-permute-start | bytes 3145736 | tf_op jit(solution)/shard_map/ppermute | solution.py:245
  445.4 21.8 %collective-permute-start.29 = (bf16[512,1024]{1,0:T(8,128)(2,1)S(1)}, bf16[512,1024]{1,0:T(8,128)(2,1)S(1)}, u32[]{:S(2)}, u32[]{:S(2)}) collective-permute-start(bf16[512,1024]{1,0:T(8,128)(2,1)S(1)} %constant_dynamic-slice_fusion.4), channel_id=1, source_target_pairs={{0,8},{8,0},{16,24},{24,16},{1,9},{9,1},{17,25},{25,17},{2,10},{10... | collective-permute-start | bytes 3145736 | tf_op jit(solution)/shard_map/dp_expand/ppermute | solution.py:296
  448.5 21.6 %collective-permute-start.28 = (bf16[256,2048]{1,0:T(8,128)(2,1)S(1)}, bf16[256,2048]{1,0:T(8,128)(2,1)S(1)}, u32[]{:S(2)}, u32[]{:S(2)}) collective-permute-start(bf16[256,2048]{1,0:T(8,128)(2,1)S(1)} %constant_dynamic-slice_fusion.3), channel_id=1, source_target_pairs={{0,16},{8,24},{16,0},{24,8},{1,17},{9,25},{17,1},{25,9},{2,18},{10... | collective-permute-start | bytes 3145736 | tf_op jit(solution)/shard_map/dp_contract/ppermute | solution.py:296
  471.6 47.5 %collective-permute-start.34 = (bf16[512,1024]{1,0:T(8,128)(2,1)}, bf16[512,1024]{1,0:T(8,128)(2,1)}, u32[]{:S(2)}, u32[]{:S(2)}) collective-permute-start(bf16[512,1024]{1,0:T(8,128)(2,1)} %add_convert_fusion.5), channel_id=1, source_target_pairs={{0,16},{8,24},{16,0},{24,8},{1,17},{9,25},{17,1},{25,9},{2,18},{10... | collective-permute-start | bytes 3145736 | tf_op jit(solution)/shard_map/dp_expand/ppermute | solution.py:296
  473.1 46.0 %collective-permute-start.33 = (bf16[512,1024]{1,0:T(8,128)(2,1)}, bf16[512,1024]{1,0:T(8,128)(2,1)}, u32[]{:S(2)}, u32[]{:S(2)}) collective-permute-start(bf16[512,1024]{1,0:T(8,128)(2,1)} %add_convert_fusion.5), channel_id=1, source_target_pairs={{0,8},{8,0},{16,24},{24,16},{1,9},{9,1},{17,25},{25,17},{2,10},{10... | collective-permute-start | bytes 3145736 | tf_op jit(solution)/shard_map/dp_expand/ppermute | solution.py:296
  475.9 43.2 %collective-permute-start.32 = (bf16[256,2048]{1,0:T(8,128)(2,1)}, bf16[256,2048]{1,0:T(8,128)(2,1)}, u32[]{:S(2)}, u32[]{:S(2)}) collective-permute-start(bf16[256,2048]{1,0:T(8,128)(2,1)} %add_convert_fusion.6), channel_id=1, source_target_pairs={{0,8},{8,0},{16,24},{24,16},{1,9},{9,1},{17,25},{25,17},{2,10},{10... | collective-permute-start | bytes 3145736 | tf_op jit(solution)/shard_map/dp_contract/ppermute | solution.py:296
  476.5 27.8 %collective-permute-start.35 = (bf16[256,2048]{1,0:T(8,128)(2,1)}, bf16[256,2048]{1,0:T(8,128)(2,1)S(1)}, u32[]{:S(2)}, u32[]{:S(2)}) collective-permute-start(bf16[256,2048]{1,0:T(8,128)(2,1)} %add_convert_fusion.7), channel_id=1, source_target_pairs={{0,2},{1,3},{2,6},{3,7},{6,4},{7,5},{4,0},{5,1},{8,10},{9,11},{10,... | collective-permute-start | bytes 3145736 | tf_op jit(solution)/shard_map/branch_ring1/ppermute | solution.py:241
  504.3 20.2 %collective-permute-start.31 = (bf16[256,2048]{1,0:T(8,128)(2,1)}, bf16[256,2048]{1,0:T(8,128)(2,1)}, u32[]{:S(2)}, u32[]{:S(2)}) collective-permute-start(bf16[256,2048]{1,0:T(8,128)(2,1)} %add_convert_fusion.6), channel_id=1, source_target_pairs={{0,16},{8,24},{16,0},{24,8},{1,17},{9,25},{17,1},{25,9},{2,18},{10... | collective-permute-start | bytes 3145736 | tf_op jit(solution)/shard_map/dp_contract/ppermute | solution.py:296
  509.1 21.1 %collective-permute-start.37 = (bf16[256,2048]{1,0:T(8,128)(2,1)}, bf16[256,2048]{1,0:T(8,128)(2,1)}, u32[]{:S(2)}, u32[]{:S(2)}) collective-permute-start(bf16[256,2048]{1,0:T(8,128)(2,1)} %add_convert_fusion.4), channel_id=1, source_target_pairs={{0,2},{1,3},{2,6},{3,7},{6,4},{7,5},{4,0},{5,1},{8,10},{9,11},{10,... | collective-permute-start | bytes 3145736 | tf_op jit(solution)/shard_map/branch_ring2/ppermute | solution.py:241
  544.9 41.8 %collective-permute-start.42 = (bf16[128,2048]{1,0:T(8,128)(2,1)S(1)}, bf16[128,2048]{1,0:T(8,128)(2,1)S(1)}, u32[]{:S(2)}, u32[]{:S(2)}) collective-permute-start(bf16[128,2048]{1,0:T(8,128)(2,1)S(1)} %constant_dynamic-slice_fusion.7), channel_id=1, source_target_pairs={{0,8},{8,0},{16,24},{24,16},{1,9},{9,1},{17,25},{25,17},{2,10},{10... | collective-permute-start | bytes 1572872 | tf_op jit(solution)/shard_map/dp_output/ppermute | solution.py:296
  559.5 27.2 %collective-permute-start.40 = (bf16[512,768]{0,1:T(8,128)(2,1)S(1)}, bf16[512,768]{0,1:T(8,128)(2,1)S(1)}, u32[]{:S(2)}, u32[]{:S(2)}) collective-permute-start(bf16[512,768]{0,1:T(8,128)(2,1)S(1)} %constant_dynamic-slice_fusion.5), channel_id=1, source_target_pairs={{0,8},{8,0},{16,24},{24,16},{1,9},{9,1},{17,25},{25,17},{2,10},{10... | collective-permute-start | bytes 2359304 | tf_op jit(solution)/shard_map/dp_projection0/ppermute | solution.py:296
  559.7 27.0 %collective-permute-start.41 = (bf16[512,768]{0,1:T(8,128)(2,1)S(1)}, bf16[512,768]{0,1:T(8,128)(2,1)S(1)}, u32[]{:S(2)}, u32[]{:S(2)}) collective-permute-start(bf16[512,768]{0,1:T(8,128)(2,1)S(1)} %constant_dynamic-slice_fusion.6), channel_id=1, source_target_pairs={{0,16},{8,24},{16,0},{24,8},{1,17},{9,25},{17,1},{25,9},{2,18},{10... | collective-permute-start | bytes 2359304 | tf_op jit(solution)/shard_map/dp_projection1024/ppermute | solution.py:296
  561.3 35.7 %collective-permute-start.38 = (bf16[256,2048]{1,0:T(8,128)(2,1)}, bf16[256,2048]{1,0:T(8,128)(2,1)S(1)}, u32[]{:S(2)}, u32[]{:S(2)}) collective-permute-start(bf16[256,2048]{1,0:T(8,128)(2,1)} %collective-permute-done.31), channel_id=1, source_target_pairs={{0,8},{8,0},{16,24},{24,16},{1,9},{9,1},{17,25},{25,17},{2,10},{10... | collective-permute-start | bytes 3145736 | tf_op jit(solution)/shard_map/dp_contract/ppermute | solution.py:296
  563.3 33.7 %collective-permute-start.39 = (bf16[512,1024]{1,0:T(8,128)(2,1)}, bf16[512,1024]{1,0:T(8,128)(2,1)S(1)}, u32[]{:S(2)}, u32[]{:S(2)}) collective-permute-start(bf16[512,1024]{1,0:T(8,128)(2,1)} %collective-permute-done.33), channel_id=1, source_target_pairs={{0,16},{8,24},{16,0},{24,8},{1,17},{9,25},{17,1},{25,9},{2,18},{10... | collective-permute-start | bytes 3145736 | tf_op jit(solution)/shard_map/dp_expand/ppermute | solution.py:296
  597.3 17.4 %collective-permute-start.44 = (bf16[256,768]{0,1:T(8,128)(2,1)S(1)}, bf16[256,768]{0,1:T(8,128)(2,1)S(1)}, u32[]{:S(2)}, u32[]{:S(2)}) collective-permute-start(bf16[256,768]{0,1:T(8,128)(2,1)S(1)} %constant_dynamic-slice_fusion.9), channel_id=1, source_target_pairs={{0,8},{8,0},{16,24},{24,16},{1,9},{9,1},{17,25},{25,17},{2,10},{10... | collective-permute-start | bytes 1179656 | tf_op jit(solution)/shard_map/dp_projection1024/ppermute | solution.py:296
  614.8 22.9 %collective-permute-start.50 = (bf16[256,768]{0,1:T(8,128)(2,1)S(1)}, bf16[256,768]{0,1:T(8,128)(2,1)S(1)}, u32[]{:S(2)}, u32[]{:S(2)}) collective-permute-start(bf16[256,768]{0,1:T(8,128)(2,1)S(1)} %add_convert_fusion.15), channel_id=1, source_target_pairs={{0,16},{8,24},{16,0},{24,8},{1,17},{9,25},{17,1},{25,9},{2,18},{10... | collective-permute-start | bytes 1179656 | tf_op jit(solution)/shard_map/dp_projection1024/ppermute | solution.py:296
  616.4 21.8 %collective-permute-start.49 = (bf16[256,768]{0,1:T(8,128)(2,1)S(1)}, bf16[256,768]{0,1:T(8,128)(2,1)}, u32[]{:S(2)}, u32[]{:S(2)}) collective-permute-start(bf16[256,768]{0,1:T(8,128)(2,1)S(1)} %add_convert_fusion.15), channel_id=1, source_target_pairs={{0,8},{8,0},{16,24},{24,16},{1,9},{9,1},{17,25},{25,17},{2,10},{10... | collective-permute-start | bytes 1179656 | tf_op jit(solution)/shard_map/dp_projection1024/ppermute | solution.py:296
  619.4 19.0 %collective-permute-start.48 = (bf16[256,768]{0,1:T(8,128)(2,1)S(1)}, bf16[256,768]{0,1:T(8,128)(2,1)S(1)}, u32[]{:S(2)}, u32[]{:S(2)}) collective-permute-start(bf16[256,768]{0,1:T(8,128)(2,1)S(1)} %get-tuple-element.149), channel_id=1, source_target_pairs={{0,8},{8,0},{16,24},{24,16},{1,9},{9,1},{17,25},{25,17},{2,10},{10... | collective-permute-start | bytes 1179656 | tf_op jit(solution)/shard_map/dp_projection0/ppermute | solution.py:296
  621.4 17.0 %collective-permute-start.47 = (bf16[256,768]{0,1:T(8,128)(2,1)S(1)}, bf16[256,768]{0,1:T(8,128)(2,1)}, u32[]{:S(2)}, u32[]{:S(2)}) collective-permute-start(bf16[256,768]{0,1:T(8,128)(2,1)S(1)} %get-tuple-element.149), channel_id=1, source_target_pairs={{0,16},{8,24},{16,0},{24,8},{1,17},{9,25},{17,1},{25,9},{2,18},{10... | collective-permute-start | bytes 1179656 | tf_op jit(solution)/shard_map/dp_projection0/ppermute | solution.py:296
  637.6 56.1 %collective-permute-start.24 = (bf16[256,2048]{1,0:T(8,128)(2,1)}, bf16[256,2048]{1,0:T(8,128)(2,1)}, u32[]{:S(2)}, u32[]{:S(2)}) collective-permute-start(bf16[256,2048]{1,0:T(8,128)(2,1)} %slice.240), channel_id=1, source_target_pairs={{0,1},{1,0},{2,3},{3,2},{4,5},{5,4},{6,7},{7,6},{8,9},{9,8},{10,11... | collective-permute-start | bytes 3145736 | tf_op jit(solution)/shard_map/ppermute | solution.py:245
  638.4 19.0 %collective-permute-start.55 = (bf16[64,2048]{1,0:T(8,128)(2,1)}, bf16[64,2048]{1,0:T(8,128)(2,1)}, u32[]{:S(2)}, u32[]{:S(2)}) collective-permute-start(bf16[64,2048]{1,0:T(8,128)(2,1)} %collective-permute-done.51), channel_id=1, source_target_pairs={{0,8},{8,0},{16,24},{24,16},{1,9},{9,1},{17,25},{25,17},{2,10},{10... | collective-permute-start | bytes 786440 | tf_op jit(solution)/shard_map/dp_output/ppermute | solution.py:296
  639.2 18.2 %collective-permute-start.53 = (bf16[256,768]{0,1:T(8,128)(2,1)}, bf16[256,768]{0,1:T(8,128)(2,1)}, u32[]{:S(2)}, u32[]{:S(2)}) collective-permute-start(bf16[256,768]{0,1:T(8,128)(2,1)} %collective-permute-done.47), channel_id=1, source_target_pairs={{0,8},{8,0},{16,24},{24,16},{1,9},{9,1},{17,25},{25,17},{2,10},{10... | collective-permute-start | bytes 1179656 | tf_op jit(solution)/shard_map/dp_projection0/ppermute | solution.py:296
  656.8 36.9 %collective-permute-start.46 = (bf16[256,2048]{1,0:T(8,128)(2,1)}, bf16[256,2048]{1,0:T(8,128)(2,1)}, u32[]{:S(2)}, u32[]{:S(2)}) collective-permute-start(bf16[256,2048]{1,0:T(8,128)(2,1)} %add_convert_fusion.3), channel_id=1, source_target_pairs={{0,2},{1,3},{2,6},{3,7},{6,4},{7,5},{4,0},{5,1},{8,10},{9,11},{10,... | collective-permute-start | bytes 3145736 | tf_op jit(solution)/shard_map/branch_ring3/ppermute | solution.py:241
  (74 other events, 507.4 us)
Sparse Core Ops, SparseCore 0:
  12.7 94.0 all-gather.3
  108.4 113.9 all-gather.5
  390.3 80.4 all-gather.7
  530.3 92.9 reduce-scatter.1

commit v4 on v3

--- a/solution.py
+++ b/solution.py
@@ -506,13 +506,14 @@
     mixed_rows = (unit_two * feedforward_gain + feedforward_shift).astype(bf16)
 
     mixed, activated, grad_pre, mixed_terms, mixed_arrivals = [], [], [], [], []
+    mixed_sent = []
     moving = after(mixed_rows, grad_out)
 
     def mixed_step(step):
         mixed.append(jnp.concatenate([moving, swap_cores(moving)], axis=0))
         rows = mixed[step]
         if step > 2:
-            rows = after(rows, mixed_arrivals[step - 3])
+            rows = after(rows, mixed_sent[step - 2])
         grad_activated = dot(chip_rows(grad_out, step), contract_weight, 1, 1)
         pre_act = dot(rows, expand_weight, 1, 0) + expand_bias
         value, gelu_pull = jax.vjp(gelu_tanh, pre_act)
@@ -532,7 +533,8 @@
         if step:
             with jax.named_scope(f"grad_mixed_ring{step}"):
                 total = chip_total(mixed_terms[step], mixed_arrivals)
-                mixed_arrivals.append(ring_step(total.astype(bf16)))
+                mixed_sent.append(total.astype(bf16))
+                mixed_arrivals.append(ring_step(mixed_sent[-1]))
     second = mixed_arrivals[-2]
     activated_all = after(ordered(activated), second)
     grad_pre_all = after(ordered(grad_pre), second)
@@ -562,8 +564,7 @@
         for block in branch_terms
     ]
     branch_sent = branch_totals[1].astype(bf16)
-    grad_hidden_low = exchange.hop(grad_hidden_low)
-    for _ in bits[1:]:
+    for _ in bits:
         grad_hidden_low = exchange.hop(grad_hidden_low, *branch_terms, branch_sent)[0]
     grad_hidden_all, branch_sent = lax.optimization_barrier(
         (after(grad_hidden_all, grad_hidden_low), branch_sent)
@@ -623,16 +624,14 @@
     for _ in bits[1:]:
         exchange.hop()
     branch_arrived = exchange.hop(branch_arrived)
-    sums_by_row, branch_arrived = lax.optimization_barrier((sums_by_row, branch_arrived))
+    sums_by_row, branch_arrived = exchange.hop(sums_by_row, branch_arrived)
     for step in range(3, chips):
         branch_arrived = branch_step(step)
-    branch = branch_totals[0] + branch_arrived.astype(f32)
-    layer_output = (local_live * (hidden + branch + contract_bias)).astype(bf16)
-    exchange.hop()
     while exchange.flying:
-        sums_by_row = exchange.hop(sums_by_row)
+        exchange.hop()
     with jax.named_scope("small_sums"):
         sums = small_sum(jnp.concatenate([sums_by_row.reshape(-1), sums_by_width]), ("dp",))
+        sums, branch_arrived = lax.optimization_barrier((sums, branch_arrived))
         sums_by_width = sums[sums_by_row.size :]
         sums_by_row = small_sum(
             sums[: sums_by_row.size].reshape(sums_by_row.shape), ("tensor",)
@@ -669,6 +668,8 @@
             output_gradient, block, cut_place(mask, bits, output_local.shape[0])
         )
 
+    branch = branch_totals[0] + branch_arrived.astype(f32)
+    layer_output = (local_live * (hidden + branch + contract_bias)).astype(bf16)
     query_value_gradient = sums_by_width[: 2 * local_width].reshape(2, local_width)
     expand_bias_gradient = sums_by_width[2 * local_width :]
     return (

time: 713 us -> 702 us (0.985)
  waiting for transfers between devices: 269 us -> 258 us
    ppermute x31, waiting for transfers between devices: 104 us -> 89.3 us  [flip_dp(): return lax.ppermute(value, 'dp', [(i, i ^ bit) for i in range(size)])]
    unnamed x115 -> x135, local copies, waits for them, and re-layouts: 18.5 us -> 18.3 us
  transfers between devices with their start and end apart: 66 -> 66, of which waited for: 28 -> 29; matrix products, arithmetic and copies ran while one was open for 40% -> 41% of each run, Pallas kernels for 5% -> 6%
where the time goes in v4:
time: 702 us; the launch traced here: 692 us
  waiting for transfers between devices  258 us (37%)
  matrix products  141 us (20%)
  local copies, waits for them, and re-layouts  80.5 us (11%)
  other arithmetic  80.1 us (11%)
  starting transfers between devices  68.5 us (10%)
  Pallas kernels  38.1 us (5%)
  between operations  25.1 us (4%)
    dot_general x25, matrix products, dot(): lax.dot_general(a, b, (((a_axis,), (b_axis,)), ((), ())), preferred_eleme...  141 us
    ppermute x12, waiting for transfers between devices, ring_step(): return lax.ppermute(value, 'tensor', pairs)  104 us
    ppermute x31, waiting for transfers between devices, flip_dp(): return lax.ppermute(value, 'dp', [(i, i ^ bit) for i in range(size)])  89.3 us
    all_to_all x1, waiting for transfers between devices, shards(): lax.all_to_all(context.reshape(tensor_size, shard_rows, local_width), 'te...  45.2 us
    ppermute x31, starting transfers between devices, flip_dp(): return lax.ppermute(value, 'dp', [(i, i ^ bit) for i in range(size)])  34.2 us
    dynamic_update_slice x13, other arithmetic, put(): lax.dynamic_update_slice(full, block.astype(full.dtype), (row, column))  26.4 us
    pallas_call x1, Pallas kernels, attend_back(): pl.pallas_call(functools.partial(attend_back_kernel, block, local_heads),...  21.6 us
    unnamed x135, local copies, waits for them, and re-layouts  18.3 us
  transfers between devices with their start and end apart: 66, of which 29 were waited for; matrix products, arithmetic and copies ran while one was open for 41% of the time, Pallas kernels for 6%

profile of v4, /device:TPU:0, one launch (start us, length us, event | category | flops | bytes accessed | tf_op | source)
XLA Modules:
  0.0 691.7 jit_solution(17265213846881590051)
XLA Ops:
  15.2 7.3 %collective-permute-done = bf16[256,512]{1,0:T(8,128)(2,1)S(1)} collective-permute-done((bf16[256,512]{1,0:T(8,128)(2,1)S(1)}, bf16[256,512]{1,0:T(8,128)(2,1)S(1)}, u32[]{:S(2)}, u32[]{:S(2)}) %collective-permute-start) | collective-permute-done | bytes 262176 | tf_op jit(solution)/shard_map/weight_ring/ppermute | solution.py:241
  28.3 14.2 %collective-permute-done.4 = bf16[256,512]{1,0:T(8,128)(2,1)S(1)} collective-permute-done((bf16[256,512]{1,0:T(8,128)(2,1)S(1)}, bf16[256,512]{1,0:T(8,128)(2,1)S(1)}, u32[]{:S(2)}, u32[]{:S(2)}) %collective-permute-start.4) | collective-permute-done | bytes 262176 | tf_op jit(solution)/shard_map/weight_ring/ppermute | solution.py:241
  45.7 17.1 %collective-permute-done.5 = bf16[256,512]{1,0:T(8,128)(2,1)S(1)} collective-permute-done((bf16[256,512]{1,0:T(8,128)(2,1)S(1)}, bf16[256,512]{1,0:T(8,128)(2,1)S(1)}, u32[]{:S(2)}, u32[]{:S(2)}) %collective-permute-start.5) | collective-permute-done | bytes 262176 | tf_op jit(solution)/shard_map/weight_ring/ppermute | solution.py:241
  66.7 11.0 %collective-permute-done.6 = bf16[512,512]{1,0:T(8,128)(2,1)S(1)} collective-permute-done((bf16[512,512]{1,0:T(8,128)(2,1)S(1)}, bf16[512,512]{1,0:T(8,128)(2,1)S(1)}, u32[]{:S(2)}, u32[]{:S(2)}) %collective-permute-start.6) | collective-permute-done | bytes 524320 | tf_op jit(solution)/shard_map/weight_dp/ppermute | solution.py:296
  77.7 9.9 %collective-permute-done.2 = bf16[512,512]{1,0:T(8,128)(2,1)} collective-permute-done((bf16[512,512]{1,0:T(8,128)(2,1)S(1)}, bf16[512,512]{1,0:T(8,128)(2,1)}, u32[]{:S(2)}, u32[]{:S(2)}) %collective-permute-start.2) | collective-permute-done | bytes 524320 | tf_op jit(solution)/shard_map/weight_dp/ppermute | solution.py:296
  89.4 3.7 collective-permute-done.3
  98.4 4.8 copy.77
  106.7 10.1 %add_convert_fusion.q_ref.k_ref.v_ref = bf16[2048,768]{1,0:T(8,128)(2,1)S(1)} fusion(f32[768]{0:T(1024)S(1)} %pad_maximum_fusion.3, bf16[2048,2048]{1,0:T(8,128)(2,1)} %all-gather.4.cloned.1.call-done, bf16[2048,768]{0,1:T(8,128)(2,1)} %bitcast.177), kind=kOutput, calls=%fused_computation.6 | convolution fusion | flops 6445596672 | bytes 14683136 | tf_op jit(solution)/shard_map/dot_general | solution.py:430
  116.8 16.5 %shard_map.686 = (bf16[2048,256]{1,0:T(8,128)(2,1)}, f32[2,1,2048]{2,1,0:T(1,128)S(1)}) custom-call(s32[2]{0:T(128)S(1)} %get-tuple-element.156.bounds_ref, bf16[2048,768]{1,0:T(8,128)(2,1)S(1)} %add_convert_fusion.q_ref.k_ref.v_ref, bf16[2048,768]{1,0:T(8,128)(2,1)S(1)} %add_convert_fusion.q_ref.k_ref.v_ref, ...), custom_call_target="tpu_custom_call" | custom-call | flops 4294967296 | bytes 4194304 | tf_op jit(solution)/shard_map/pallas_call | solution.py:73
  133.3 14.4 %all-to-all-start = ((bf16[8,256,256]{2,1,0:T(8,128)(2,1)}), bf16[8,256,256]{2,1,0:T(8,128)(2,1)S(1)}, u32[]{:S(2)}, u32[]{:S(2)}) async-start(bf16[8,256,256]{2,1,0:T(8,128)(2,1)} %bitcast.4), calls=%async_computation | async-start | bytes 2097152 | tf_op jit(solution)/shard_map/all_to_all | solution.py:485
  157.6 45.2 %all-to-all-done = bf16[8,256,256]{2,1,0:T(8,128)(2,1)S(1)} async-done(((bf16[8,256,256]{2,1,0:T(8,128)(2,1)}), bf16[8,256,256]{2,1,0:T(8,128)(2,1)S(1)}, u32[]{:S(2)}, u32[]{:S(2)}) %all-to-all-start) | async-done | bytes 1048608 | tf_op jit(solution)/shard_map/all_to_all | solution.py:485
  206.5 3.8 fusion.133
  212.4 9.5 %all-gather.6.cloned.1.call-done = bf16[2048,2048]{1,0:T(8,128)(2,1)} async-done(((bf16[256,2048]{1,0:T(8,128)(2,1)}), bf16[2048,2048]{1,0:T(8,128)(2,1)}) %all-gather.6.cloned.1.call-update) | async-done | bytes 8388624 | tf_op jit(solution)/shard_map/all_gather | solution.py:480
  223.8 4.3 constant_dynamic-slice_fusion.17
  229.4 5.0 fusion.47
  242.3 8.1 %collective-permute-done.12 = bf16[256,2048]{1,0:T(8,128)(2,1)} collective-permute-done((bf16[256,2048]{1,0:T(8,128)(2,1)}, bf16[256,2048]{1,0:T(8,128)(2,1)}, u32[]{:S(2)}, u32[]{:S(2)}) %collective-permute-start.12) | collective-permute-done | bytes 1048608 | tf_op jit(solution)/shard_map/mixed_ring1/ppermute | solution.py:241
  253.3 4.9 fusion.63
  258.3 6.7 fusion.31
  267.5 9.8 %collective-permute-done.13 = bf16[256,2048]{1,0:T(8,128)(2,1)S(1)} collective-permute-done((bf16[256,2048]{1,0:T(8,128)(2,1)}, bf16[256,2048]{1,0:T(8,128)(2,1)S(1)}, u32[]{:S(2)}, u32[]{:S(2)}) %collective-permute-start.13) | collective-permute-done | bytes 1048608 | tf_op jit(solution)/shard_map/mixed_ring2/ppermute | solution.py:241
  282.1 3.7 fusion.71
  285.8 6.7 fusion.38
  295.2 9.2 %collective-permute-done.15 = bf16[256,2048]{1,0:T(8,128)(2,1)S(1)} collective-permute-done((bf16[256,2048]{1,0:T(8,128)(2,1)S(1)}, bf16[256,2048]{1,0:T(8,128)(2,1)S(1)}, u32[]{:S(2)}, u32[]{:S(2)}) %collective-permute-start.15) | collective-permute-done | bytes 1048608 | tf_op jit(solution)/shard_map/mixed_ring3/ppermute | solution.py:241
  304.6 20.9 %collective-permute-done.20 = bf16[256,2048]{1,0:T(8,128)(2,1)S(1)} collective-permute-done((bf16[256,2048]{1,0:T(8,128)(2,1)S(1)}, bf16[256,2048]{1,0:T(8,128)(2,1)S(1)}, u32[]{:S(2)}, u32[]{:S(2)}) %collective-permute-start.20) | collective-permute-done | bytes 1048608 | tf_op jit(solution)/shard_map/grad_mixed_ring1/ppermute | solution.py:241
  329.2 7.0 %multiply_convert_fusion.4 = (bf16[512,1024]{1,0:T(8,128)(2,1)S(1)}, bf16[512,1024]{1,0:T(8,128)(2,1)S(1)}, bf16[512,1024]{1,0:T(8,128)(2,1)S(1)}, bf16[512,1024]{1,0:T(8,128)(2,1)S(1)}, f32[512,1024]{1,0:T(8,128)S(1)}) fusion(f32[1024]{0:T(1024)S(1)} %copy-done.62, f32[512,1024]{1,0:T(8,128)} %fusion.71, f32[512,1024]{1,0:T(8,128)} %fusion.63, ...), kind=kOutput, calls=%fused_computation.128 | convolution fusion | flops 2168455168 | bytes 18878464 | tf_op jit(solution)/shard_map/mixed_ring3/dot_general | solution.py:430
  336.3 7.2 %fusion.45 = bf16[512,1024]{1,0:T(8,128)(2,1)S(1)} fusion(f32[512,1024]{1,0:T(8,128)S(1)} %get-tuple-element.198, bf16[1024,2048]{1,0:T(8,128)(2,1)} %param.75, bf16[256,2048]{1,0:T(8,128)(2,1)S(1)} %get-tuple-element.163, bf16[256,2048]{1,0:T(8,128)(2,1)S(1)} %get-tuple-element.158, f32[1024]{0:T(1024)S(1)} %copy-done.62), kind=kOutput, calls=%fused_computation.80 | convolution fusion | flops 2162688000 | bytes 9441280 | tf_op jit(solution)/shard_map/mixed_ring3/dot_general | solution.py:430
  354.3 11.0 %multiply_convert_fusion.1 = bf16[1024,2048]{1,0:T(8,128)(2,1)} fusion(bf16[2048,1024]{1,0:T(8,128)(2,1)S(1)} %bitcast.176, bf16[2048,2048]{1,0:T(8,128)(2,1)S(1)} %bitcast.174, f32[]{:T(128)S(6)} %div.65), kind=kOutput, calls=%fused_computation.2 | convolution fusion | flops 8594128896 | bytes 16777220 | tf_op jit(solution)/shard_map/contract_gradient/dot_general | solution.py:430
  365.3 10.9 %multiply_convert_fusion = bf16[2048,1024]{1,0:T(8,128)(2,1)} fusion(bf16[2048,2048]{1,0:T(8,128)(2,1)S(1)} %bitcast.175, bf16[2048,1024]{1,0:T(8,128)(2,1)S(1)} %bitcast.171, f32[]{:T(128)S(6)} %div.65), kind=kOutput, calls=%fused_computation.1 | convolution fusion | flops 8594128896 | bytes 16777220 | tf_op jit(solution)/shard_map/expand_gradient/dot_general | solution.py:430
  393.3 5.2 convolution_convert_fusion.3
  399.7 3.7 convolution_convert_fusion.4
  403.5 3.7 convolution_convert_fusion.2
  412.2 23.3 %collective-permute-done.27 = bf16[512,2048]{1,0:T(8,128)(2,1)S(1)} collective-permute-done((bf16[512,2048]{1,0:T(8,128)(2,1)S(1)}, bf16[512,2048]{1,0:T(8,128)(2,1)S(1)}, u32[]{:S(2)}, u32[]{:S(2)}) %collective-permute-start.27) | collective-permute-done | bytes 2097184 | tf_op jit(solution)/shard_map/dp_contract/ppermute | solution.py:296
  448.0 13.7 %collective-permute-done.29 = bf16[256,2048]{1,0:T(8,128)(2,1)} collective-permute-done((bf16[256,2048]{1,0:T(8,128)(2,1)}, bf16[256,2048]{1,0:T(8,128)(2,1)}, u32[]{:S(2)}, u32[]{:S(2)}) %collective-permute-start.29) | collective-permute-done | bytes 1048608 | tf_op jit(solution)/shard_map/dp_contract/ppermute | solution.py:296
  461.7 4.6 collective-permute-done.30
  474.0 5.8 convolution_convert_fusion.9.grad_ref
  479.8 21.6 %shard_map.687 = bf16[2048,768]{1,0:T(8,128)(2,1)S(1)} custom-call(s32[2]{0:T(128)S(1)} %get-tuple-element.156.bounds_ref, bf16[2048,768]{1,0:T(8,128)(2,1)} %copy-done.3, bf16[2048,768]{1,0:T(8,128)(2,1)} %copy-done.3, bf16[2048,768]{1,0:T(8,128)(2,1)} %copy-done.3, bf16[2048,256]{1,0:T(8,128)(2,1)S(1)} %convolution_convert_fusion.9.grad_ref, ...), custom_call_target="tpu_custom_call" | custom-call | flops 10737418240 | bytes 8388608 | tf_op jit(solution)/shard_map/pallas_call | solution.py:174
  501.6 4.0 add_convert_fusion.4
  507.2 9.1 %convolution_convert_fusion = bf16[2048,2048]{1,0:T(8,128)(2,1)} fusion(bf16[2048,768]{1,0:T(8,128)(2,1)S(1)} %shard_map.687, bf16[2048,768]{0,1:T(8,128)(2,1)S(1)} %bitcast.178), kind=kOutput, calls=%fused_computation.3 | convolution fusion | flops 6446645248 | bytes 14680064 | tf_op jit(solution)/shard_map/normed_terms/dot_general | solution.py:430
  516.4 5.2 collective-permute-done.34
  521.6 7.5 %collective-permute-done.36 = bf16[256,2048]{1,0:T(8,128)(2,1)} collective-permute-done((bf16[256,2048]{1,0:T(8,128)(2,1)}, bf16[256,2048]{1,0:T(8,128)(2,1)}, u32[]{:S(2)}, u32[]{:S(2)}) %collective-permute-start.36) | collective-permute-done | bytes 1048608 | tf_op jit(solution)/shard_map/branch_ring2/ppermute | solution.py:241
  541.0 10.4 %multiply_convert_fusion.2 = bf16[2048,768]{0,1:T(8,128)(2,1)S(1)} fusion(bf16[2048,2048]{1,0:T(8,128)(2,1)} %all-gather.4.cloned.1.call-done, bf16[2048,768]{1,0:T(8,128)(2,1)} %copy-done.1, f32[]{:T(128)S(6)} %div.65), kind=kOutput, calls=%fused_computation.5 | convolution fusion | flops 6445596672 | bytes 14680068 | tf_op jit(solution)/shard_map/projection_gradient/dot_general | solution.py:430
  552.9 6.1 fusion.5
  561.2 4.5 broadcast_in_dim.159
  568.4 4.5 broadcast_in_dim.160
  595.5 9.6 %collective-permute-done.44 = bf16[64,2048]{1,0:T(8,128)(2,1)S(1)} collective-permute-done((bf16[64,2048]{1,0:T(8,128)(2,1)S(1)}, bf16[64,2048]{1,0:T(8,128)(2,1)S(1)}, u32[]{:S(2)}, u32[]{:S(2)}) %collective-permute-start.44) | collective-permute-done | bytes 262176 | tf_op jit(solution)/shard_map/dp_output/ppermute | solution.py:296
  614.8 6.1 reduce-scatter.2.cloned.1.call-done
  630.0 4.9 collective-permute-done.47
  663.1 4.0 collective-permute-done.54
  672.1 5.4 copy.78
  (399 shorter events, 220.9 us)
Async XLA Ops:
  7.2 99.4 %all-gather.4.cloned.1.call-start = ((), (), s32[]{:S(2)}) async-start(), calls=%async_computation.2 | async-start | bytes 9437184 | tf_op jit(solution)/shard_map/all_gather | solution.py:452
  12.0 209.8 %all-gather.6.cloned.1.call-start = ((), (), s32[]{:S(2)}) async-start(), calls=%async_computation.3 | async-start | bytes 9437184 | tf_op jit(solution)/shard_map/all_gather | solution.py:480
  22.5 20.0 %collective-permute-start.4 = (bf16[256,512]{1,0:T(8,128)(2,1)S(1)}, bf16[256,512]{1,0:T(8,128)(2,1)S(1)}, u32[]{:S(2)}, u32[]{:S(2)}) collective-permute-start(bf16[256,512]{1,0:T(8,128)(2,1)S(1)} %collective-permute-done), channel_id=1, source_target_pairs={{0,2},{1,3},{2,6},{3,7},{6,4},{7,5},{4,0},{5,1},{8,10},{9,11},{10,... | collective-permute-start | bytes 786440 | tf_op jit(solution)/shard_map/weight_ring/ppermute | solution.py:241
  26.8 38.1 %collective-permute-start.1 = (bf16[512,512]{1,0:T(8,128)(2,1)S(1)}, bf16[512,512]{1,0:T(8,128)(2,1)S(1)}, u32[]{:S(2)}, u32[]{:S(2)}) collective-permute-start(bf16[512,512]{1,0:T(8,128)(2,1)S(1)} %get-tuple-element.176), channel_id=1, source_target_pairs={{0,8},{8,0},{16,24},{24,16},{1,9},{9,1},{17,25},{25,17},{2,10},{10... | collective-permute-start | bytes 1572872 | tf_op jit(solution)/shard_map/weight_dp/ppermute | solution.py:296
  42.5 20.2 %collective-permute-start.5 = (bf16[256,512]{1,0:T(8,128)(2,1)S(1)}, bf16[256,512]{1,0:T(8,128)(2,1)S(1)}, u32[]{:S(2)}, u32[]{:S(2)}) collective-permute-start(bf16[256,512]{1,0:T(8,128)(2,1)S(1)} %collective-permute-done.4), channel_id=1, source_target_pairs={{0,2},{1,3},{2,6},{3,7},{6,4},{7,5},{4,0},{5,1},{8,10},{9,11},{10,... | collective-permute-start | bytes 786440 | tf_op jit(solution)/shard_map/weight_ring/ppermute | solution.py:241
  62.8 14.9 %collective-permute-start.6 = (bf16[512,512]{1,0:T(8,128)(2,1)S(1)}, bf16[512,512]{1,0:T(8,128)(2,1)S(1)}, u32[]{:S(2)}, u32[]{:S(2)}) collective-permute-start(bf16[512,512]{1,0:T(8,128)(2,1)S(1)} %constant_dynamic-update-slice_fusion.12), channel_id=1, source_target_pairs={{0,16},{8,24},{16,0},{24,8},{1,17},{9,25},{17,1},{25,9},{2,18},{10... | collective-permute-start | bytes 1572872 | tf_op jit(solution)/shard_map/weight_dp/ppermute | solution.py:296
  62.9 24.7 %collective-permute-start.2 = (bf16[512,512]{1,0:T(8,128)(2,1)S(1)}, bf16[512,512]{1,0:T(8,128)(2,1)}, u32[]{:S(2)}, u32[]{:S(2)}) collective-permute-start(bf16[512,512]{1,0:T(8,128)(2,1)S(1)} %get-tuple-element.176), channel_id=1, source_target_pairs={{0,16},{8,24},{16,0},{24,8},{1,17},{9,25},{17,1},{25,9},{2,18},{10... | collective-permute-start | bytes 1572872 | tf_op jit(solution)/shard_map/weight_dp/ppermute | solution.py:296
  64.9 28.3 %collective-permute-start.3 = (bf16[512,512]{1,0:T(8,128)(2,1)S(1)}, bf16[512,512]{1,0:T(8,128)(2,1)}, u32[]{:S(2)}, u32[]{:S(2)}) collective-permute-start(bf16[512,512]{1,0:T(8,128)(2,1)S(1)} %collective-permute-done.1), channel_id=1, source_target_pairs={{0,16},{8,24},{16,0},{24,8},{1,17},{9,25},{17,1},{25,9},{2,18},{10... | collective-permute-start | bytes 1572872 | tf_op jit(solution)/shard_map/weight_dp/ppermute | solution.py:296
  65.0 31.8 %collective-permute-start.7 = (bf16[512,512]{1,0:T(8,128)(2,1)S(1)}, bf16[512,512]{1,0:T(8,128)(2,1)S(1)}, u32[]{:S(2)}, u32[]{:S(2)}) collective-permute-start(bf16[512,512]{1,0:T(8,128)(2,1)S(1)} %constant_dynamic-update-slice_fusion.12), channel_id=1, source_target_pairs={{0,8},{8,0},{16,24},{24,16},{1,9},{9,1},{17,25},{25,17},{2,10},{10... | collective-permute-start | bytes 1572872 | tf_op jit(solution)/shard_map/weight_dp/ppermute | solution.py:296
  77.7 19.8 %collective-permute-start.8 = (bf16[512,512]{1,0:T(8,128)(2,1)S(1)}, bf16[512,512]{1,0:T(8,128)(2,1)S(1)}, u32[]{:S(2)}, u32[]{:S(2)}) collective-permute-start(bf16[512,512]{1,0:T(8,128)(2,1)S(1)} %collective-permute-done.6), channel_id=1, source_target_pairs={{0,8},{8,0},{16,24},{24,16},{1,9},{9,1},{17,25},{25,17},{2,10},{10... | collective-permute-start | bytes 1572872 | tf_op jit(solution)/shard_map/weight_dp/ppermute | solution.py:296
  133.3 69.5 %all-to-all-start = ((bf16[8,256,256]{2,1,0:T(8,128)(2,1)}), bf16[8,256,256]{2,1,0:T(8,128)(2,1)S(1)}, u32[]{:S(2)}, u32[]{:S(2)}) async-start(bf16[8,256,256]{2,1,0:T(8,128)(2,1)} %bitcast.4), calls=%async_computation | async-start | bytes 2097152 | tf_op jit(solution)/shard_map/all_to_all | solution.py:485
  147.7 326.1 %all-gather.8.cloned.1.call-start = ((), (), s32[]{:S(2)}) async-start(), calls=%async_computation.4 | async-start | bytes 9437184 | tf_op jit(solution)/shard_map/grad_hidden_gather/all_gather | solution.py:554
  223.5 26.8 %collective-permute-start.12 = (bf16[256,2048]{1,0:T(8,128)(2,1)}, bf16[256,2048]{1,0:T(8,128)(2,1)}, u32[]{:S(2)}, u32[]{:S(2)}) collective-permute-start(bf16[256,2048]{1,0:T(8,128)(2,1)} %add_convert_fusion.11), channel_id=1, source_target_pairs={{0,2},{1,3},{2,6},{3,7},{6,4},{7,5},{4,0},{5,1},{8,10},{9,11},{10,... | collective-permute-start | bytes 3145736 | tf_op jit(solution)/shard_map/mixed_ring1/ppermute | solution.py:241
  241.4 137.5 %collective-permute-start.11 = (bf16[256,2048]{1,0:T(8,128)(2,1)}, bf16[256,2048]{1,0:T(8,128)(2,1)}, u32[]{:S(2)}, u32[]{:S(2)}) collective-permute-start(bf16[256,2048]{1,0:T(8,128)(2,1)} %slice.216), channel_id=1, source_target_pairs={{0,1},{1,0},{2,3},{3,2},{4,5},{5,4},{6,7},{7,6},{8,9},{9,8},{10,11... | collective-permute-start | bytes 3145736 | tf_op jit(solution)/shard_map/grad_mixed_own/ppermute | solution.py:245
  250.4 27.0 %collective-permute-start.13 = (bf16[256,2048]{1,0:T(8,128)(2,1)}, bf16[256,2048]{1,0:T(8,128)(2,1)S(1)}, u32[]{:S(2)}, u32[]{:S(2)}) collective-permute-start(bf16[256,2048]{1,0:T(8,128)(2,1)} %collective-permute-done.12), channel_id=1, source_target_pairs={{0,2},{1,3},{2,6},{3,7},{6,4},{7,5},{4,0},{5,1},{8,10},{9,11},{10,... | collective-permute-start | bytes 3145736 | tf_op jit(solution)/shard_map/mixed_ring2/ppermute | solution.py:241
  277.4 27.0 %collective-permute-start.15 = (bf16[256,2048]{1,0:T(8,128)(2,1)S(1)}, bf16[256,2048]{1,0:T(8,128)(2,1)S(1)}, u32[]{:S(2)}, u32[]{:S(2)}) collective-permute-start(bf16[256,2048]{1,0:T(8,128)(2,1)S(1)} %collective-permute-done.13), channel_id=1, source_target_pairs={{0,2},{1,3},{2,6},{3,7},{6,4},{7,5},{4,0},{5,1},{8,10},{9,11},{10,... | collective-permute-start | bytes 3145736 | tf_op jit(solution)/shard_map/mixed_ring3/ppermute | solution.py:241
  280.4 45.1 %collective-permute-start.20 = (bf16[256,2048]{1,0:T(8,128)(2,1)S(1)}, bf16[256,2048]{1,0:T(8,128)(2,1)S(1)}, u32[]{:S(2)}, u32[]{:S(2)}) collective-permute-start(bf16[256,2048]{1,0:T(8,128)(2,1)S(1)} %add_convert_fusion.10), channel_id=1, source_target_pairs={{0,2},{1,3},{2,6},{3,7},{6,4},{7,5},{4,0},{5,1},{8,10},{9,11},{10,... | collective-permute-start | bytes 3145736 | tf_op jit(solution)/shard_map/grad_mixed_ring1/ppermute | solution.py:241
  295.0 30.5 %collective-permute-start.18 = (bf16[256,2048]{1,0:T(8,128)(2,1)S(1)}, bf16[256,2048]{1,0:T(8,128)(2,1)S(1)}, u32[]{:S(2)}, u32[]{:S(2)}) collective-permute-start(bf16[256,2048]{1,0:T(8,128)(2,1)S(1)} %slice.218), channel_id=1, source_target_pairs={{0,1},{1,0},{2,3},{3,2},{4,5},{5,4},{6,7},{7,6},{8,9},{9,8},{10,11... | collective-permute-start | bytes 3145736 | tf_op jit(solution)/shard_map/grad_mixed_ring2/ppermute | solution.py:245
  304.3 22.9 %collective-permute-start.16 = (bf16[256,2048]{1,0:T(8,128)(2,1)S(1)}, bf16[256,2048]{1,0:T(8,128)(2,1)S(1)}, u32[]{:S(2)}, u32[]{:S(2)}) collective-permute-start(bf16[256,2048]{1,0:T(8,128)(2,1)S(1)} %collective-permute-done.15), channel_id=1, source_target_pairs={{0,1},{1,0},{2,3},{3,2},{4,5},{5,4},{6,7},{7,6},{8,9},{9,8},{10,11... | collective-permute-start | bytes 3145736 | tf_op jit(solution)/shard_map/mixed_ring3/ppermute | solution.py:245
  327.0 25.3 %collective-permute-start.22 = (bf16[256,2048]{1,0:T(8,128)(2,1)}, bf16[256,2048]{1,0:T(8,128)(2,1)}, u32[]{:S(2)}, u32[]{:S(2)}) collective-permute-start(bf16[256,2048]{1,0:T(8,128)(2,1)} %add_convert_fusion.9), channel_id=1, source_target_pairs={{0,2},{1,3},{2,6},{3,7},{6,4},{7,5},{4,0},{5,1},{8,10},{9,11},{10,... | collective-permute-start | bytes 3145736 | tf_op jit(solution)/shard_map/grad_mixed_ring2/ppermute | solution.py:241
  354.0 25.0 %collective-permute-start.23 = (bf16[256,2048]{1,0:T(8,128)(2,1)S(1)}, bf16[256,2048]{1,0:T(8,128)(2,1)S(1)}, u32[]{:S(2)}, u32[]{:S(2)}) collective-permute-start(bf16[256,2048]{1,0:T(8,128)(2,1)S(1)} %add_convert_fusion.8), channel_id=1, source_target_pairs={{0,2},{1,3},{2,6},{3,7},{6,4},{7,5},{4,0},{5,1},{8,10},{9,11},{10,... | collective-permute-start | bytes 3145736 | tf_op jit(solution)/shard_map/grad_mixed_ring3/ppermute | solution.py:241
  387.7 233.3 %reduce-scatter.2.cloned.1.call-start = ((), (), s32[]{:S(2)}) async-start(), calls=%async_computation.5 | async-start | bytes 9437184 | tf_op jit(solution)/shard_map/grad_normed_scatter/reduce_scatter | solution.py:590
  390.0 45.4 %collective-permute-start.27 = (bf16[512,2048]{1,0:T(8,128)(2,1)S(1)}, bf16[512,2048]{1,0:T(8,128)(2,1)S(1)}, u32[]{:S(2)}, u32[]{:S(2)}) collective-permute-start(bf16[512,2048]{1,0:T(8,128)(2,1)S(1)} %constant_dynamic-slice_fusion.1), channel_id=1, source_target_pairs={{0,8},{8,0},{16,24},{24,16},{1,9},{9,1},{17,25},{25,17},{2,10},{10... | collective-permute-start | bytes 6291464 | tf_op jit(solution)/shard_map/dp_contract/ppermute | solution.py:296
  391.8 45.2 %collective-permute-start.28 = (bf16[1024,1024]{1,0:T(8,128)(2,1)S(1)}, bf16[1024,1024]{1,0:T(8,128)(2,1)S(1)}, u32[]{:S(2)}, u32[]{:S(2)}) collective-permute-start(bf16[1024,1024]{1,0:T(8,128)(2,1)S(1)} %constant_dynamic-slice_fusion.2), channel_id=1, source_target_pairs={{0,16},{8,24},{16,0},{24,8},{1,17},{9,25},{17,1},{25,9},{2,18},{10... | collective-permute-start | bytes 6291464 | tf_op jit(solution)/shard_map/dp_expand/ppermute | solution.py:296
  439.6 22.1 %collective-permute-start.29 = (bf16[256,2048]{1,0:T(8,128)(2,1)}, bf16[256,2048]{1,0:T(8,128)(2,1)}, u32[]{:S(2)}, u32[]{:S(2)}) collective-permute-start(bf16[256,2048]{1,0:T(8,128)(2,1)} %constant_dynamic-slice_fusion.3), channel_id=1, source_target_pairs={{0,16},{8,24},{16,0},{24,8},{1,17},{9,25},{17,1},{25,9},{2,18},{10... | collective-permute-start | bytes 3145736 | tf_op jit(solution)/shard_map/dp_contract/ppermute | solution.py:296
  444.4 21.8 %collective-permute-start.30 = (bf16[512,1024]{1,0:T(8,128)(2,1)}, bf16[512,1024]{1,0:T(8,128)(2,1)}, u32[]{:S(2)}, u32[]{:S(2)}) collective-permute-start(bf16[512,1024]{1,0:T(8,128)(2,1)} %constant_dynamic-slice_fusion.4), channel_id=1, source_target_pairs={{0,8},{8,0},{16,24},{24,16},{1,9},{9,1},{17,25},{25,17},{2,10},{10... | collective-permute-start | bytes 3145736 | tf_op jit(solution)/shard_map/dp_expand/ppermute | solution.py:296
  448.0 53.6 %collective-permute-start.35 = (bf16[256,2048]{1,0:T(8,128)(2,1)}, bf16[256,2048]{1,0:T(8,128)(2,1)}, u32[]{:S(2)}, u32[]{:S(2)}) collective-permute-start(bf16[256,2048]{1,0:T(8,128)(2,1)} %slice.244), channel_id=1, source_target_pairs={{0,1},{1,0},{2,3},{3,2},{4,5},{5,4},{6,7},{7,6},{8,9},{9,8},{10,11... | collective-permute-start | bytes 3145736 | tf_op jit(solution)/shard_map/ppermute | solution.py:245
  468.8 47.6 %collective-permute-start.31 = (bf16[256,2048]{1,0:T(8,128)(2,1)}, bf16[256,2048]{1,0:T(8,128)(2,1)}, u32[]{:S(2)}, u32[]{:S(2)}) collective-permute-start(bf16[256,2048]{1,0:T(8,128)(2,1)} %add_convert_fusion.6), channel_id=1, source_target_pairs={{0,16},{8,24},{16,0},{24,8},{1,17},{9,25},{17,1},{25,9},{2,18},{10... | collective-permute-start | bytes 3145736 | tf_op jit(solution)/shard_map/dp_contract/ppermute | solution.py:296
  469.4 47.0 %collective-permute-start.32 = (bf16[256,2048]{1,0:T(8,128)(2,1)}, bf16[256,2048]{1,0:T(8,128)(2,1)}, u32[]{:S(2)}, u32[]{:S(2)}) collective-permute-start(bf16[256,2048]{1,0:T(8,128)(2,1)} %add_convert_fusion.6), channel_id=1, source_target_pairs={{0,8},{8,0},{16,24},{24,16},{1,9},{9,1},{17,25},{25,17},{2,10},{10... | collective-permute-start | bytes 3145736 | tf_op jit(solution)/shard_map/dp_contract/ppermute | solution.py:296
  473.2 43.1 %collective-permute-start.33 = (bf16[512,1024]{1,0:T(8,128)(2,1)}, bf16[512,1024]{1,0:T(8,128)(2,1)}, u32[]{:S(2)}, u32[]{:S(2)}) collective-permute-start(bf16[512,1024]{1,0:T(8,128)(2,1)} %add_convert_fusion.5), channel_id=1, source_target_pairs={{0,8},{8,0},{16,24},{24,16},{1,9},{9,1},{17,25},{25,17},{2,10},{10... | collective-permute-start | bytes 3145736 | tf_op jit(solution)/shard_map/dp_expand/ppermute | solution.py:296
  473.9 27.6 %collective-permute-start.26 = (bf16[256,2048]{1,0:T(8,128)(2,1)}, bf16[256,2048]{1,0:T(8,128)(2,1)S(1)}, u32[]{:S(2)}, u32[]{:S(2)}) collective-permute-start(bf16[256,2048]{1,0:T(8,128)(2,1)} %add_convert_fusion.7), channel_id=1, source_target_pairs={{0,2},{1,3},{2,6},{3,7},{6,4},{7,5},{4,0},{5,1},{8,10},{9,11},{10,... | collective-permute-start | bytes 3145736 | tf_op jit(solution)/shard_map/branch_ring1/ppermute | solution.py:241
  501.5 20.1 %collective-permute-start.34 = (bf16[512,1024]{1,0:T(8,128)(2,1)}, bf16[512,1024]{1,0:T(8,128)(2,1)}, u32[]{:S(2)}, u32[]{:S(2)}) collective-permute-start(bf16[512,1024]{1,0:T(8,128)(2,1)} %add_convert_fusion.5), channel_id=1, source_target_pairs={{0,16},{8,24},{16,0},{24,8},{1,17},{9,25},{17,1},{25,9},{2,18},{10... | collective-permute-start | bytes 3145736 | tf_op jit(solution)/shard_map/dp_expand/ppermute | solution.py:296
  505.5 23.6 %collective-permute-start.36 = (bf16[256,2048]{1,0:T(8,128)(2,1)}, bf16[256,2048]{1,0:T(8,128)(2,1)}, u32[]{:S(2)}, u32[]{:S(2)}) collective-permute-start(bf16[256,2048]{1,0:T(8,128)(2,1)} %add_convert_fusion.4), channel_id=1, source_target_pairs={{0,2},{1,3},{2,6},{3,7},{6,4},{7,5},{4,0},{5,1},{8,10},{9,11},{10,... | collective-permute-start | bytes 3145736 | tf_op jit(solution)/shard_map/branch_ring2/ppermute | solution.py:241
  537.4 50.1 %collective-permute-start.37 = (bf16[256,2048]{1,0:T(8,128)(2,1)}, bf16[256,2048]{1,0:T(8,128)(2,1)S(1)}, u32[]{:S(2)}, u32[]{:S(2)}) collective-permute-start(bf16[256,2048]{1,0:T(8,128)(2,1)} %collective-permute-done.31), channel_id=1, source_target_pairs={{0,8},{8,0},{16,24},{24,16},{1,9},{9,1},{17,25},{25,17},{2,10},{10... | collective-permute-start | bytes 3145736 | tf_op jit(solution)/shard_map/dp_contract/ppermute | solution.py:296
  539.9 47.6 %collective-permute-start.38 = (bf16[512,1024]{1,0:T(8,128)(2,1)}, bf16[512,1024]{1,0:T(8,128)(2,1)S(1)}, u32[]{:S(2)}, u32[]{:S(2)}) collective-permute-start(bf16[512,1024]{1,0:T(8,128)(2,1)} %collective-permute-done.33), channel_id=1, source_target_pairs={{0,16},{8,24},{16,0},{24,8},{1,17},{9,25},{17,1},{25,9},{2,18},{10... | collective-permute-start | bytes 3145736 | tf_op jit(solution)/shard_map/dp_expand/ppermute | solution.py:296
  551.7 35.8 %collective-permute-start.39 = (bf16[512,768]{0,1:T(8,128)(2,1)S(1)}, bf16[512,768]{0,1:T(8,128)(2,1)S(1)}, u32[]{:S(2)}, u32[]{:S(2)}) collective-permute-start(bf16[512,768]{0,1:T(8,128)(2,1)S(1)} %constant_dynamic-slice_fusion.5), channel_id=1, source_target_pairs={{0,8},{8,0},{16,24},{24,16},{1,9},{9,1},{17,25},{25,17},{2,10},{10... | collective-permute-start | bytes 2359304 | tf_op jit(solution)/shard_map/dp_projection0/ppermute | solution.py:296
  551.9 35.6 %collective-permute-start.40 = (bf16[512,768]{0,1:T(8,128)(2,1)S(1)}, bf16[512,768]{0,1:T(8,128)(2,1)S(1)}, u32[]{:S(2)}, u32[]{:S(2)}) collective-permute-start(bf16[512,768]{0,1:T(8,128)(2,1)S(1)} %constant_dynamic-slice_fusion.6), channel_id=1, source_target_pairs={{0,16},{8,24},{16,0},{24,8},{1,17},{9,25},{17,1},{25,9},{2,18},{10... | collective-permute-start | bytes 2359304 | tf_op jit(solution)/shard_map/dp_projection1024/ppermute | solution.py:296
  559.1 28.4 %collective-permute-start.41 = (bf16[128,2048]{1,0:T(8,128)(2,1)S(1)}, bf16[128,2048]{1,0:T(8,128)(2,1)S(1)}, u32[]{:S(2)}, u32[]{:S(2)}) collective-permute-start(bf16[128,2048]{1,0:T(8,128)(2,1)S(1)} %constant_dynamic-slice_fusion.7), channel_id=1, source_target_pairs={{0,8},{8,0},{16,24},{24,16},{1,9},{9,1},{17,25},{25,17},{2,10},{10... | collective-permute-start | bytes 1572872 | tf_op jit(solution)/shard_map/dp_output/ppermute | solution.py:296
  587.5 52.3 %collective-permute-start.53 = (bf16[256,2048]{1,0:T(8,128)(2,1)}, bf16[256,2048]{1,0:T(8,128)(2,1)}, u32[]{:S(2)}, u32[]{:S(2)}) collective-permute-start(bf16[256,2048]{1,0:T(8,128)(2,1)} %slice.248), channel_id=1, source_target_pairs={{0,1},{1,0},{2,3},{3,2},{4,5},{5,4},{6,7},{7,6},{8,9},{9,8},{10,11... | collective-permute-start | bytes 3145736 | tf_op jit(solution)/shard_map/ppermute | solution.py:245
  587.9 17.2 %collective-permute-start.42 = (bf16[256,768]{0,1:T(8,128)(2,1)S(1)}, bf16[256,768]{0,1:T(8,128)(2,1)S(1)}, u32[]{:S(2)}, u32[]{:S(2)}) collective-permute-start(bf16[256,768]{0,1:T(8,128)(2,1)S(1)} %constant_dynamic-slice_fusion.8), channel_id=1, source_target_pairs={{0,16},{8,24},{16,0},{24,8},{1,17},{9,25},{17,1},{25,9},{2,18},{10... | collective-permute-start | bytes 1179656 | tf_op jit(solution)/shard_map/dp_projection0/ppermute | solution.py:296
  589.0 16.1 %collective-permute-start.43 = (bf16[256,768]{0,1:T(8,128)(2,1)S(1)}, bf16[256,768]{0,1:T(8,128)(2,1)S(1)}, u32[]{:S(2)}, u32[]{:S(2)}) collective-permute-start(bf16[256,768]{0,1:T(8,128)(2,1)S(1)} %constant_dynamic-slice_fusion.9), channel_id=1, source_target_pairs={{0,8},{8,0},{16,24},{24,16},{1,9},{9,1},{17,25},{25,17},{2,10},{10... | collective-permute-start | bytes 1179656 | tf_op jit(solution)/shard_map/dp_projection1024/ppermute | solution.py:296
  608.1 21.9 %collective-permute-start.45 = (bf16[256,768]{0,1:T(8,128)(2,1)}, bf16[256,768]{0,1:T(8,128)(2,1)}, u32[]{:S(2)}, u32[]{:S(2)}) collective-permute-start(bf16[256,768]{0,1:T(8,128)(2,1)} %get-tuple-element.151), channel_id=1, source_target_pairs={{0,16},{8,24},{16,0},{24,8},{1,17},{9,25},{17,1},{25,9},{2,18},{10... | collective-permute-start | bytes 1179656 | tf_op jit(solution)/shard_map/dp_projection0/ppermute | solution.py:296
  608.9 21.2 %collective-permute-start.46 = (bf16[256,768]{0,1:T(8,128)(2,1)}, bf16[256,768]{0,1:T(8,128)(2,1)}, u32[]{:S(2)}, u32[]{:S(2)}) collective-permute-start(bf16[256,768]{0,1:T(8,128)(2,1)} %get-tuple-element.151), channel_id=1, source_target_pairs={{0,8},{8,0},{16,24},{24,16},{1,9},{9,1},{17,25},{25,17},{2,10},{10... | collective-permute-start | bytes 1179656 | tf_op jit(solution)/shard_map/dp_projection0/ppermute | solution.py:296
  638.8 16.1 %collective-permute-start.51 = (f32[13824]{0:T(1024)S(1)}, f32[13824]{0:T(1024)S(1)}, u32[]{:S(2)}, u32[]{:S(2)}) collective-permute-start(f32[13824]{0:T(1024)S(1)} %pad_maximum_fusion.2), channel_id=1, source_target_pairs={{0,8},{8,0},{16,24},{24,16},{1,9},{9,1},{17,25},{25,17},{2,10},{10... | collective-permute-start | bytes 165896 | tf_op jit(solution)/shard_map/small_sums/ppermute | solution.py:389
  642.5 24.6 %collective-permute-start.54 = (bf16[256,2048]{1,0:T(8,128)(2,1)S(1)}, bf16[256,2048]{1,0:T(8,128)(2,1)}, u32[]{:S(2)}, u32[]{:S(2)}) collective-permute-start(bf16[256,2048]{1,0:T(8,128)(2,1)S(1)} %add_convert_fusion.3), channel_id=1, source_target_pairs={{0,2},{1,3},{2,6},{3,7},{6,4},{7,5},{4,0},{5,1},{8,10},{9,11},{10,... | collective-permute-start | bytes 3145736 | tf_op jit(solution)/shard_map/branch_ring3/ppermute | solution.py:241
  644.1 15.7 %collective-permute-start.58 = (bf16[256,768]{0,1:T(8,128)(2,1)}, bf16[256,768]{0,1:T(8,128)(2,1)S(1)}, u32[]{:S(2)}, u32[]{:S(2)}) collective-permute-start(bf16[256,768]{0,1:T(8,128)(2,1)} %collective-permute-done.45), channel_id=1, source_target_pairs={{0,8},{8,0},{16,24},{24,16},{1,9},{9,1},{17,25},{25,17},{2,10},{10... | collective-permute-start | bytes 1179656 | tf_op jit(solution)/shard_map/dp_projection0/ppermute | solution.py:296
  645.1 14.8 %collective-permute-start.59 = (bf16[256,768]{0,1:T(8,128)(2,1)S(1)}, bf16[256,768]{0,1:T(8,128)(2,1)S(1)}, u32[]{:S(2)}, u32[]{:S(2)}) collective-permute-start(bf16[256,768]{0,1:T(8,128)(2,1)S(1)} %copy-done.36), channel_id=1, source_target_pairs={{0,16},{8,24},{16,0},{24,8},{1,17},{9,25},{17,1},{25,9},{2,18},{10... | collective-permute-start | bytes 1179656 | tf_op jit(solution)/shard_map/dp_projection1024/ppermute | solution.py:296
  659.2 20.2 %collective-permute-start.24 = (bf16[256,2048]{1,0:T(8,128)(2,1)}, bf16[256,2048]{1,0:T(8,128)(2,1)}, u32[]{:S(2)}, u32[]{:S(2)}) collective-permute-start(bf16[256,2048]{1,0:T(8,128)(2,1)} %slice.240), channel_id=1, source_target_pairs={{0,1},{1,0},{2,3},{3,2},{4,5},{5,4},{6,7},{7,6},{8,9},{9,8},{10,11... | collective-permute-start | bytes 3145736 | tf_op jit(solution)/shard_map/ppermute | solution.py:245
  (85 other events, 618.2 us)
Sparse Core Ops, SparseCore 0:
  12.1 94.0 all-gather.3
  107.8 113.9 all-gather.5
  387.8 80.4 all-gather.7
  529.3 91.5 reduce-scatter.1

commit v5 on v4

--- a/solution.py
+++ b/solution.py
@@ -630,12 +630,10 @@
     while exchange.flying:
         exchange.hop()
     with jax.named_scope("small_sums"):
-        sums = small_sum(jnp.concatenate([sums_by_row.reshape(-1), sums_by_width]), ("dp",))
-        sums, branch_arrived = lax.optimization_barrier((sums, branch_arrived))
-        sums_by_width = sums[sums_by_row.size :]
-        sums_by_row = small_sum(
-            sums[: sums_by_row.size].reshape(sums_by_row.shape), ("tensor",)
-        )
+        sums_by_width = small_sum(sums_by_width, ("dp",))
+        sums_by_row = small_sum(sums_by_row, ("dp",))
+        sums_by_row, branch_arrived = lax.optimization_barrier((sums_by_row, branch_arrived))
+        sums_by_row = small_sum(sums_by_row, ("tensor",))
         sums_by_row = lax.dynamic_slice_in_dim(sums_by_row, rank * own_columns, own_columns, 1)
     projection_parts = [
         (start, order, exchange.done[f"projection{start}"]) for start, order in projection_orders

time: 702 us -> 701 us (level)
    ppermute x31, waiting for transfers between devices: 89.3 us -> 97.6 us  [flip_dp(): return lax.ppermute(value, 'dp', [(i, i ^ bit) for i in range(size)])]
    unnamed x135 -> x117, local copies, waits for them, and re-layouts: 18.3 us -> 17.1 us
  transfers between devices with their start and end apart: 66 -> 68, of which waited for: 29 -> 30; matrix products, arithmetic and copies ran while one was open for 41% -> 40% of each run, Pallas kernels for 6% -> 6%
where the time goes in v5:
time: 701 us; the launch traced here: 689 us
  waiting for transfers between devices  261 us (37%)
  matrix products  143 us (20%)
  other arithmetic  79.4 us (11%)
  local copies, waits for them, and re-layouts  74.4 us (11%)
  starting transfers between devices  68.7 us (10%)
  Pallas kernels  38.1 us (5%)
  between operations  24.9 us (4%)
    dot_general x25, matrix products, dot(): lax.dot_general(a, b, (((a_axis,), (b_axis,)), ((), ())), preferred_eleme...  143 us
    ppermute x12, waiting for transfers between devices, ring_step(): return lax.ppermute(value, 'tensor', pairs)  100 us
    ppermute x31, waiting for transfers between devices, flip_dp(): return lax.ppermute(value, 'dp', [(i, i ^ bit) for i in range(size)])  97.6 us
    all_to_all x1, waiting for transfers between devices, shards(): lax.all_to_all(context.reshape(tensor_size, shard_rows, local_width), 'te...  45.2 us
    ppermute x31, starting transfers between devices, flip_dp(): return lax.ppermute(value, 'dp', [(i, i ^ bit) for i in range(size)])  31.5 us
    dynamic_update_slice x13, other arithmetic, put(): lax.dynamic_update_slice(full, block.astype(full.dtype), (row, column))  26.4 us
    pallas_call x1, Pallas kernels, attend_back(): pl.pallas_call(functools.partial(attend_back_kernel, block, local_heads),...  21.6 us
    unnamed x117, local copies, waits for them, and re-layouts  17.1 us
  transfers between devices with their start and end apart: 68, of which 30 were waited for; matrix products, arithmetic and copies ran while one was open for 40% of the time, Pallas kernels for 6%

profile of v5, /device:TPU:0, one launch (start us, length us, event | category | flops | bytes accessed | tf_op | source)
XLA Modules:
  0.0 689.3 jit_solution(372239840170479425)
XLA Ops:
  15.2 7.3 %collective-permute-done = bf16[256,512]{1,0:T(8,128)(2,1)S(1)} collective-permute-done((bf16[256,512]{1,0:T(8,128)(2,1)S(1)}, bf16[256,512]{1,0:T(8,128)(2,1)S(1)}, u32[]{:S(2)}, u32[]{:S(2)}) %collective-permute-start) | collective-permute-done | bytes 262176 | tf_op jit(solution)/shard_map/weight_ring/ppermute | solution.py:241
  28.3 14.2 %collective-permute-done.4 = bf16[256,512]{1,0:T(8,128)(2,1)S(1)} collective-permute-done((bf16[256,512]{1,0:T(8,128)(2,1)S(1)}, bf16[256,512]{1,0:T(8,128)(2,1)S(1)}, u32[]{:S(2)}, u32[]{:S(2)}) %collective-permute-start.4) | collective-permute-done | bytes 262176 | tf_op jit(solution)/shard_map/weight_ring/ppermute | solution.py:241
  45.7 17.1 %collective-permute-done.5 = bf16[256,512]{1,0:T(8,128)(2,1)S(1)} collective-permute-done((bf16[256,512]{1,0:T(8,128)(2,1)S(1)}, bf16[256,512]{1,0:T(8,128)(2,1)S(1)}, u32[]{:S(2)}, u32[]{:S(2)}) %collective-permute-start.5) | collective-permute-done | bytes 262176 | tf_op jit(solution)/shard_map/weight_ring/ppermute | solution.py:241
  66.7 11.0 %collective-permute-done.6 = bf16[512,512]{1,0:T(8,128)(2,1)S(1)} collective-permute-done((bf16[512,512]{1,0:T(8,128)(2,1)S(1)}, bf16[512,512]{1,0:T(8,128)(2,1)S(1)}, u32[]{:S(2)}, u32[]{:S(2)}) %collective-permute-start.6) | collective-permute-done | bytes 524320 | tf_op jit(solution)/shard_map/weight_dp/ppermute | solution.py:296
  77.7 9.9 %collective-permute-done.2 = bf16[512,512]{1,0:T(8,128)(2,1)} collective-permute-done((bf16[512,512]{1,0:T(8,128)(2,1)S(1)}, bf16[512,512]{1,0:T(8,128)(2,1)}, u32[]{:S(2)}, u32[]{:S(2)}) %collective-permute-start.2) | collective-permute-done | bytes 524320 | tf_op jit(solution)/shard_map/weight_dp/ppermute | solution.py:296
  89.4 3.7 collective-permute-done.3
  99.1 4.9 copy.77
  106.7 10.1 %add_convert_fusion.q_ref.k_ref.v_ref = bf16[2048,768]{1,0:T(8,128)(2,1)S(1)} fusion(f32[768]{0:T(1024)S(1)} %pad_maximum_fusion.2, bf16[2048,2048]{1,0:T(8,128)(2,1)} %all-gather.4.cloned.1.call-done, bf16[2048,768]{0,1:T(8,128)(2,1)} %bitcast.177), kind=kOutput, calls=%fused_computation.6 | convolution fusion | flops 6445596672 | bytes 14683136 | tf_op jit(solution)/shard_map/dot_general | solution.py:430
  116.8 16.5 %shard_map.686 = (bf16[2048,256]{1,0:T(8,128)(2,1)}, f32[2,1,2048]{2,1,0:T(1,128)S(1)}) custom-call(s32[2]{0:T(128)S(1)} %get-tuple-element.156.bounds_ref, bf16[2048,768]{1,0:T(8,128)(2,1)S(1)} %add_convert_fusion.q_ref.k_ref.v_ref, bf16[2048,768]{1,0:T(8,128)(2,1)S(1)} %add_convert_fusion.q_ref.k_ref.v_ref, ...), custom_call_target="tpu_custom_call" | custom-call | flops 4294967296 | bytes 4194304 | tf_op jit(solution)/shard_map/pallas_call | solution.py:73
  133.3 14.4 %all-to-all-start = ((bf16[8,256,256]{2,1,0:T(8,128)(2,1)}), bf16[8,256,256]{2,1,0:T(8,128)(2,1)S(1)}, u32[]{:S(2)}, u32[]{:S(2)}) async-start(bf16[8,256,256]{2,1,0:T(8,128)(2,1)} %bitcast.4), calls=%async_computation | async-start | bytes 2097152 | tf_op jit(solution)/shard_map/all_to_all | solution.py:485
  157.6 45.2 %all-to-all-done = bf16[8,256,256]{2,1,0:T(8,128)(2,1)S(1)} async-done(((bf16[8,256,256]{2,1,0:T(8,128)(2,1)}), bf16[8,256,256]{2,1,0:T(8,128)(2,1)S(1)}, u32[]{:S(2)}, u32[]{:S(2)}) %all-to-all-start) | async-done | bytes 1048608 | tf_op jit(solution)/shard_map/all_to_all | solution.py:485
  206.5 3.7 fusion.133
  212.4 9.5 %all-gather.6.cloned.1.call-done = bf16[2048,2048]{1,0:T(8,128)(2,1)} async-done(((bf16[256,2048]{1,0:T(8,128)(2,1)}), bf16[2048,2048]{1,0:T(8,128)(2,1)}) %all-gather.6.cloned.1.call-update) | async-done | bytes 8388624 | tf_op jit(solution)/shard_map/all_gather | solution.py:480
  223.8 4.3 constant_dynamic-slice_fusion.17
  229.4 5.0 fusion.47
  242.4 7.9 %collective-permute-done.12 = bf16[256,2048]{1,0:T(8,128)(2,1)S(1)} collective-permute-done((bf16[256,2048]{1,0:T(8,128)(2,1)}, bf16[256,2048]{1,0:T(8,128)(2,1)S(1)}, u32[]{:S(2)}, u32[]{:S(2)}) %collective-permute-start.12) | collective-permute-done | bytes 1048608 | tf_op jit(solution)/shard_map/mixed_ring1/ppermute | solution.py:241
  256.6 6.7 fusion.31
  263.2 4.6 convolution_convert_fusion.7
  268.0 9.1 %collective-permute-done.13 = bf16[256,2048]{1,0:T(8,128)(2,1)S(1)} collective-permute-done((bf16[256,2048]{1,0:T(8,128)(2,1)S(1)}, bf16[256,2048]{1,0:T(8,128)(2,1)S(1)}, u32[]{:S(2)}, u32[]{:S(2)}) %collective-permute-start.13) | collective-permute-done | bytes 1048608 | tf_op jit(solution)/shard_map/mixed_ring2/ppermute | solution.py:241
  284.9 5.7 fusion.38
  290.6 4.6 convolution_convert_fusion.6
  296.0 8.3 %collective-permute-done.15 = bf16[256,2048]{1,0:T(8,128)(2,1)S(1)} collective-permute-done((bf16[256,2048]{1,0:T(8,128)(2,1)S(1)}, bf16[256,2048]{1,0:T(8,128)(2,1)S(1)}, u32[]{:S(2)}, u32[]{:S(2)}) %collective-permute-start.15) | collective-permute-done | bytes 1048608 | tf_op jit(solution)/shard_map/mixed_ring3/ppermute | solution.py:241
  304.6 21.8 %collective-permute-done.20 = bf16[256,2048]{1,0:T(8,128)(2,1)S(1)} collective-permute-done((bf16[256,2048]{1,0:T(8,128)(2,1)S(1)}, bf16[256,2048]{1,0:T(8,128)(2,1)S(1)}, u32[]{:S(2)}, u32[]{:S(2)}) %collective-permute-start.20) | collective-permute-done | bytes 1048608 | tf_op jit(solution)/shard_map/grad_mixed_ring1/ppermute | solution.py:241
  330.1 7.9 %multiply_convert_fusion.4 = (bf16[512,1024]{1,0:T(8,128)(2,1)S(1)}, bf16[512,1024]{1,0:T(8,128)(2,1)S(1)}, bf16[512,1024]{1,0:T(8,128)(2,1)S(1)}, bf16[512,1024]{1,0:T(8,128)(2,1)S(1)}, f32[512,1024]{1,0:T(8,128)}) fusion(f32[1024]{0:T(1024)S(1)} %copy-done.52, f32[512,1024]{1,0:T(8,128)} %copy-done.54, f32[512,1024]{1,0:T(8,128)} %fusion.63, ...), kind=kOutput, calls=%fused_computation.128 | convolution fusion | flops 2168455168 | bytes 18878464 | tf_op jit(solution)/shard_map/mixed_ring3/dot_general | solution.py:430
  338.0 8.2 %fusion.45 = bf16[512,1024]{1,0:T(8,128)(2,1)S(1)} fusion(f32[512,1024]{1,0:T(8,128)} %get-tuple-element.198, bf16[1024,2048]{1,0:T(8,128)(2,1)} %param.75, bf16[256,2048]{1,0:T(8,128)(2,1)S(1)} %get-tuple-element.163, bf16[256,2048]{1,0:T(8,128)(2,1)S(1)} %get-tuple-element.158, f32[1024]{0:T(1024)S(1)} %copy-done.52), kind=kOutput, calls=%fused_computation.80 | convolution fusion | flops 2162688000 | bytes 9441280 | tf_op jit(solution)/shard_map/mixed_ring3/dot_general | solution.py:430
  350.0 4.1 collective-permute-done.22
  356.0 10.8 %multiply_convert_fusion.1 = bf16[1024,2048]{1,0:T(8,128)(2,1)} fusion(bf16[2048,1024]{1,0:T(8,128)(2,1)S(1)} %bitcast.176, bf16[2048,2048]{1,0:T(8,128)(2,1)S(1)} %bitcast.174, f32[]{:T(128)S(6)} %div.65), kind=kOutput, calls=%fused_computation.2 | convolution fusion | flops 8594128896 | bytes 16777220 | tf_op jit(solution)/shard_map/contract_gradient/dot_general | solution.py:430
  366.9 10.8 %multiply_convert_fusion = bf16[2048,1024]{1,0:T(8,128)(2,1)} fusion(bf16[2048,2048]{1,0:T(8,128)(2,1)S(1)} %bitcast.175, bf16[2048,1024]{1,0:T(8,128)(2,1)S(1)} %bitcast.171, f32[]{:T(128)S(6)} %div.65), kind=kOutput, calls=%fused_computation.1 | convolution fusion | flops 8594128896 | bytes 16777220 | tf_op jit(solution)/shard_map/expand_gradient/dot_general | solution.py:430
  395.2 5.2 convolution_convert_fusion.3
  401.6 3.8 convolution_convert_fusion.4
  414.1 23.4 %collective-permute-done.27 = bf16[512,2048]{1,0:T(8,128)(2,1)S(1)} collective-permute-done((bf16[512,2048]{1,0:T(8,128)(2,1)S(1)}, bf16[512,2048]{1,0:T(8,128)(2,1)S(1)}, u32[]{:S(2)}, u32[]{:S(2)}) %collective-permute-start.27) | collective-permute-done | bytes 2097184 | tf_op jit(solution)/shard_map/dp_contract/ppermute | solution.py:296
  448.8 14.6 %collective-permute-done.30 = bf16[512,1024]{1,0:T(8,128)(2,1)} collective-permute-done((bf16[512,1024]{1,0:T(8,128)(2,1)}, bf16[512,1024]{1,0:T(8,128)(2,1)}, u32[]{:S(2)}, u32[]{:S(2)}) %collective-permute-start.30) | collective-permute-done | bytes 1048608 | tf_op jit(solution)/shard_map/dp_expand/ppermute | solution.py:296
  463.3 3.7 collective-permute-done.29
  475.7 5.8 convolution_convert_fusion.9.grad_ref
  481.5 21.6 %shard_map.687 = bf16[2048,768]{1,0:T(8,128)(2,1)S(1)} custom-call(s32[2]{0:T(128)S(1)} %get-tuple-element.156.bounds_ref, bf16[2048,768]{1,0:T(8,128)(2,1)} %copy-done.4, bf16[2048,768]{1,0:T(8,128)(2,1)} %copy-done.4, bf16[2048,768]{1,0:T(8,128)(2,1)} %copy-done.4, bf16[2048,256]{1,0:T(8,128)(2,1)S(1)} %convolution_convert_fusion.9.grad_ref, ...), custom_call_target="tpu_custom_call" | custom-call | flops 10737418240 | bytes 8388608 | tf_op jit(solution)/shard_map/pallas_call | solution.py:174
  503.8 4.2 add_convert_fusion.4
  509.3 9.3 %convolution_convert_fusion = bf16[2048,2048]{1,0:T(8,128)(2,1)} fusion(bf16[2048,768]{1,0:T(8,128)(2,1)S(1)} %shard_map.687, bf16[2048,768]{0,1:T(8,128)(2,1)S(1)} %bitcast.178), kind=kOutput, calls=%fused_computation.3 | convolution fusion | flops 6446645248 | bytes 14680064 | tf_op jit(solution)/shard_map/normed_terms/dot_general | solution.py:430
  518.6 5.2 collective-permute-done.31
  523.8 5.9 collective-permute-done.36
  542.8 6.3 fusion.5
  550.7 9.6 %multiply_convert_fusion.2 = bf16[2048,768]{0,1:T(8,128)(2,1)S(1)} fusion(bf16[2048,2048]{1,0:T(8,128)(2,1)} %all-gather.4.cloned.1.call-done, bf16[2048,768]{1,0:T(8,128)(2,1)S(1)} %copy-done.3, f32[]{:T(128)S(6)} %div.65), kind=kOutput, calls=%fused_computation.5 | convolution fusion | flops 6445596672 | bytes 14680068 | tf_op jit(solution)/shard_map/projection_gradient/dot_general | solution.py:430
  564.9 4.5 broadcast_in_dim.159
  572.2 4.5 broadcast_in_dim.160
  590.8 8.3 %collective-permute-done.37 = bf16[256,2048]{1,0:T(8,128)(2,1)S(1)} collective-permute-done((bf16[256,2048]{1,0:T(8,128)(2,1)}, bf16[256,2048]{1,0:T(8,128)(2,1)S(1)}, u32[]{:S(2)}, u32[]{:S(2)}) %collective-permute-start.37) | collective-permute-done | bytes 1048608 | tf_op jit(solution)/shard_map/dp_contract/ppermute | solution.py:296
  608.4 5.5 collective-permute-done.42
  631.0 8.9 %collective-permute-done.46 = bf16[256,768]{0,1:T(8,128)(2,1)S(1)} collective-permute-done((bf16[256,768]{0,1:T(8,128)(2,1)}, bf16[256,768]{0,1:T(8,128)(2,1)S(1)}, u32[]{:S(2)}, u32[]{:S(2)}) %collective-permute-start.46) | collective-permute-done | bytes 393248 | tf_op jit(solution)/shard_map/dp_projection0/ppermute | solution.py:296
  665.5 4.2 collective-permute-start.56
  670.5 5.4 copy.78
  (382 shorter events, 217.8 us)
Async XLA Ops:
  7.2 99.4 %all-gather.4.cloned.1.call-start = ((), (), s32[]{:S(2)}) async-start(), calls=%async_computation.2 | async-start | bytes 9437184 | tf_op jit(solution)/shard_map/all_gather | solution.py:452
  12.0 209.8 %all-gather.6.cloned.1.call-start = ((), (), s32[]{:S(2)}) async-start(), calls=%async_computation.3 | async-start | bytes 9437184 | tf_op jit(solution)/shard_map/all_gather | solution.py:480
  22.5 20.0 %collective-permute-start.4 = (bf16[256,512]{1,0:T(8,128)(2,1)S(1)}, bf16[256,512]{1,0:T(8,128)(2,1)S(1)}, u32[]{:S(2)}, u32[]{:S(2)}) collective-permute-start(bf16[256,512]{1,0:T(8,128)(2,1)S(1)} %collective-permute-done), channel_id=1, source_target_pairs={{0,2},{1,3},{2,6},{3,7},{6,4},{7,5},{4,0},{5,1},{8,10},{9,11},{10,... | collective-permute-start | bytes 786440 | tf_op jit(solution)/shard_map/weight_ring/ppermute | solution.py:241
  26.8 38.1 %collective-permute-start.1 = (bf16[512,512]{1,0:T(8,128)(2,1)S(1)}, bf16[512,512]{1,0:T(8,128)(2,1)S(1)}, u32[]{:S(2)}, u32[]{:S(2)}) collective-permute-start(bf16[512,512]{1,0:T(8,128)(2,1)S(1)} %get-tuple-element.176), channel_id=1, source_target_pairs={{0,8},{8,0},{16,24},{24,16},{1,9},{9,1},{17,25},{25,17},{2,10},{10... | collective-permute-start | bytes 1572872 | tf_op jit(solution)/shard_map/weight_dp/ppermute | solution.py:296
  42.5 20.2 %collective-permute-start.5 = (bf16[256,512]{1,0:T(8,128)(2,1)S(1)}, bf16[256,512]{1,0:T(8,128)(2,1)S(1)}, u32[]{:S(2)}, u32[]{:S(2)}) collective-permute-start(bf16[256,512]{1,0:T(8,128)(2,1)S(1)} %collective-permute-done.4), channel_id=1, source_target_pairs={{0,2},{1,3},{2,6},{3,7},{6,4},{7,5},{4,0},{5,1},{8,10},{9,11},{10,... | collective-permute-start | bytes 786440 | tf_op jit(solution)/shard_map/weight_ring/ppermute | solution.py:241
  62.8 14.9 %collective-permute-start.6 = (bf16[512,512]{1,0:T(8,128)(2,1)S(1)}, bf16[512,512]{1,0:T(8,128)(2,1)S(1)}, u32[]{:S(2)}, u32[]{:S(2)}) collective-permute-start(bf16[512,512]{1,0:T(8,128)(2,1)S(1)} %constant_dynamic-update-slice_fusion.12), channel_id=1, source_target_pairs={{0,16},{8,24},{16,0},{24,8},{1,17},{9,25},{17,1},{25,9},{2,18},{10... | collective-permute-start | bytes 1572872 | tf_op jit(solution)/shard_map/weight_dp/ppermute | solution.py:296
  62.9 24.7 %collective-permute-start.2 = (bf16[512,512]{1,0:T(8,128)(2,1)S(1)}, bf16[512,512]{1,0:T(8,128)(2,1)}, u32[]{:S(2)}, u32[]{:S(2)}) collective-permute-start(bf16[512,512]{1,0:T(8,128)(2,1)S(1)} %get-tuple-element.176), channel_id=1, source_target_pairs={{0,16},{8,24},{16,0},{24,8},{1,17},{9,25},{17,1},{25,9},{2,18},{10... | collective-permute-start | bytes 1572872 | tf_op jit(solution)/shard_map/weight_dp/ppermute | solution.py:296
  64.9 28.3 %collective-permute-start.3 = (bf16[512,512]{1,0:T(8,128)(2,1)S(1)}, bf16[512,512]{1,0:T(8,128)(2,1)}, u32[]{:S(2)}, u32[]{:S(2)}) collective-permute-start(bf16[512,512]{1,0:T(8,128)(2,1)S(1)} %collective-permute-done.1), channel_id=1, source_target_pairs={{0,16},{8,24},{16,0},{24,8},{1,17},{9,25},{17,1},{25,9},{2,18},{10... | collective-permute-start | bytes 1572872 | tf_op jit(solution)/shard_map/weight_dp/ppermute | solution.py:296
  65.0 31.8 %collective-permute-start.7 = (bf16[512,512]{1,0:T(8,128)(2,1)S(1)}, bf16[512,512]{1,0:T(8,128)(2,1)S(1)}, u32[]{:S(2)}, u32[]{:S(2)}) collective-permute-start(bf16[512,512]{1,0:T(8,128)(2,1)S(1)} %constant_dynamic-update-slice_fusion.12), channel_id=1, source_target_pairs={{0,8},{8,0},{16,24},{24,16},{1,9},{9,1},{17,25},{25,17},{2,10},{10... | collective-permute-start | bytes 1572872 | tf_op jit(solution)/shard_map/weight_dp/ppermute | solution.py:296
  77.7 19.8 %collective-permute-start.8 = (bf16[512,512]{1,0:T(8,128)(2,1)S(1)}, bf16[512,512]{1,0:T(8,128)(2,1)S(1)}, u32[]{:S(2)}, u32[]{:S(2)}) collective-permute-start(bf16[512,512]{1,0:T(8,128)(2,1)S(1)} %collective-permute-done.6), channel_id=1, source_target_pairs={{0,8},{8,0},{16,24},{24,16},{1,9},{9,1},{17,25},{25,17},{2,10},{10... | collective-permute-start | bytes 1572872 | tf_op jit(solution)/shard_map/weight_dp/ppermute | solution.py:296
  133.3 69.4 %all-to-all-start = ((bf16[8,256,256]{2,1,0:T(8,128)(2,1)}), bf16[8,256,256]{2,1,0:T(8,128)(2,1)S(1)}, u32[]{:S(2)}, u32[]{:S(2)}) async-start(bf16[8,256,256]{2,1,0:T(8,128)(2,1)} %bitcast.4), calls=%async_computation | async-start | bytes 2097152 | tf_op jit(solution)/shard_map/all_to_all | solution.py:485
  147.7 327.8 %all-gather.8.cloned.1.call-start = ((), (), s32[]{:S(2)}) async-start(), calls=%async_computation.4 | async-start | bytes 9437184 | tf_op jit(solution)/shard_map/grad_hidden_gather/all_gather | solution.py:554
  223.5 26.7 %collective-permute-start.12 = (bf16[256,2048]{1,0:T(8,128)(2,1)}, bf16[256,2048]{1,0:T(8,128)(2,1)S(1)}, u32[]{:S(2)}, u32[]{:S(2)}) collective-permute-start(bf16[256,2048]{1,0:T(8,128)(2,1)} %add_convert_fusion.11), channel_id=1, source_target_pairs={{0,2},{1,3},{2,6},{3,7},{6,4},{7,5},{4,0},{5,1},{8,10},{9,11},{10,... | collective-permute-start | bytes 3145736 | tf_op jit(solution)/shard_map/mixed_ring1/ppermute | solution.py:241
  241.5 139.3 %collective-permute-start.11 = (bf16[256,2048]{1,0:T(8,128)(2,1)}, bf16[256,2048]{1,0:T(8,128)(2,1)}, u32[]{:S(2)}, u32[]{:S(2)}) collective-permute-start(bf16[256,2048]{1,0:T(8,128)(2,1)} %slice.209), channel_id=1, source_target_pairs={{0,1},{1,0},{2,3},{3,2},{4,5},{5,4},{6,7},{7,6},{8,9},{9,8},{10,11... | collective-permute-start | bytes 3145736 | tf_op jit(solution)/shard_map/grad_mixed_own/ppermute | solution.py:245
  250.3 26.8 %collective-permute-start.13 = (bf16[256,2048]{1,0:T(8,128)(2,1)S(1)}, bf16[256,2048]{1,0:T(8,128)(2,1)S(1)}, u32[]{:S(2)}, u32[]{:S(2)}) collective-permute-start(bf16[256,2048]{1,0:T(8,128)(2,1)S(1)} %collective-permute-done.12), channel_id=1, source_target_pairs={{0,2},{1,3},{2,6},{3,7},{6,4},{7,5},{4,0},{5,1},{8,10},{9,11},{10,... | collective-permute-start | bytes 3145736 | tf_op jit(solution)/shard_map/mixed_ring2/ppermute | solution.py:241
  277.0 18.2 %collective-permute-start.19 = (bf16[256,2048]{1,0:T(8,128)(2,1)S(1)}, bf16[256,2048]{1,0:T(8,128)(2,1)S(1)}, u32[]{:S(2)}, u32[]{:S(2)}) collective-permute-start(bf16[256,2048]{1,0:T(8,128)(2,1)S(1)} %slice.213), channel_id=1, source_target_pairs={{0,1},{1,0},{2,3},{3,2},{4,5},{5,4},{6,7},{7,6},{8,9},{9,8},{10,11... | collective-permute-start | bytes 3145736 | tf_op jit(solution)/shard_map/grad_mixed_ring1/ppermute | solution.py:245
  277.0 27.3 %collective-permute-start.15 = (bf16[256,2048]{1,0:T(8,128)(2,1)S(1)}, bf16[256,2048]{1,0:T(8,128)(2,1)S(1)}, u32[]{:S(2)}, u32[]{:S(2)}) collective-permute-start(bf16[256,2048]{1,0:T(8,128)(2,1)S(1)} %collective-permute-done.13), channel_id=1, source_target_pairs={{0,2},{1,3},{2,6},{3,7},{6,4},{7,5},{4,0},{5,1},{8,10},{9,11},{10,... | collective-permute-start | bytes 3145736 | tf_op jit(solution)/shard_map/mixed_ring3/ppermute | solution.py:241
  295.7 30.7 %collective-permute-start.20 = (bf16[256,2048]{1,0:T(8,128)(2,1)S(1)}, bf16[256,2048]{1,0:T(8,128)(2,1)S(1)}, u32[]{:S(2)}, u32[]{:S(2)}) collective-permute-start(bf16[256,2048]{1,0:T(8,128)(2,1)S(1)} %add_convert_fusion.10), channel_id=1, source_target_pairs={{0,2},{1,3},{2,6},{3,7},{6,4},{7,5},{4,0},{5,1},{8,10},{9,11},{10,... | collective-permute-start | bytes 3145736 | tf_op jit(solution)/shard_map/grad_mixed_ring1/ppermute | solution.py:241
  295.9 30.5 %collective-permute-start.18 = (bf16[256,2048]{1,0:T(8,128)(2,1)S(1)}, bf16[256,2048]{1,0:T(8,128)(2,1)S(1)}, u32[]{:S(2)}, u32[]{:S(2)}) collective-permute-start(bf16[256,2048]{1,0:T(8,128)(2,1)S(1)} %slice.211), channel_id=1, source_target_pairs={{0,1},{1,0},{2,3},{3,2},{4,5},{5,4},{6,7},{7,6},{8,9},{9,8},{10,11... | collective-permute-start | bytes 3145736 | tf_op jit(solution)/shard_map/grad_mixed_ring2/ppermute | solution.py:245
  304.3 23.8 %collective-permute-start.16 = (bf16[256,2048]{1,0:T(8,128)(2,1)S(1)}, bf16[256,2048]{1,0:T(8,128)(2,1)S(1)}, u32[]{:S(2)}, u32[]{:S(2)}) collective-permute-start(bf16[256,2048]{1,0:T(8,128)(2,1)S(1)} %collective-permute-done.15), channel_id=1, source_target_pairs={{0,1},{1,0},{2,3},{3,2},{4,5},{5,4},{6,7},{7,6},{8,9},{9,8},{10,11... | collective-permute-start | bytes 3145736 | tf_op jit(solution)/shard_map/mixed_ring3/ppermute | solution.py:245
  327.9 26.2 %collective-permute-start.22 = (bf16[256,2048]{1,0:T(8,128)(2,1)}, bf16[256,2048]{1,0:T(8,128)(2,1)}, u32[]{:S(2)}, u32[]{:S(2)}) collective-permute-start(bf16[256,2048]{1,0:T(8,128)(2,1)} %add_convert_fusion.9), channel_id=1, source_target_pairs={{0,2},{1,3},{2,6},{3,7},{6,4},{7,5},{4,0},{5,1},{8,10},{9,11},{10,... | collective-permute-start | bytes 3145736 | tf_op jit(solution)/shard_map/grad_mixed_ring2/ppermute | solution.py:241
  355.7 25.1 %collective-permute-start.23 = (bf16[256,2048]{1,0:T(8,128)(2,1)S(1)}, bf16[256,2048]{1,0:T(8,128)(2,1)S(1)}, u32[]{:S(2)}, u32[]{:S(2)}) collective-permute-start(bf16[256,2048]{1,0:T(8,128)(2,1)S(1)} %add_convert_fusion.8), channel_id=1, source_target_pairs={{0,2},{1,3},{2,6},{3,7},{6,4},{7,5},{4,0},{5,1},{8,10},{9,11},{10,... | collective-permute-start | bytes 3145736 | tf_op jit(solution)/shard_map/grad_mixed_ring3/ppermute | solution.py:241
  389.5 234.2 %reduce-scatter.2.cloned.1.call-start = ((), (), s32[]{:S(2)}) async-start(), calls=%async_computation.5 | async-start | bytes 9437184 | tf_op jit(solution)/shard_map/grad_normed_scatter/reduce_scatter | solution.py:590
  391.9 45.6 %collective-permute-start.27 = (bf16[512,2048]{1,0:T(8,128)(2,1)S(1)}, bf16[512,2048]{1,0:T(8,128)(2,1)S(1)}, u32[]{:S(2)}, u32[]{:S(2)}) collective-permute-start(bf16[512,2048]{1,0:T(8,128)(2,1)S(1)} %constant_dynamic-slice_fusion.1), channel_id=1, source_target_pairs={{0,8},{8,0},{16,24},{24,16},{1,9},{9,1},{17,25},{25,17},{2,10},{10... | collective-permute-start | bytes 6291464 | tf_op jit(solution)/shard_map/dp_contract/ppermute | solution.py:296
  393.7 45.3 %collective-permute-start.28 = (bf16[1024,1024]{1,0:T(8,128)(2,1)S(1)}, bf16[1024,1024]{1,0:T(8,128)(2,1)S(1)}, u32[]{:S(2)}, u32[]{:S(2)}) collective-permute-start(bf16[1024,1024]{1,0:T(8,128)(2,1)S(1)} %constant_dynamic-slice_fusion.2), channel_id=1, source_target_pairs={{0,16},{8,24},{16,0},{24,8},{1,17},{9,25},{17,1},{25,9},{2,18},{10... | collective-permute-start | bytes 6291464 | tf_op jit(solution)/shard_map/dp_expand/ppermute | solution.py:296
  441.1 22.2 %collective-permute-start.30 = (bf16[512,1024]{1,0:T(8,128)(2,1)}, bf16[512,1024]{1,0:T(8,128)(2,1)}, u32[]{:S(2)}, u32[]{:S(2)}) collective-permute-start(bf16[512,1024]{1,0:T(8,128)(2,1)} %constant_dynamic-slice_fusion.4), channel_id=1, source_target_pairs={{0,8},{8,0},{16,24},{24,16},{1,9},{9,1},{17,25},{25,17},{2,10},{10... | collective-permute-start | bytes 3145736 | tf_op jit(solution)/shard_map/dp_expand/ppermute | solution.py:296
  444.8 22.2 %collective-permute-start.29 = (bf16[256,2048]{1,0:T(8,128)(2,1)}, bf16[256,2048]{1,0:T(8,128)(2,1)}, u32[]{:S(2)}, u32[]{:S(2)}) collective-permute-start(bf16[256,2048]{1,0:T(8,128)(2,1)} %constant_dynamic-slice_fusion.3), channel_id=1, source_target_pairs={{0,16},{8,24},{16,0},{24,8},{1,17},{9,25},{17,1},{25,9},{2,18},{10... | collective-permute-start | bytes 3145736 | tf_op jit(solution)/shard_map/dp_contract/ppermute | solution.py:296
  448.8 55.0 %collective-permute-start.35 = (bf16[256,2048]{1,0:T(8,128)(2,1)}, bf16[256,2048]{1,0:T(8,128)(2,1)}, u32[]{:S(2)}, u32[]{:S(2)}) collective-permute-start(bf16[256,2048]{1,0:T(8,128)(2,1)} %slice.237), channel_id=1, source_target_pairs={{0,1},{1,0},{2,3},{3,2},{4,5},{5,4},{6,7},{7,6},{8,9},{9,8},{10,11... | collective-permute-start | bytes 3145736 | tf_op jit(solution)/shard_map/ppermute | solution.py:245
  469.5 49.1 %collective-permute-start.34 = (bf16[512,1024]{1,0:T(8,128)(2,1)}, bf16[512,1024]{1,0:T(8,128)(2,1)}, u32[]{:S(2)}, u32[]{:S(2)}) collective-permute-start(bf16[512,1024]{1,0:T(8,128)(2,1)} %add_convert_fusion.5), channel_id=1, source_target_pairs={{0,16},{8,24},{16,0},{24,8},{1,17},{9,25},{17,1},{25,9},{2,18},{10... | collective-permute-start | bytes 3145736 | tf_op jit(solution)/shard_map/dp_expand/ppermute | solution.py:296
  471.0 47.6 %collective-permute-start.33 = (bf16[512,1024]{1,0:T(8,128)(2,1)}, bf16[512,1024]{1,0:T(8,128)(2,1)}, u32[]{:S(2)}, u32[]{:S(2)}) collective-permute-start(bf16[512,1024]{1,0:T(8,128)(2,1)} %add_convert_fusion.5), channel_id=1, source_target_pairs={{0,8},{8,0},{16,24},{24,16},{1,9},{9,1},{17,25},{25,17},{2,10},{10... | collective-permute-start | bytes 3145736 | tf_op jit(solution)/shard_map/dp_expand/ppermute | solution.py:296
  474.8 43.9 %collective-permute-start.32 = (bf16[256,2048]{1,0:T(8,128)(2,1)}, bf16[256,2048]{1,0:T(8,128)(2,1)}, u32[]{:S(2)}, u32[]{:S(2)}) collective-permute-start(bf16[256,2048]{1,0:T(8,128)(2,1)} %add_convert_fusion.6), channel_id=1, source_target_pairs={{0,8},{8,0},{16,24},{24,16},{1,9},{9,1},{17,25},{25,17},{2,10},{10... | collective-permute-start | bytes 3145736 | tf_op jit(solution)/shard_map/dp_contract/ppermute | solution.py:296
  475.6 27.6 %collective-permute-start.26 = (bf16[256,2048]{1,0:T(8,128)(2,1)}, bf16[256,2048]{1,0:T(8,128)(2,1)S(1)}, u32[]{:S(2)}, u32[]{:S(2)}) collective-permute-start(bf16[256,2048]{1,0:T(8,128)(2,1)} %add_convert_fusion.7), channel_id=1, source_target_pairs={{0,2},{1,3},{2,6},{3,7},{6,4},{7,5},{4,0},{5,1},{8,10},{9,11},{10,... | collective-permute-start | bytes 3145736 | tf_op jit(solution)/shard_map/branch_ring1/ppermute | solution.py:241
  503.2 20.6 %collective-permute-start.31 = (bf16[256,2048]{1,0:T(8,128)(2,1)}, bf16[256,2048]{1,0:T(8,128)(2,1)}, u32[]{:S(2)}, u32[]{:S(2)}) collective-permute-start(bf16[256,2048]{1,0:T(8,128)(2,1)} %add_convert_fusion.6), channel_id=1, source_target_pairs={{0,16},{8,24},{16,0},{24,8},{1,17},{9,25},{17,1},{25,9},{2,18},{10... | collective-permute-start | bytes 3145736 | tf_op jit(solution)/shard_map/dp_contract/ppermute | solution.py:296
  508.0 21.7 %collective-permute-start.36 = (bf16[256,2048]{1,0:T(8,128)(2,1)}, bf16[256,2048]{1,0:T(8,128)(2,1)}, u32[]{:S(2)}, u32[]{:S(2)}) collective-permute-start(bf16[256,2048]{1,0:T(8,128)(2,1)} %add_convert_fusion.4), channel_id=1, source_target_pairs={{0,2},{1,3},{2,6},{3,7},{6,4},{7,5},{4,0},{5,1},{8,10},{9,11},{10,... | collective-permute-start | bytes 3145736 | tf_op jit(solution)/shard_map/branch_ring2/ppermute | solution.py:241
  549.2 41.5 %collective-permute-start.41 = (bf16[128,2048]{1,0:T(8,128)(2,1)S(1)}, bf16[128,2048]{1,0:T(8,128)(2,1)S(1)}, u32[]{:S(2)}, u32[]{:S(2)}) collective-permute-start(bf16[128,2048]{1,0:T(8,128)(2,1)S(1)} %constant_dynamic-slice_fusion.7), channel_id=1, source_target_pairs={{0,8},{8,0},{16,24},{24,16},{1,9},{9,1},{17,25},{25,17},{2,10},{10... | collective-permute-start | bytes 1572872 | tf_op jit(solution)/shard_map/dp_output/ppermute | solution.py:296
  560.7 30.1 %collective-permute-start.39 = (bf16[512,768]{0,1:T(8,128)(2,1)S(1)}, bf16[512,768]{0,1:T(8,128)(2,1)S(1)}, u32[]{:S(2)}, u32[]{:S(2)}) collective-permute-start(bf16[512,768]{0,1:T(8,128)(2,1)S(1)} %constant_dynamic-slice_fusion.5), channel_id=1, source_target_pairs={{0,8},{8,0},{16,24},{24,16},{1,9},{9,1},{17,25},{25,17},{2,10},{10... | collective-permute-start | bytes 2359304 | tf_op jit(solution)/shard_map/dp_projection0/ppermute | solution.py:296
  561.3 29.4 %collective-permute-start.40 = (bf16[512,768]{0,1:T(8,128)(2,1)S(1)}, bf16[512,768]{0,1:T(8,128)(2,1)S(1)}, u32[]{:S(2)}, u32[]{:S(2)}) collective-permute-start(bf16[512,768]{0,1:T(8,128)(2,1)S(1)} %constant_dynamic-slice_fusion.6), channel_id=1, source_target_pairs={{0,16},{8,24},{16,0},{24,8},{1,17},{9,25},{17,1},{25,9},{2,18},{10... | collective-permute-start | bytes 2359304 | tf_op jit(solution)/shard_map/dp_projection1024/ppermute | solution.py:296
  562.5 36.5 %collective-permute-start.37 = (bf16[256,2048]{1,0:T(8,128)(2,1)}, bf16[256,2048]{1,0:T(8,128)(2,1)S(1)}, u32[]{:S(2)}, u32[]{:S(2)}) collective-permute-start(bf16[256,2048]{1,0:T(8,128)(2,1)} %collective-permute-done.31), channel_id=1, source_target_pairs={{0,8},{8,0},{16,24},{24,16},{1,9},{9,1},{17,25},{25,17},{2,10},{10... | collective-permute-start | bytes 3145736 | tf_op jit(solution)/shard_map/dp_contract/ppermute | solution.py:296
  563.8 35.2 %collective-permute-start.38 = (bf16[512,1024]{1,0:T(8,128)(2,1)}, bf16[512,1024]{1,0:T(8,128)(2,1)S(1)}, u32[]{:S(2)}, u32[]{:S(2)}) collective-permute-start(bf16[512,1024]{1,0:T(8,128)(2,1)} %collective-permute-done.33), channel_id=1, source_target_pairs={{0,16},{8,24},{16,0},{24,8},{1,17},{9,25},{17,1},{25,9},{2,18},{10... | collective-permute-start | bytes 3145736 | tf_op jit(solution)/shard_map/dp_expand/ppermute | solution.py:296
  590.7 54.1 %collective-permute-start.53 = (bf16[256,2048]{1,0:T(8,128)(2,1)}, bf16[256,2048]{1,0:T(8,128)(2,1)}, u32[]{:S(2)}, u32[]{:S(2)}) collective-permute-start(bf16[256,2048]{1,0:T(8,128)(2,1)} %slice.241), channel_id=1, source_target_pairs={{0,1},{1,0},{2,3},{3,2},{4,5},{5,4},{6,7},{7,6},{8,9},{9,8},{10,11... | collective-permute-start | bytes 3145736 | tf_op jit(solution)/shard_map/ppermute | solution.py:245
  614.0 17.0 %collective-permute-start.48 = (bf16[256,768]{0,1:T(8,128)(2,1)S(1)}, bf16[256,768]{0,1:T(8,128)(2,1)}, u32[]{:S(2)}, u32[]{:S(2)}) collective-permute-start(bf16[256,768]{0,1:T(8,128)(2,1)S(1)} %add_convert_fusion.15), channel_id=1, source_target_pairs={{0,16},{8,24},{16,0},{24,8},{1,17},{9,25},{17,1},{25,9},{2,18},{10... | collective-permute-start | bytes 1179656 | tf_op jit(solution)/shard_map/dp_projection1024/ppermute | solution.py:296
  615.0 16.0 %collective-permute-start.47 = (bf16[256,768]{0,1:T(8,128)(2,1)S(1)}, bf16[256,768]{0,1:T(8,128)(2,1)}, u32[]{:S(2)}, u32[]{:S(2)}) collective-permute-start(bf16[256,768]{0,1:T(8,128)(2,1)S(1)} %add_convert_fusion.15), channel_id=1, source_target_pairs={{0,8},{8,0},{16,24},{24,16},{1,9},{9,1},{17,25},{25,17},{2,10},{10... | collective-permute-start | bytes 1179656 | tf_op jit(solution)/shard_map/dp_projection1024/ppermute | solution.py:296
  640.0 13.7 %collective-permute-start.51 = (f32[6,2048]{1,0:T(8,128)S(1)}, f32[6,2048]{1,0:T(8,128)S(1)}, u32[]{:S(2)}, u32[]{:S(2)}) collective-permute-start(f32[6,2048]{1,0:T(8,128)S(1)} %broadcast_multiply_fusion), channel_id=1, source_target_pairs={{0,8},{8,0},{16,24},{24,16},{1,9},{9,1},{17,25},{25,17},{2,10},{10... | collective-permute-start | bytes 147464 | tf_op jit(solution)/shard_map/small_sums/ppermute | solution.py:389
  641.5 16.6 %collective-permute-start.60 = (bf16[64,2048]{1,0:T(8,128)(2,1)}, bf16[64,2048]{1,0:T(8,128)(2,1)S(1)}, u32[]{:S(2)}, u32[]{:S(2)}) collective-permute-start(bf16[64,2048]{1,0:T(8,128)(2,1)} %collective-permute-done.49), channel_id=1, source_target_pairs={{0,8},{8,0},{16,24},{24,16},{1,9},{9,1},{17,25},{25,17},{2,10},{10... | collective-permute-start | bytes 786440 | tf_op jit(solution)/shard_map/dp_output/ppermute | solution.py:296
  642.0 16.1 %collective-permute-start.58 = (bf16[256,768]{0,1:T(8,128)(2,1)S(1)}, bf16[256,768]{0,1:T(8,128)(2,1)S(1)}, u32[]{:S(2)}, u32[]{:S(2)}) collective-permute-start(bf16[256,768]{0,1:T(8,128)(2,1)S(1)} %collective-permute-done.45), channel_id=1, source_target_pairs={{0,8},{8,0},{16,24},{24,16},{1,9},{9,1},{17,25},{25,17},{2,10},{10... | collective-permute-start | bytes 1179656 | tf_op jit(solution)/shard_map/dp_projection0/ppermute | solution.py:296
  643.5 14.6 %collective-permute-start.59 = (bf16[256,768]{0,1:T(8,128)(2,1)}, bf16[256,768]{0,1:T(8,128)(2,1)S(1)}, u32[]{:S(2)}, u32[]{:S(2)}) collective-permute-start(bf16[256,768]{0,1:T(8,128)(2,1)} %collective-permute-done.47), channel_id=1, source_target_pairs={{0,16},{8,24},{16,0},{24,8},{1,17},{9,25},{17,1},{25,9},{2,18},{10... | collective-permute-start | bytes 1179656 | tf_op jit(solution)/shard_map/dp_projection1024/ppermute | solution.py:296
  647.4 16.3 %collective-permute-start.54 = (bf16[256,2048]{1,0:T(8,128)(2,1)S(1)}, bf16[256,2048]{1,0:T(8,128)(2,1)}, u32[]{:S(2)}, u32[]{:S(2)}) collective-permute-start(bf16[256,2048]{1,0:T(8,128)(2,1)S(1)} %add_convert_fusion.3), channel_id=1, source_target_pairs={{0,2},{1,3},{2,6},{3,7},{6,4},{7,5},{4,0},{5,1},{8,10},{9,11},{10,... | collective-permute-start | bytes 3145736 | tf_op jit(solution)/shard_map/branch_ring3/ppermute | solution.py:241
  658.1 18.4 %collective-permute-start.24 = (bf16[256,2048]{1,0:T(8,128)(2,1)}, bf16[256,2048]{1,0:T(8,128)(2,1)}, u32[]{:S(2)}, u32[]{:S(2)}) collective-permute-start(bf16[256,2048]{1,0:T(8,128)(2,1)} %slice.233), channel_id=1, source_target_pairs={{0,1},{1,0},{2,3},{3,2},{4,5},{5,4},{6,7},{7,6},{8,9},{9,8},{10,11... | collective-permute-start | bytes 3145736 | tf_op jit(solution)/shard_map/ppermute | solution.py:245
  (77 other events, 495.1 us)
Sparse Core Ops, SparseCore 0:
  12.1 94.0 all-gather.3
  107.8 113.9 all-gather.5
  389.6 80.4 all-gather.7
  529.8 89.8 reduce-scatter.1
